TPU v7x, 32 devices: a whole 2x2x4 slice. The times are simulated.
32 devices in a mesh: chan: 4 (over y, core), space: 8 (over z, x).
Axes of the slice: x: 2, y: 2, z: 4, core: 2. Of those that a mesh axis runs over, the one named last changes fastest.
Arguments:
- features: bfloat16 [2, 256, 53760], P(None, 'chan', 'space'), may hold values from -6 to 6
- image_sizes: int32 [2, 192], replicated, may hold values from 10 to 18, as said below
- conv_in_w: bfloat16 [3, 3, 256, 512], P(None, None, 'chan'), may hold values from -0.125 to 0.125
- proj_w: bfloat16 [256, 512], P('chan'), may hold values from -0.375 to 0.375
- conv_mid_w: bfloat16 [3, 3, 3, 512, 512], P(None, None, None, 'chan'), may hold values from -0.09375 to 0.09375
- norm_gain: float32 [5, 512], P(None, 'chan'), may hold values from 0.1 to 1.9
- norm_bias: float32 [5, 512], P(None, 'chan'), may hold values from -2.5 to 2.5
- out_grad: bfloat16 [2, 512, 13440], P(None, 'chan', 'space'), may hold values from -6 to 6
Outputs:
- block_out: bfloat16 [2, 512, 13440], P(None, 'chan', 'space')
- feature_grad: float32 [2, 256, 53760], P(None, 'chan', 'space')
- conv_in_grad: float32 [3, 3, 256, 512], P(None, None, 'chan')
- proj_grad: float32 [256, 512], P('chan')
- conv_mid_grad: float32 [3, 3, 3, 512, 512], P(None, None, None, 'chan')
- gain_grad: float32 [5, 512], P(None, 'chan')
- bias_grad: float32 [5, 512], P(None, 'chan')
Inputs may be any that keep to these rules, and one draw needn't show every extreme that they name: `image_sizes`: in each micro-batch a third of the 192 images have side 10, a third side 14 and a third side 18, in an order that varies.
All inputs are finite; a program needn't handle non-finite values.
Results may differ from a plain program's by a relative error of at most 0.033.
Values may be sent and summed in bfloat16 or wider, within the bound.
No kernel may reach another device: no remote copies, remote signals or barrier semaphores. Data moves between devices by JAX's collectives and lax.ppermute only.
A program may use at most 192 MiB of HBM per device.

v0:
```python
import jax
import jax.numpy as jnp
from jax import lax
from jax.sharding import PartitionSpec as P

MICRO = 2
WIN = 20


eps_norm = 1e-05


def with_halo(block, sides, width):
    for axis, dim in sides:
        count = lax.axis_size(axis)
        forward = [(i, i + 1) for i in range(count - 1)]
        backward = [(target, source) for source, target in forward]
        low = lax.ppermute(
            lax.slice_in_dim(block, block.shape[dim] - width, None, axis=dim), axis, forward
        )
        high = lax.ppermute(lax.slice_in_dim(block, 0, width, axis=dim), axis, backward)
        block = jnp.concatenate([low, block, high], axis=dim)
    return block


def shifted_2(value, axis, steps):
    count = lax.axis_size(axis)
    first, last = (max(0, -steps), min(count, count - steps))
    return lax.ppermute(value, axis, [(source, source + steps) for source in range(first, last)])


def as_sent(x):

    def short(part):
        return part.astype(jnp.bfloat16) if part.dtype == jnp.float32 else part

    return jax.tree.map(short, x)


def canvas_rows(sizes_row, first_row, row_count):
    sides_out = sizes_row // 2
    starts = jnp.cumsum(sides_out) - sides_out
    global_rows = first_row + jnp.arange(row_count, dtype=jnp.int32)
    inside = (
        (global_rows[:, None] >= starts[None, :])
        & (global_rows[:, None] < (starts + sides_out)[None, :])
    ).astype(jnp.int32)
    begins = jnp.sum(inside * starts[None, :], axis=1)
    widths = jnp.sum(inside * sides_out[None, :], axis=1)
    return (global_rows - begins, widths)


def row_masks(local_rows, widths, columns):
    column_ids = jnp.arange(columns, dtype=jnp.int32)
    inside_mask = (column_ids[None, :] < widths[:, None]).astype(jnp.float32).reshape(-1)
    upper_mask = jnp.repeat(((local_rows > 0) & (widths > 0)).astype(jnp.float32), columns)
    lower_mask = jnp.repeat((local_rows < widths - 1).astype(jnp.float32), columns)
    return (inside_mask, upper_mask, lower_mask)


def input_mask(widths, columns):
    column_ids = jnp.arange(columns, dtype=jnp.int32)
    single = (column_ids[None, :] < 2 * widths[:, None]).astype(jnp.float32)
    return jnp.broadcast_to(single[:, None, :], (widths.shape[0], 2, columns)).reshape(-1)


def mid_columns(source_ext, upper_mask, lower_mask, width_out, position_count):
    pieces = []
    for row_step, row_keep in ((-1, upper_mask), (0, None), (1, lower_mask)):
        row_view = lax.slice_in_dim(
            source_ext,
            (1 + row_step) * width_out,
            (1 + row_step) * width_out + position_count,
            axis=1,
        )
        if row_keep is not None:
            row_view = row_view * row_keep[None, :]
        padded = jnp.pad(row_view, ((0, 0), (1, 1)))
        for col_step in (-1, 0, 1):
            pieces.append(padded[:, 1 + col_step : 1 + col_step + position_count])
    return jnp.concatenate(pieces, axis=0)


def entry_columns(source, prior_row, upper_mask, width_out):
    channels = source.shape[0]
    rows_out = source.shape[1] // (4 * width_out)
    position_count = rows_out * width_out
    phases = source.reshape(channels, rows_out, 2, width_out, 2)
    prior_split = prior_row.reshape(channels, width_out, 2)
    pieces = []
    for row_step in (-1, 0, 1):
        sources = []
        for parity in (0, 1):
            phase_view = phases[:, :, 0 if row_step == 0 else 1, :, parity].reshape(
                channels, position_count
            )
            if row_step == -1:
                phase_view = (
                    jnp.concatenate([prior_split[:, :, parity], phase_view], axis=1)[
                        :, :position_count
                    ]
                    * upper_mask[None, :]
                )
            sources.append(phase_view)
        pieces.append(jnp.pad(sources[1], ((0, 0), (1, 0)))[:, :position_count])
        pieces.append(sources[0])
        pieces.append(sources[1])
    return jnp.concatenate(pieces, axis=0)


def entry_adjoint(tap_grads, short_input, upper_mask, width_out):
    channels = tap_grads.shape[1]
    position_count = tap_grads.shape[2]
    rows_out = position_count // width_out
    empty_phase = jnp.zeros_like(short_input)
    phase_grads = [[short_input, empty_phase], [empty_phase, empty_phase]]
    prior_parts = []
    for row_index in range(3):
        left_grad = tap_grads[3 * row_index]
        parity_zero = tap_grads[3 * row_index + 1]
        parity_one = tap_grads[3 * row_index + 2] + jnp.pad(left_grad, ((0, 0), (0, 1)))[:, 1:]
        for parity, grad_view in ((0, parity_zero), (1, parity_one)):
            if row_index == 0:
                masked = grad_view * upper_mask[None, :]
                prior_parts.append(masked[:, :width_out])
                phase_grads[1][parity] = jnp.pad(masked[:, width_out:], ((0, 0), (0, width_out)))
            else:
                row_parity = 0 if row_index == 1 else 1
                phase_grads[row_parity][parity] = phase_grads[row_parity][parity] + grad_view
    shaped = [
        [grad_part.reshape(channels, rows_out, width_out) for grad_part in grad_pair]
        for grad_pair in phase_grads
    ]
    full_grad = jnp.stack([jnp.stack(shaped[0], -1), jnp.stack(shaped[1], -1)], 2).reshape(
        channels, 4 * position_count
    )
    prior_grad = jnp.stack(prior_parts, -1).reshape(channels, 2 * width_out)
    return (full_grad, prior_grad)


def silu_slope(values):
    sigmoid_value = jax.nn.sigmoid(values)
    return sigmoid_value * (1.0 + values * (1.0 - sigmoid_value))


def silu_of(values):
    return values * jax.nn.sigmoid(values)


def rims(source, width_out):
    return with_halo(source, (("space", 1),), width_out)


def space_sums(first_sum, second_sum):
    return lax.psum((first_sum, second_sum), "space")


def reduce_channels(term_fn, rows_each):
    return lax.psum_scatter(
        term_fn(jnp.int32(0), lax.axis_size("chan") * rows_each).astype(jnp.bfloat16),
        "chan",
        scatter_dimension=0,
        tiled=True,
    ).astype(jnp.float32)


def column_term(weight_mat, columns_mat):

    def channel_term(row_start, count_rows):
        return lax.dot_general(
            weight_mat, columns_mat, (((0,), (0,)), ((), ())), preferred_element_type=jnp.float32
        )

    return channel_term


def norm_forward(source, inside_mask, total_count, gain_row, bias_row):
    masked = source * inside_mask[None, :]
    first_sum, second_sum = space_sums(jnp.sum(masked, axis=1), jnp.sum(masked * source, axis=1))
    mean_value = first_sum / total_count
    inverse = lax.rsqrt(second_sum / total_count - mean_value * mean_value + eps_norm)
    scaled = (source - mean_value[:, None]) * inverse[:, None]
    normed = inside_mask[None, :] * (gain_row[:, None] * scaled + bias_row[:, None])
    return (normed, scaled, inverse)


def norm_backward(grad_out, scaled, inverse, inside_mask, total_count, gain_row):
    masked = grad_out * inside_mask[None, :]
    grad_sum, grad_dot = space_sums(jnp.sum(masked, axis=1), jnp.sum(masked * scaled, axis=1))
    source_grad = (
        inside_mask[None, :]
        * (gain_row * inverse)[:, None]
        * (masked - grad_sum[:, None] / total_count - scaled * (grad_dot / total_count)[:, None])
    )
    return (source_grad.astype(jnp.bfloat16), grad_sum, grad_dot)


def tap_stack(grad_ext, upper_ext, lower_ext, width_out, position_count):
    shifted = []
    for row_step, row_keep in ((-1, upper_ext), (0, None), (1, lower_ext)):
        weighted = grad_ext if row_keep is None else grad_ext * row_keep[None, :]
        padded = jnp.pad(weighted, ((0, 0), (1, 1)))
        for col_step in (-1, 0, 1):
            offset = (1 - row_step) * width_out - col_step + 1
            shifted.append(padded[:, offset : offset + position_count])
    return jnp.stack(shifted, 0)


def mid_forward(source, weight_mat, upper_low, lower_low, width_out, position_count, rows_each):
    source_ext = rims(source, width_out)
    columns_mat = mid_columns(source_ext, upper_low, lower_low, width_out, position_count)
    return (reduce_channels(column_term(weight_mat, columns_mat), rows_each), columns_mat)


def mid_backward(
    grad_ext, columns_mat, weight_taps, upper_ext, lower_ext, width_out, position_count
):
    shard_rows = lax.all_gather(grad_ext, "chan", axis=0, tiled=True)
    own_rows = lax.slice_in_dim(shard_rows, width_out, width_out + position_count, axis=1)
    partial_weight = lax.dot_general(
        columns_mat, own_rows, (((1,), (1,)), ((), ())), preferred_element_type=jnp.float32
    )
    stacked = tap_stack(shard_rows, upper_ext, lower_ext, width_out, position_count)
    input_grad = jnp.einsum("tco,toq->cq", weight_taps, stacked, preferred_element_type=jnp.float32)
    return (input_grad, partial_weight)


def entry_backward(grad_entry, entry_cols, entry_taps):
    shard_rows = lax.all_gather(grad_entry, "chan", axis=0, tiled=True)
    partial_weight = lax.dot_general(
        entry_cols, shard_rows, (((1,), (1,)), ((), ())), preferred_element_type=jnp.float32
    )
    tap_grads = jnp.einsum(
        "tco,oq->tcq", entry_taps, shard_rows, preferred_element_type=jnp.float32
    )
    return (tap_grads, partial_weight)


def shortcut_backward(grad_short, phase_zero, proj_w):
    shard_rows = lax.all_gather(grad_short, "chan", axis=0, tiled=True)
    partial_weight = lax.dot_general(
        phase_zero, shard_rows, (((1,), (1,)), ((), ())), preferred_element_type=jnp.float32
    )
    input_grad = jnp.dot(proj_w, shard_rows, preferred_element_type=jnp.float32)
    return (input_grad, partial_weight)


def shards(features, image_sizes, conv_in_w, proj_w, conv_mid_w, norm_gain, norm_bias, out_grad):
    width_out = WIN // 2
    chans_in = features.shape[1]
    rows_each = norm_gain.shape[1]
    rows_dev = features.shape[2] // (4 * width_out)
    position_count = rows_dev * width_out
    first_row = lax.axis_index("space") * rows_dev
    entry_mat = conv_in_w.reshape(9 * chans_in, -1)
    out_width = entry_mat.shape[1]
    entry_taps = conv_in_w.reshape(9, chans_in, out_width)
    mid_mats = conv_mid_w.reshape(3, 9 * rows_each, out_width)
    mid_taps = conv_mid_w.reshape(3, 9, rows_each, out_width)
    mid_total = jnp.zeros((3, 9 * rows_each, out_width), jnp.float32)
    weight_totals = (
        jnp.zeros((9 * chans_in, out_width), jnp.float32),
        jnp.zeros((chans_in, out_width), jnp.float32),
        mid_total,
    )
    gain_total = jnp.zeros((5, rows_each), jnp.float32)
    bias_total = jnp.zeros((5, rows_each), jnp.float32)
    outputs_list = []
    grads_list = []
    for micro_index in range(MICRO):
        sizes_row = image_sizes[micro_index]
        local_ext, width_ext = canvas_rows(sizes_row, first_row - 1, rows_dev + 2)
        inside_ext, upper_ext, lower_ext = row_masks(local_ext, width_ext, width_out)
        inside_mask = inside_ext[width_out : width_out + position_count]
        upper_mask = upper_ext[width_out : width_out + position_count]
        lower_mask = lower_ext[width_out : width_out + position_count]
        inside_in = input_mask(width_ext[1 : rows_dev + 1], WIN)
        sides_out = sizes_row // 2
        total_count = jnp.sum((sides_out * sides_out).astype(jnp.float32))
        upper_low = upper_mask.astype(jnp.bfloat16)
        lower_low = lower_mask.astype(jnp.bfloat16)
        upper_ext_low = upper_ext.astype(jnp.bfloat16)
        lower_ext_low = lower_ext.astype(jnp.bfloat16)
        source = features[micro_index] * inside_in.astype(jnp.bfloat16)[None, :]
        prior_row = shifted_2(source[:, -WIN:], "space", 1)
        entry_cols = entry_columns(source, prior_row, upper_low, width_out)
        phase_zero = entry_cols[4 * chans_in : 5 * chans_in]
        entry_sum = reduce_channels(column_term(entry_mat, entry_cols), rows_each)
        short_sum = reduce_channels(column_term(proj_w, phase_zero), rows_each)
        norm_zero, scaled_zero, inverse_zero = norm_forward(
            entry_sum, inside_mask, total_count, norm_gain[0], norm_bias[0]
        )
        first_low = silu_of(norm_zero).astype(jnp.bfloat16)
        second_sum, second_cols = mid_forward(
            first_low, mid_mats[0], upper_low, lower_low, width_out, position_count, rows_each
        )
        norm_one, scaled_one, inverse_one = norm_forward(
            second_sum, inside_mask, total_count, norm_gain[1], norm_bias[1]
        )
        norm_two, scaled_two, inverse_two = norm_forward(
            short_sum, inside_mask, total_count, norm_gain[2], norm_bias[2]
        )
        joined_pre = norm_one + norm_two
        joined = silu_of(joined_pre)
        joined_low = joined.astype(jnp.bfloat16)
        third_sum, third_cols = mid_forward(
            joined_low, mid_mats[1], upper_low, lower_low, width_out, position_count, rows_each
        )
        norm_three, scaled_three, inverse_three = norm_forward(
            third_sum, inside_mask, total_count, norm_gain[3], norm_bias[3]
        )
        third_low = silu_of(norm_three).astype(jnp.bfloat16)
        fourth_sum, fourth_cols = mid_forward(
            third_low, mid_mats[2], upper_low, lower_low, width_out, position_count, rows_each
        )
        norm_four, scaled_four, inverse_four = norm_forward(
            fourth_sum, inside_mask, total_count, norm_gain[4], norm_bias[4]
        )
        final_pre = norm_four + joined
        outputs_list.append(silu_of(final_pre).astype(jnp.bfloat16))
        grad_final = out_grad[micro_index].astype(jnp.float32) * silu_slope(final_pre)
        grad_four, bias_four, gain_four = norm_backward(
            grad_final, scaled_four, inverse_four, inside_mask, total_count, norm_gain[4]
        )
        grad_third, weight_four = mid_backward(
            rims(grad_four, width_out),
            fourth_cols,
            mid_taps[2],
            upper_ext_low,
            lower_ext_low,
            width_out,
            position_count,
        )
        grad_three, bias_three, gain_three = norm_backward(
            grad_third * silu_slope(norm_three),
            scaled_three,
            inverse_three,
            inside_mask,
            total_count,
            norm_gain[3],
        )
        grad_joined_conv, weight_three = mid_backward(
            rims(grad_three, width_out),
            third_cols,
            mid_taps[1],
            upper_ext_low,
            lower_ext_low,
            width_out,
            position_count,
        )
        grad_joined = (grad_final + grad_joined_conv) * silu_slope(joined_pre)
        grad_second, bias_one, gain_one = norm_backward(
            grad_joined, scaled_one, inverse_one, inside_mask, total_count, norm_gain[1]
        )
        grad_short, bias_two, gain_two = norm_backward(
            grad_joined, scaled_two, inverse_two, inside_mask, total_count, norm_gain[2]
        )
        grad_first_conv, weight_two = mid_backward(
            rims(grad_second, width_out),
            second_cols,
            mid_taps[0],
            upper_ext_low,
            lower_ext_low,
            width_out,
            position_count,
        )
        short_input, weight_short = shortcut_backward(grad_short, phase_zero, proj_w)
        grad_entry, bias_zero, gain_zero = norm_backward(
            grad_first_conv * silu_slope(norm_zero),
            scaled_zero,
            inverse_zero,
            inside_mask,
            total_count,
            norm_gain[0],
        )
        tap_grads, weight_entry = entry_backward(grad_entry, entry_cols, entry_taps)
        input_grad, prior_grad = entry_adjoint(tap_grads, short_input, upper_mask, width_out)
        received = shifted_2(prior_grad, "space", -1)
        input_grad = jnp.concatenate(
            [input_grad[:, :-WIN], input_grad[:, -WIN:] + received], axis=1
        )
        grads_list.append(input_grad * inside_in[None, :])
        gain_total = gain_total + jnp.stack([gain_zero, gain_one, gain_two, gain_three, gain_four])
        bias_total = bias_total + jnp.stack([bias_zero, bias_one, bias_two, bias_three, bias_four])
        micro_weights = (
            weight_entry,
            weight_short,
            jnp.stack([weight_two, weight_three, weight_four]),
        )
        weight_totals = jax.tree.map(
            lambda total_a, total_b: total_a + total_b, weight_totals, micro_weights
        )
    weight_totals = jax.tree.map(
        lambda part: part.astype(jnp.float32), lax.psum(as_sent(weight_totals), "space")
    )
    block_out = jnp.stack(outputs_list)
    feature_grad = jnp.stack(grads_list)
    conv_in_grad = weight_totals[0].reshape(3, 3, chans_in, out_width)
    proj_grad = weight_totals[1]
    conv_mid_grad = weight_totals[2].reshape(3, 3, 3, rows_each, out_width)
    return (block_out, feature_grad, conv_in_grad, proj_grad, conv_mid_grad, gain_total, bias_total)


def solution(mesh):
    placed = (
        P(None, "chan", "space"),
        P(),
        P(None, None, "chan", None),
        P("chan", None),
        P(None, None, None, "chan", None),
        P(None, "chan"),
        P(None, "chan"),
        P(None, "chan", "space"),
    )
    return jax.shard_map(
        shards,
        mesh=mesh,
        in_specs=placed,
        out_specs=(
            P(None, "chan", "space"),
            P(None, "chan", "space"),
            P(None, None, "chan", None),
            P("chan", None),
            P(None, None, None, "chan", None),
            P(None, "chan"),
            P(None, "chan"),
        ),
        check_vma=False,
    )
```

profile of v0, /device:TPU:0, one launch (start us, length us, event | category | flops | bytes accessed | tf_op | source)
XLA Modules:
  0.0 1121.7 jit_solution(16737099204674322714)
XLA Ops:
  14.7 4.8 collective-permute-start.7
  29.7 11.7 %slice_reduce_fusion.1 = (bf16[64,168,10]{0,2,1:T(8,128)(2,1)}, bf16[64,168,10]{0,2,1:T(8,128)(2,1)}, bf16[64,168,10]{0,2,1:T(8,128)(2,1)}, bf16[64,168,10]{0,2,1:T(8,128)(2,1)S(1)}) fusion(bf16[64,168,2,10,2]{0,4,3,2,1:T(2,128)(2,1)S(1)} %broadcast_multiply_fusion.12), kind=kLoop, calls=%fused_computation.356 | loop fusion | bytes 1720320 | tf_op jit(solution)/shard_map/slice | solution.py:94
  52.4 5.1 concatenate.138
  67.1 11.7 %slice_reduce_fusion.5 = (bf16[64,168,10]{0,2,1:T(8,128)(2,1)S(1)}, bf16[64,168,10]{0,2,1:T(8,128)(2,1)}, bf16[64,168,10]{0,2,1:T(8,128)(2,1)}, bf16[64,168,10]{0,2,1:T(8,128)(2,1)}) fusion(bf16[64,168,2,10,2]{0,4,3,2,1:T(2,128)(2,1)S(1)} %broadcast_multiply_fusion.13), kind=kLoop, calls=%fused_computation.360 | loop fusion | bytes 1720320 | tf_op jit(solution)/shard_map/slice | solution.py:94
  85.7 5.2 concatenate.126
  105.5 21.3 %reduce-scatter.31.cloned.1.call-done = bf16[128,1680]{1,0:T(8,128)(2,1)} async-done(((bf16[512,1680]{1,0:T(8,128)(2,1)}), bf16[128,1680]{1,0:T(8,128)(2,1)}) %reduce-scatter.31.cloned.1.call-update) | async-done | bytes 430096
  128.4 21.4 %all-reduce.55 = (f32[128]{0:T(128)S(1)}, f32[128]{0:T(128)S(1)}, f32[128]{0:T(128)S(1)}, f32[128]{0:T(128)S(1)}) all-reduce(f32[128]{0:T(128)S(1)} %get-tuple-element.78, f32[128]{0:T(128)S(1)} %get-tuple-element.77, f32[128]{0:T(128)S(1)} %get-tuple-element.68, ...), channel_id=1, replica_groups=mesh['chan'=4,'space'=8] {'space'}, use_global_device_ids=true, to_apply=%region_36.37 | all-reduce | flops 512 | bytes 4096 | tf_op jit(solution)/shard_map/psum | solution.py:155
  154.0 3.9 fusion.285
  170.1 3.7 copy.129
  173.9 3.7 collective-permute-start.1
  193.6 30.8 %reduce-scatter.43.cloned.1.call-done = bf16[128,1680]{1,0:T(8,128)(2,1)} async-done(((bf16[512,1680]{1,0:T(8,128)(2,1)}), bf16[128,1680]{1,0:T(8,128)(2,1)}) %reduce-scatter.43.cloned.1.call-update) | async-done | bytes 430096
  226.1 31.3 %reduce-scatter.33.cloned.1.call-done = bf16[128,1680]{1,0:T(8,128)(2,1)} async-done(((bf16[512,1680]{1,0:T(8,128)(2,1)}), bf16[128,1680]{1,0:T(8,128)(2,1)}) %reduce-scatter.33.cloned.1.call-update) | async-done | bytes 430096
  259.1 21.6 %all-reduce.54 = (f32[128]{0:T(128)S(1)}, f32[128]{0:T(128)S(1)}, f32[128]{0:T(128)S(1)}, f32[128]{0:T(128)S(1)}, f32[128]{0:T(128)S(1)}, /*index=5*/f32[128]{0:T(128)S(1)}, f32[128]{0:T(128)S(1)}, f32[128]{0:T(128)S(1)}) all-reduce(f32[128]{0:T(128)S(1)} %get-tuple-element.83, ...), channel_id=1, replica_groups=mesh['chan'=4,'space'=8] {'space'}, use_global_device_ids=true, to_apply=%region_47.48 | all-reduce | flops 1024 | bytes 8192 | tf_op jit(solution)/shard_map/psum | solution.py:155
  297.1 3.7 copy.133
  300.8 3.6 collective-permute-start.3
  316.4 3.7 copy.123
  320.2 8.1 reduce-scatter.47.cloned.1.call-done
  330.4 31.1 %reduce-scatter.37.cloned.1.call-done = bf16[128,1680]{1,0:T(8,128)(2,1)} async-done(((bf16[512,1680]{1,0:T(8,128)(2,1)}), bf16[128,1680]{1,0:T(8,128)(2,1)}) %reduce-scatter.37.cloned.1.call-update) | async-done | bytes 430096
  363.0 21.4 %all-reduce.53 = (f32[128]{0:T(128)S(1)}, f32[128]{0:T(128)S(1)}, f32[128]{0:T(128)S(1)}, f32[128]{0:T(128)S(1)}) all-reduce(f32[128]{0:T(128)S(1)} %get-tuple-element.74, f32[128]{0:T(128)S(1)} %get-tuple-element.73, f32[128]{0:T(128)S(1)} %get-tuple-element.64, ...), channel_id=1, replica_groups=mesh['chan'=4,'space'=8] {'space'}, use_global_device_ids=true, to_apply=%region_52.53 | all-reduce | flops 512 | bytes 4096 | tf_op jit(solution)/shard_map/psum | solution.py:155
  400.9 3.7 copy.135
  404.7 3.6 collective-permute-start.5
  420.2 3.7 copy.125
  424.0 8.1 reduce-scatter.49.cloned.1.call-done
  433.7 30.8 %reduce-scatter.39.cloned.1.call-done = bf16[128,1680]{1,0:T(8,128)(2,1)} async-done(((bf16[512,1680]{1,0:T(8,128)(2,1)}), bf16[128,1680]{1,0:T(8,128)(2,1)}) %reduce-scatter.39.cloned.1.call-update) | async-done | bytes 430096
  466.1 21.4 %all-reduce.52 = (f32[128]{0:T(128)S(1)}, f32[128]{0:T(128)S(1)}, f32[128]{0:T(128)S(1)}, f32[128]{0:T(128)S(1)}) all-reduce(f32[128]{0:T(128)S(1)} %get-tuple-element.72, f32[128]{0:T(128)S(1)} %get-tuple-element.71, f32[128]{0:T(128)S(1)} %get-tuple-element.62, ...), channel_id=1, replica_groups=mesh['chan'=4,'space'=8] {'space'}, use_global_device_ids=true, to_apply=%region_57.58 | all-reduce | flops 512 | bytes 4096 | tf_op jit(solution)/shard_map/psum | solution.py:155
  494.4 17.2 %all-reduce.51 = (f32[128]{0:T(128)S(1)}, f32[128]{0:T(128)S(1)}, f32[128]{0:T(128)S(1)}, f32[128]{0:T(128)S(1)}) all-reduce(f32[128]{0:T(128)S(1)} %get-tuple-element.46, f32[128]{0:T(128)S(1)} %get-tuple-element.45, f32[128]{0:T(128)S(1)} %get-tuple-element.44, ...), channel_id=1, replica_groups=mesh['chan'=4,'space'=8] {'space'}, use_global_device_ids=true, to_apply=%region_81.82 | all-reduce | flops 512 | bytes 4096 | tf_op jit(solution)/shard_map/psum | solution.py:155
  516.6 4.5 collective-permute-start.21
  522.4 5.1 concatenate.154
  530.7 5.4 collective-permute-start.14
  537.5 4.6 concatenate.148
  542.1 6.8 all-gather.21.cloned.1.call-done
  565.5 5.7 all-gather.11.cloned.1.call-done
  578.4 10.8 fusion.280
  589.2 5.4 fusion.278
  594.5 21.3 %all-reduce.50 = (f32[128]{0:T(128)S(1)}, f32[128]{0:T(128)S(1)}, f32[128]{0:T(128)S(1)}, f32[128]{0:T(128)S(1)}) all-reduce(f32[128]{0:T(128)S(1)} %get-tuple-element.60, f32[128]{0:T(128)S(1)} %get-tuple-element.59, f32[128]{0:T(128)S(1)} %get-tuple-element.53, ...), channel_id=1, replica_groups=mesh['chan'=4,'space'=8] {'space'}, use_global_device_ids=true, to_apply=%region_85.86 | all-reduce | flops 512 | bytes 4096 | tf_op jit(solution)/shard_map/psum | solution.py:155
  620.8 4.5 collective-permute-start.23
  626.7 5.1 concatenate.155
  636.9 4.8 collective-permute-start.16
  643.0 5.1 concatenate.149
  667.8 5.3 all-gather.13.cloned.1.call-done
  680.6 11.0 fusion.191
  691.6 6.1 fusion.135
  697.7 21.3 %all-reduce.49 = (f32[128]{0:T(128)S(1)}, f32[128]{0:T(128)S(1)}, f32[128]{0:T(128)S(1)}, f32[128]{0:T(128)S(1)}) all-reduce(f32[128]{0:T(128)S(1)} %get-tuple-element.55, f32[128]{0:T(128)S(1)} %get-tuple-element.56, f32[128]{0:T(128)S(1)} %get-tuple-element.48, ...), channel_id=1, replica_groups=mesh['chan'=4,'space'=8] {'space'}, use_global_device_ids=true, to_apply=%region_91.92 | all-reduce | flops 512 | bytes 4096 | tf_op jit(solution)/shard_map/psum | solution.py:155
  724.0 4.5 collective-permute-start.25
  729.9 5.0 concatenate.156
  739.9 4.8 collective-permute-start.18
  746.0 5.1 concatenate.150
  770.5 5.7 all-gather.17.cloned.1.call-done
  783.4 10.8 fusion.279
  794.3 5.4 fusion.277
  799.6 21.3 %all-reduce.48 = (f32[128]{0:T(128)S(1)}, f32[128]{0:T(128)S(1)}, f32[128]{0:T(128)S(1)}, f32[128]{0:T(128)S(1)}, f32[128]{0:T(128)S(1)}, /*index=5*/f32[128]{0:T(128)S(1)}) all-reduce(f32[128]{0:T(128)S(1)} %get-tuple-element.58, f32[128]{0:T(128)S(1)} %get-tuple-element.57, ...), channel_id=1, replica_groups=mesh['chan'=4,'space'=8] {'space'}, use_global_device_ids=true, to_apply=%region_95.96 | all-reduce | flops 768 | bytes 6144 | tf_op jit(solution)/shard_map/psum | solution.py:155
  837.1 6.1 convolution_bitcast_fusion.2
  843.2 3.8 convolution_bitcast_fusion.5
  847.0 3.8 convolution_bitcast_fusion.3
  850.9 3.8 convolution_bitcast_fusion.6
  856.2 4.6 convolution_bitcast_fusion.4
  894.5 6.8 copy.113
  930.7 6.8 copy.102
  937.5 4.2 slice_bitcast_fusion.1
  948.5 6.0 maximum_multiply_fusion.1
  954.6 4.6 maximum_multiply_fusion
  962.6 6.1 copy.116
  968.7 136.1 %all-reduce.59.cloned.1.call-done = (bf16[3,3,64,512]{3,2,1,0:T(8,128)(2,1)}, bf16[64,512]{1,0:T(8,128)(2,1)}, bf16[3,3,3,128,512]{4,3,2,1,0:T(8,128)(2,1)}) async-done(((bf16[3,3,64,512]{3,2,1,0:T(8,128)(2,1)}, bf16[64,512]{1,0:T(8,128)(2,1)}, bf16[3,3,3,128,512]{4,3,2,1,0:T(8,128)(2,1)}), (bf16[3,3,64,512]{3,2,1,0:T(8,128)(2,1)}, bf16[64,512]{1,0:T(8,128)(2,1)}, ...) | async-done | bytes 4194320 | tf_op jit(solution)/shard_map/psum | solution.py:394
  1108.6 5.9 reshape.455
  (677 shorter events, 373.8 us)
Async XLA Ops:
  7.2 50.3 %copy-start = (bf16[3,3,64,512]{3,2,1,0:T(8,128)(2,1)S(1)}, bf16[3,3,64,512]{3,2,1,0:T(8,128)(2,1)}, u32[]{:S(2)}) copy-start(bf16[3,3,64,512]{3,2,1,0:T(8,128)(2,1)} %param.10) | copy-start | bytes 1769476
  7.2 96.6 %reduce-scatter.41.cloned.1.call-start = ((), (), s32[]{:S(2)}) async-start(), calls=%async_computation.25 | async-start | bytes 2293760
  14.7 35.3 %collective-permute-start.7 = (bf16[64,20]{1,0:T(8,128)(2,1)S(1)}, bf16[64,20]{1,0:T(8,128)(2,1)S(1)}, u32[]{:S(2)}, u32[]{:S(2)}) collective-permute-start(bf16[64,20]{1,0:T(8,128)(2,1)S(1)} %slice_multiply_fusion), channel_id=1, source_target_pairs={{0,1},{1,2},{2,3},{3,4},{4,5},{5,6},{6,7},{8,9},{9,10},{10,11},{11... | collective-permute-start | bytes 7688 | tf_op jit(solution)/shard_map/ppermute | solution.py:29
  20.2 63.2 %collective-permute-start = (bf16[64,20]{1,0:T(8,128)(2,1)S(1)}, bf16[64,20]{1,0:T(8,128)(2,1)S(1)}, u32[]{:S(2)}, u32[]{:S(2)}) collective-permute-start(bf16[64,20]{1,0:T(8,128)(2,1)S(1)} %slice_multiply_fusion.1), channel_id=1, source_target_pairs={{0,1},{1,2},{2,3},{3,4},{4,5},{5,6},{6,7},{8,9},{9,10},{10,11},{11... | collective-permute-start | bytes 7688 | tf_op jit(solution)/shard_map/ppermute | solution.py:29
  46.9 49.7 %copy-start.29 = (bf16[64,1680]{0,1:T(8,128)(2,1)}, bf16[64,1680]{0,1:T(8,128)(2,1)S(1)}, u32[]{:S(2)}) copy-start(bf16[64,1680]{0,1:T(8,128)(2,1)S(1)} %reshape_squeeze.35) | copy-start | bytes 645124
  63.0 63.8 %reduce-scatter.31.cloned.1.call-start = ((), (), s32[]{:S(2)}) async-start(), calls=%async_computation.20 | async-start | bytes 2293760
  81.7 18.1 %copy-start.37 = (bf16[64,1680]{0,1:T(8,128)(2,1)}, bf16[64,1680]{0,1:T(8,128)(2,1)S(1)}, u32[]{:S(2)}) copy-start(bf16[64,1680]{0,1:T(8,128)(2,1)S(1)} %reshape_squeeze.31) | copy-start | bytes 645124
  96.5 94.5 %reduce-scatter.45.cloned.1.call-start = ((), (), s32[]{:S(2)}) async-start(), calls=%async_computation.27 | async-start | bytes 2293760
  99.7 92.6 %reduce-scatter.35.cloned.1.call-start = ((), (), s32[]{:S(2)}) async-start(), calls=%async_computation.22 | async-start | bytes 2293760
  103.0 121.4 %reduce-scatter.43.cloned.1.call-start = ((), (), s32[]{:S(2)}) async-start(), calls=%async_computation.26 | async-start | bytes 2293760
  103.2 49.5 %copy-start.96 = (f32[128]{0:T(128)}, f32[128]{0:T(128)S(1)}, u32[]{:S(2)}) copy-start(f32[128]{0:T(128)S(1)} %get-tuple-element.272) | copy-start | bytes 1540
  103.3 49.4 %copy-start.98 = (f32[128]{0:T(128)}, f32[128]{0:T(128)S(1)}, u32[]{:S(2)}) copy-start(f32[128]{0:T(128)S(1)} %get-tuple-element.268) | copy-start | bytes 1540
  105.2 52.7 %copy-start.25 = (bf16[128,1680]{0,1:T(8,128)(2,1)}, bf16[128,1680]{0,1:T(8,128)(2,1)S(1)}, u32[]{:S(2)}) copy-start(bf16[128,1680]{0,1:T(8,128)(2,1)S(1)} %copy.128) | copy-start | bytes 1290244
  128.1 29.8 %copy-start.22 = (bf16[128,1680]{0,1:T(8,128)(2,1)}, bf16[128,1680]{0,1:T(8,128)(2,1)S(1)}, u32[]{:S(2)}) copy-start(bf16[128,1680]{0,1:T(8,128)(2,1)S(1)} %copy.118) | copy-start | bytes 1290244
  152.7 6.8 collective-permute-start.8
  158.3 5.5 collective-permute-start.9
  173.8 83.6 %reduce-scatter.33.cloned.1.call-start = ((), (), s32[]{:S(2)}) async-start(), calls=%async_computation.21 | async-start | bytes 2293760
  173.9 5.3 collective-permute-start.1
  177.9 5.5 collective-permute-start.2
  190.9 137.3 %reduce-scatter.47.cloned.1.call-start = ((), (), s32[]{:S(2)}) async-start(), calls=%async_computation.28 | async-start | bytes 2293760
  225.7 266.4 %copy-start.18 = (bf16[128,1680]{0,1:T(8,128)(2,1)}, bf16[128,1680]{0,1:T(8,128)(2,1)S(1)}, u32[]{:S(2)}) copy-start(bf16[128,1680]{0,1:T(8,128)(2,1)S(1)} %copy.130) | copy-start | bytes 1290244
  258.7 230.1 %copy-start.16 = (bf16[128,1680]{0,1:T(8,128)(2,1)}, bf16[128,1680]{0,1:T(8,128)(2,1)S(1)}, u32[]{:S(2)}) copy-start(bf16[128,1680]{0,1:T(8,128)(2,1)S(1)} %copy.120) | copy-start | bytes 1290244
  283.9 2.6 collective-permute-start.10
  285.2 5.5 collective-permute-start.11
  300.8 60.6 %reduce-scatter.37.cloned.1.call-start = ((), (), s32[]{:S(2)}) async-start(), calls=%async_computation.23 | async-start | bytes 2293760
  300.8 5.0 collective-permute-start.3
  304.5 5.5 collective-permute-start.4
  320.1 111.9 %reduce-scatter.49.cloned.1.call-start = ((), (), s32[]{:S(2)}) async-start(), calls=%async_computation.29 | async-start | bytes 2293760
  362.7 23.0 %copy-start.31 = (bf16[128,1680]{0,1:T(8,128)(2,1)}, bf16[128,1680]{0,1:T(8,128)(2,1)S(1)}, u32[]{:S(2)}) copy-start(bf16[128,1680]{0,1:T(8,128)(2,1)S(1)} %copy.124) | copy-start | bytes 1290244
  387.8 3.1 collective-permute-start.12
  389.1 5.5 collective-permute-start.13
  404.6 59.9 %reduce-scatter.39.cloned.1.call-start = ((), (), s32[]{:S(2)}) async-start(), calls=%async_computation.24 | async-start | bytes 2293760
  404.7 5.0 collective-permute-start.5
  408.3 5.5 collective-permute-start.6
  423.9 125.0 %all-gather.21.cloned.1.call-start = ((), (), s32[]{:S(2)}) async-start(), calls=%async_computation.15 | async-start | bytes 2181120 | tf_op jit(solution)/shard_map/all_gather | solution.py:218
  494.4 34.7 %copy-start.39 = (f32[128,1680]{0,1:T(8,128)S(1)}, f32[128,1680]{0,1:T(8,128)}, u32[]{:S(2)}) copy-start(f32[128,1680]{0,1:T(8,128)} %get-tuple-element.166) | copy-start | bytes 2580484
  515.3 5.8 collective-permute-start.22
  516.6 5.9 collective-permute-start.21
  527.5 43.6 %all-gather.11.cloned.1.call-start = ((), (), s32[]{:S(2)}) async-start(), calls=%async_computation.10 | async-start | bytes 2181120 | tf_op jit(solution)/shard_map/all_gather | solution.py:218
  529.4 7.7 collective-permute-start.15
  530.7 6.8 collective-permute-start.14
  542.1 108.8 %all-gather.23.cloned.1.call-start = ((), (), s32[]{:S(2)}) async-start(), calls=%async_computation.16 | async-start | bytes 2181120 | tf_op jit(solution)/shard_map/all_gather | solution.py:218
  619.6 5.8 collective-permute-start.24
  620.8 5.9 collective-permute-start.23
  631.9 41.3 %all-gather.13.cloned.1.call-start = ((), (), s32[]{:S(2)}) async-start(), calls=%async_computation.11 | async-start | bytes 2181120 | tf_op jit(solution)/shard_map/all_gather | solution.py:218
  635.6 6.1 collective-permute-start.17
  636.9 6.1 collective-permute-start.16
  648.2 105.8 %all-gather.27.cloned.1.call-start = ((), (), s32[]{:S(2)}) async-start(), calls=%async_computation.18 | async-start | bytes 2181120 | tf_op jit(solution)/shard_map/all_gather | solution.py:218
  680.6 11.0 copy-start.17
  680.6 11.0 copy-start.40
  722.7 5.8 collective-permute-start.26
  724.0 5.9 collective-permute-start.25
  734.9 41.3 %all-gather.17.cloned.1.call-start = ((), (), s32[]{:S(2)}) async-start(), calls=%async_computation.13 | async-start | bytes 2181120 | tf_op jit(solution)/shard_map/all_gather | solution.py:218
  738.6 6.1 collective-permute-start.19
  739.9 6.1 collective-permute-start.18
  751.2 115.9 %all-gather.29.cloned.1.call-start = ((), (), s32[]{:S(2)}) async-start(), calls=%async_computation.19 | async-start | bytes 2150400 | tf_op jit(solution)/shard_map/all_gather | solution.py:229
  794.2 28.7 %copy-start.101 = (f32[128]{0:T(128)S(1)}, f32[128]{0:T(128)}, u32[]{:S(2)}) copy-start(f32[128]{0:T(128)} %get-tuple-element.280) | copy-start | bytes 1540
  794.3 28.7 %copy-start.103 = (f32[128]{0:T(128)S(1)}, f32[128]{0:T(128)}, u32[]{:S(2)}) copy-start(f32[128]{0:T(128)} %get-tuple-element.286) | copy-start | bytes 1540
  826.0 48.2 %all-gather.25.cloned.1.call-start = ((), (), s32[]{:S(2)}) async-start(), calls=%async_computation.17 | async-start | bytes 2150400 | tf_op jit(solution)/shard_map/all_gather | solution.py:240
  826.6 74.7 %all-gather.19.cloned.1.call-start = ((), (), s32[]{:S(2)}) async-start(), calls=%async_computation.14 | async-start | bytes 2150400 | tf_op jit(solution)/shard_map/all_gather | solution.py:229
  834.6 75.7 %all-gather.15.cloned.1.call-start = ((), (), s32[]{:S(2)}) async-start(), calls=%async_computation.12 | async-start | bytes 2150400 | tf_op jit(solution)/shard_map/all_gather | solution.py:240
  854.7 250.2 %all-reduce.59.cloned.1.call-start = ((), (), s32[]{:S(2)}) async-start(), calls=%async_computation.30 | async-start | bytes 8388608 | tf_op jit(solution)/shard_map/psum | solution.py:394
  878.4 68.7 %collective-permute-start.27 = (f32[64,20]{0,1:T(8,128)S(1)}, f32[64,20]{0,1:T(8,128)S(1)}, u32[]{:S(2)}, u32[]{:S(2)}) collective-permute-start(f32[64,20]{0,1:T(8,128)S(1)} %reshape.451), channel_id=1, source_target_pairs={{1,0},{2,1},{3,2},{4,3},{5,4},{6,5},{7,6},{9,8},{10,9},{11,10},{12... | collective-permute-start | bytes 15368 | tf_op jit(solution)/shard_map/ppermute | solution.py:29
  914.3 33.5 %collective-permute-start.20 = (f32[64,20]{0,1:T(8,128)S(1)}, f32[64,20]{0,1:T(8,128)S(1)}, u32[]{:S(2)}, u32[]{:S(2)}) collective-permute-start(f32[64,20]{0,1:T(8,128)S(1)} %reshape.449), channel_id=1, source_target_pairs={{1,0},{2,1},{3,2},{4,3},{5,4},{6,5},{7,6},{9,8},{10,9},{11,10},{12... | collective-permute-start | bytes 15368 | tf_op jit(solution)/shard_map/ppermute | solution.py:29
  (90 other events, 350.1 us)
Sparse Core Ops, SparseCore 0:
  63.2 30.0 reduce-scatter.40
  96.6 30.1 reduce-scatter.30
  129.3 29.8 reduce-scatter.44
  161.8 29.8 reduce-scatter.34
  194.6 29.8 reduce-scatter.42
  227.6 29.8 reduce-scatter.32
  300.9 27.3 reduce-scatter.46
  331.5 29.8 reduce-scatter.36
  404.7 27.3 reduce-scatter.48
  434.6 29.8 reduce-scatter.38
  527.7 21.2 all-gather.20
  550.3 20.8 all-gather.10
  632.0 18.8 all-gather.22
  652.3 20.8 all-gather.12
  735.0 18.8 all-gather.26
  755.3 20.8 all-gather.16
  826.1 16.9 all-gather.28
  844.6 20.6 all-gather.24
  866.8 20.6 all-gather.18
  888.9 20.6 all-gather.14
  947.2 157.6 all-reduce.58
where the time goes:
time: 1140 us; the launch traced here: 1120 us
  waiting for transfers between devices  353 us (31%)
  local copies, waits for them, and re-layouts  269 us (24%)
  blocking collectives  167 us (15%)
  other arithmetic  126 us (11%)
  matrix products  116 us (10%)
  starting transfers between devices  72.7 us (6%)
  between operations  17.4 us (2%)
    psum x8, blocking collectives, space_sums(): return lax.psum((first_sum, second_sum), 'space')  167 us
    unnamed x31, waiting for transfers between devices  162 us
    psum x1, waiting for transfers between devices, shards(): lax.psum(as_sent(weight_totals), 'space')  136 us
    unnamed x325, local copies, waits for them, and re-layouts  128 us
    dot_general x6, matrix products, mid_backward(): jnp.einsum('tco,toq->cq', weight_taps, stacked, preferred_element_type=jn...  49.4 us
    ppermute x12, starting transfers between devices, with_halo(): lax.ppermute(lax.slice_in_dim(block, block.shape[dim] - width, None, axis...  43.5 us
    concatenate x6, local copies, waits for them, and re-layouts, with_halo(): block = jnp.concatenate([low, block, high], axis=dim)  30 us
    all_gather x6, waiting for transfers between devices, mid_backward(): shard_rows = lax.all_gather(grad_ext, 'chan', axis=0, tiled=True)  28.9 us
  transfers between devices with their start and end apart: 49, of which 26 were waited for; matrix products, arithmetic and copies ran while one was open for 30% of the time, Pallas kernels for 0%

commit v1 on v0

v1 whole, which is shorter than its diff:
```python
import collections
import functools

import jax
import jax.numpy as jnp
import numpy as np
from jax import lax
from jax.experimental import pallas as pl
from jax.experimental.pallas import tpu as pltpu
from jax.sharding import PartitionSpec as P

MICRO = 2
WIN = 20
MOST_SIDE = 9
EXTRA = MOST_SIDE - 1
BLOCK = 16
ROW_BLOCK = 64
GAP = 8
EPS = 1e-05
SLACK_BYTES = 6 * 1024 * 1024
LOW = jnp.bfloat16
FULL = jnp.float32

PLAN_FIELDS = ["chans", "spaces", "splits", "rows_dev", "own_rows", "bases", "pitch", "width"]
PLAN_FIELDS += ["spots", "chans_in", "chans_out", "wide"]
Plan = collections.namedtuple("Plan", PLAN_FIELDS)

VMEM = pl.BlockSpec(memory_space=pltpu.VMEM)
SMEM = pl.BlockSpec(memory_space=pltpu.SMEM)
HBM = pl.BlockSpec(memory_space=pltpu.HBM)


def flipped(value, axis, bit):
    count = lax.axis_size(axis)
    return lax.ppermute(value, axis, [(i, i ^ bit) for i in range(count)])


def from_next(value):
    count = lax.axis_size("space")
    return lax.ppermute(value, "space", [(i + 1, i) for i in range(count - 1)])


def to_next(value):
    count = lax.axis_size("space")
    return lax.ppermute(value, "space", [(i, i + 1) for i in range(count - 1)])


def exchanged(value, chan_bits, space_bits, plan):
    count = plan.chans * plan.spaces
    flip = chan_bits * plan.spaces + space_bits
    return lax.ppermute(value, ("chan", "space"), [(i, i ^ flip) for i in range(count)])


def tied(value, *others):
    return lax.optimization_barrier((value, others))[0]


def gathered(own, plan, then=()):
    parts = {0: own}
    for rel in range(1, plan.chans):
        bit = rel & -rel
        source = parts[rel ^ bit]
        if rel != bit and then:
            source = tied(source, *then)
        parts[rel] = flipped(source, "chan", bit)
    return [parts[rel] for rel in range(plan.chans)]


def swapped(parts, plan):
    return [parts[0]] + [flipped(parts[rel], "chan", rel) for rel in range(1, plan.chans)]


def micro_sums(value, plan, jobs=()):
    bits = []
    bit = 1
    while bit < plan.splits:
        bits.append((bit, 0))
        bit *= 2
    bit = 1
    while bit < plan.spaces:
        bits.append((0, bit))
        bit *= 2
    for i in range(0, len(bits), 2):
        pair = bits[i : i + 2]
        one = exchanged(value, *pair[0], plan)
        if len(pair) == 2:
            two = exchanged(value, *pair[1], plan)
            both = exchanged(value, pair[0][0] ^ pair[1][0], pair[0][1] ^ pair[1][1], plan)
        if i == 0 and jobs:
            one = tied(one, *[job() for job in jobs])
        value = value + one
        if len(pair) == 2:
            value = value + (two + both)
    return value


class WeightSum:
    def __init__(self, keep, send, plan, across_first):
        self.send, self.plan = send, plan
        self.pair = (keep, flipped(send, "chan", 1))
        chan_steps, space_steps = [], []
        bit = 2
        while bit < plan.chans:
            chan_steps.append(("chan", bit))
            bit *= 2
        bit = 1
        while bit < plan.spaces:
            space_steps.append(("space", bit))
            bit *= 2
        if across_first:
            self.steps = space_steps[:1] + chan_steps + space_steps[1:]
        else:
            self.steps = chan_steps + space_steps
        self.gathers = [bit for _, bit in space_steps[::-1]]
        self.whole = None

    def mine(self, bit):
        return (lax.axis_index("space") // bit) % 2

    def added(self, pick):
        kept, received = (pick(part).astype(FULL) for part in self.pair)
        return (kept + received).astype(LOW)

    def advance(self):
        if self.steps:
            axis, bit = self.steps.pop(0)
            if axis == "chan":
                kept = self.added(lambda part: part[0::2])
                sent = self.added(lambda part: part[1::2])
            else:
                half = self.pair[0].shape[1] // 2
                at = self.mine(bit) * half
                kept = self.added(lambda part: lax.dynamic_slice_in_dim(part, at, half, 1))
                sent = self.added(lambda part: lax.dynamic_slice_in_dim(part, half - at, half, 1))
            self.pair = (kept, flipped(sent, axis, bit))
            return sent
        bit = self.gathers.pop(0)
        if self.whole is None:
            self.whole = self.added(lambda part: part)[0]
        else:
            self.whole = self.ordered(*self.pair)
        self.pair = (self.whole, flipped(self.whole, "space", bit), bit)
        return self.whole

    def ordered(self, own, received, bit):
        low = jnp.concatenate([own, received], axis=0)
        high = jnp.concatenate([received, own], axis=0)
        return jnp.where(self.mine(bit) == 0, low, high)

    def halves(self):
        while self.steps or self.gathers:
            self.advance()
        return self.pair


def tiles(count, size):
    return [slice(i, i + size) for i in range(0, count, size)]


def logistic(u):
    return 1.0 / (1.0 + jnp.exp(-u))


def slope(u):
    g = logistic(u)
    return g * (1.0 + u * (1.0 - g))


def moments(stat, inv_count):
    mean = stat[0:1, :] * inv_count
    inverse = lax.rsqrt(stat[1:2, :] * inv_count - mean * mean + EPS)
    return mean, inverse


def dot(a, b):
    return lax.dot_general(a, b, (((1,), (0,)), ((), ())), preferred_element_type=FULL)


def dot_t(a, b):
    return lax.dot_general(a, b, (((1,), (1,)), ((), ())), preferred_element_type=FULL)


def unit(count):
    rows = lax.broadcasted_iota(jnp.int32, (count, count), 0)
    columns = lax.broadcasted_iota(jnp.int32, (count, count), 1)
    return jnp.where(rows == columns, 1.0, 0.0).astype(LOW)


def clear_gaps(ref, spots):
    zero = jnp.zeros((GAP, ref.shape[-1]), ref.dtype)
    ref[pl.ds(0, GAP), :] = zero
    ref[pl.ds(GAP + spots, GAP), :] = zero


def column_sum(x):
    return jnp.sum(x, axis=0, keepdims=True)


def start_shards(chan, shard_refs, w_ref, sems):
    size = shard_refs[0].shape[2]
    copies = []
    for rel, ref in enumerate(shard_refs):
        place = pl.ds(pl.multiple_of((chan ^ rel) * size, size), size)
        copy = pltpu.make_async_copy(ref, w_ref.at[:, :, place, :], sems.at[rel])
        copy.start()
        copies.append(copy)
    return copies


def matmul_tile(plan):
    for size in (288, 192, 144, 96, 64):
        if plan.spots % size == 0:
            return size
    return plan.spots


def vector_tile(plan):
    return 2 * plan.pitch // 4 if plan.pitch % 32 == 0 else plan.pitch


def spread_features_kernel(plan, chan_ref, x_ref, halo_ref, picks_ref, left_ref, right_ref, out_ref):
    chan = chan_ref[0]
    size, lanes = plan.chans_in, BLOCK * 4 * plan.width
    columns = MOST_SIDE

    def stacked(part):
        blank = jnp.zeros_like(part[0])
        even, odd = [], []
        for m in range(MICRO):
            even += [part[m], blank]
            odd += [blank, part[m]]
        return jnp.concatenate(even, 0), jnp.concatenate(odd, 0)

    have = x_ref.shape[2]
    for j in range(-(-(plan.rows_dev + EXTRA) // BLOCK)):
        start = j * lanes
        if start + lanes <= have:
            even, odd = stacked([x_ref[m, :, start : start + lanes] for m in range(MICRO)])
            result = dot_t(picks_ref[0], even) + dot_t(picks_ref[1], odd)
        else:
            even, odd = stacked([x_ref[m, :, start:have] for m in range(MICRO)])
            result = dot_t(left_ref[0], even) + dot_t(left_ref[1], odd)
            even, odd = stacked([halo_ref[m] for m in range(MICRO)])
            result += dot_t(right_ref[0], even) + dot_t(right_ref[1], odd)
        result = result.astype(LOW)
        for split, base in enumerate(plan.bases):
            row = j * BLOCK - base
            if row < 0 or row >= plan.pitch:
                continue
            for m in range(MICRO):
                to = chan ^ (m * plan.splits + split)
                for phase in range(2):
                    for c in range(columns):
                        at = (phase * columns + c) * BLOCK
                        part = result[at : at + BLOCK, m * 2 * size : (m + 1) * 2 * size]
                        spot = c * plan.pitch + row
                        out_ref[to, phase, spot : spot + BLOCK] = part


def spread_rows_kernel(plan, chan_ref, x_ref, halo_ref, pick_ref, left_ref, right_ref, out_ref):
    chan = chan_ref[0]
    size, spots = plan.chans_out, ROW_BLOCK * plan.width
    have = x_ref.shape[1]
    for j in range(-(-(plan.rows_dev + EXTRA) // ROW_BLOCK)):
        start = j * spots
        for m in range(MICRO):
            if start + spots <= have:
                result = dot(pick_ref[...], x_ref[m, start : start + spots])
            else:
                result = dot(left_ref[...], x_ref[m, start:have]) + dot(right_ref[...], halo_ref[m])
            result = result.astype(LOW)
            for split, base in enumerate(plan.bases):
                low, high = max(j * ROW_BLOCK, base), min((j + 1) * ROW_BLOCK, base + plan.pitch)
                if low >= high:
                    continue
                to = chan ^ (m * plan.splits + split)
                for c in range(MOST_SIDE):
                    at = c * ROW_BLOCK + low - j * ROW_BLOCK
                    spot = c * plan.pitch + low - base
                    out_ref[to, spot : spot + high - low] = result[at : at + high - low]


def laid_rows(plan, whole_ref, m, c, low, high, phase=None):
    pieces = []
    for row in range(low, high, BLOCK):
        total = None
        for split, base in enumerate(plan.bases):
            if not base <= row < base + plan.pitch:
                continue
            spots = pl.ds(c * plan.pitch + row - base, BLOCK)
            at = m * plan.splits + split
            part = whole_ref[at, spots] if phase is None else whole_ref[at, phase, spots]
            total = part if total is None else total + part
        pieces.append(total)
    return pieces


def join_rows_kernel(plan, chan_ref, picks_ref, left_ref, right_ref, *refs):
    parts = refs[: plan.chans]
    out_ref, tail_ref, whole_ref = refs[plan.chans :]
    chan = chan_ref[0]
    for rel in range(plan.chans):
        whole_ref[chan ^ rel] = parts[rel][...]
    spots = ROW_BLOCK * plan.width
    have = out_ref.shape[1]
    limit = plan.rows_dev + EXTRA
    for j in range(-(-limit // ROW_BLOCK)):
        start = j * spots
        low, high = j * ROW_BLOCK, min((j + 1) * ROW_BLOCK, limit)
        for m in range(MICRO):
            pieces = []
            for c in range(MOST_SIDE):
                pieces += laid_rows(plan, whole_ref, m, c, low, high)
                if high - low < ROW_BLOCK:
                    blank = (ROW_BLOCK - high + low, plan.chans_out)
                    pieces.append(jnp.zeros(blank, LOW))
            rows = jnp.concatenate(pieces, 0)
            if start + spots <= have:
                out_ref[m, start : start + spots] = dot(picks_ref[...], rows).astype(LOW)
            else:
                out_ref[m, start:have] = dot(left_ref[...], rows).astype(LOW)
                tail_ref[m] = dot(right_ref[...], rows).astype(LOW)


def join_features_kernel(plan, chan_ref, picks_ref, left_ref, right_ref, *refs):
    parts = refs[: plan.chans]
    out_ref, tail_ref, whole_ref = refs[plan.chans :]
    chan = chan_ref[0]
    for rel in range(plan.chans):
        whole_ref[chan ^ rel] = parts[rel][...]
    size = plan.chans_in
    one = unit(2 * size)
    lanes = BLOCK * 4 * plan.width
    have = out_ref.shape[2]
    for j in range(-(-(plan.rows_dev + EXTRA) // BLOCK)):
        start = j * lanes
        first, second = [], []
        for m in range(MICRO):
            pieces = []
            for phase in range(2):
                for c in range(MOST_SIDE):
                    row = j * BLOCK
                    pieces += laid_rows(plan, whole_ref, m, c, row, row + BLOCK, phase)
            turned = dot_t(one, jnp.concatenate(pieces, 0)).astype(LOW)
            first.append(turned[:size])
            second.append(turned[size:])
        first, second = jnp.concatenate(first, 0), jnp.concatenate(second, 0)
        if start + lanes <= have:
            result = dot(first, picks_ref[0]) + dot(second, picks_ref[1])
            for m in range(MICRO):
                out_ref[m, :, start : start + lanes] = result[m * size : (m + 1) * size]
        else:
            result = dot(first, left_ref[0]) + dot(second, left_ref[1])
            tail = dot(first, right_ref[0]) + dot(second, right_ref[1])
            for m in range(MICRO):
                out_ref[m, :, start:have] = result[m * size : (m + 1) * size]
                tail_ref[m] = tail[m * size : (m + 1) * size].astype(LOW)


def entry_copies(plan, shard_refs, w_ref, wp_ref, sems):
    copies = []
    for rel in range(plan.chans):
        for a in range(3):
            sem = sems.at[7 * rel + 2 * a]
            source = shard_refs[rel].at[pl.ds(3 * a + 1, 2)]
            copies.append(pltpu.make_async_copy(source, w_ref.at[a, 0, rel], sem))
            sem = sems.at[7 * rel + 2 * a + 1]
            source = shard_refs[rel].at[3 * a]
            copies.append(pltpu.make_async_copy(source, w_ref.at[a, 1, rel, 1], sem))
        source = shard_refs[rel].at[9]
        copies.append(pltpu.make_async_copy(source, wp_ref.at[rel, 0], sems.at[7 * rel + 6]))
    for copy in copies:
        copy.start()
    for rel in range(plan.chans):
        blank = jnp.zeros(wp_ref.shape[2:], LOW)
        wp_ref[rel, 1] = blank
        for a in range(3):
            w_ref[a, 1, rel, 0] = blank
    return copies


def entry_forward_kernel(plan, marks_ref, *refs):
    n = plan.chans
    x_refs, shard_refs = refs[:n], refs[n : 2 * n]
    e_ref, p_ref, stat_ref, xm_ref = refs[2 * n : 2 * n + 4]
    w_ref, wp_ref, xs_ref, am_ref, sems = refs[2 * n + 4 :]
    copies = entry_copies(plan, shard_refs, w_ref, wp_ref, sems)
    size = 2 * plan.chans_in
    deep = n * size
    pitch = plan.pitch
    for k in range(3):
        am_ref[k, 0:pitch] = jnp.zeros((pitch, deep), LOW)
    clear_gaps(xs_ref, plan.spots)
    for rel in range(n):
        lanes = slice(rel * size, (rel + 1) * size)
        for t in tiles(plan.spots, vector_tile(plan)):
            own = marks_ref[t, 0:1]
            for row in range(2):
                value = x_refs[rel][row, t].astype(FULL) * own
                low = value.astype(LOW)
                xm_ref[row, t, lanes] = low
                am_ref[row, pitch + t.start : pitch + t.stop, lanes] = low
                if row == 1:
                    xs_ref[GAP + t.start : GAP + t.stop, lanes] = value
    for t in tiles(plan.spots, vector_tile(plan)):
        above = xs_ref[GAP + t.start - 1 : GAP + t.stop - 1] * marks_ref[t, 1:2]
        am_ref[2, pitch + t.start : pitch + t.stop] = above.astype(LOW)
    for copy in copies:
        copy.wait()
    weights = w_ref[...].reshape(6 * deep, plan.wide)
    proj = wp_ref[...].reshape(deep, plan.wide)
    sums = [0.0] * 4
    for t in tiles(plan.spots, matmul_tile(plan)):
        own = marks_ref[t, 0:1]
        pieces = []
        for k in (2, 0, 1):
            pieces.append(am_ref[k, pitch + t.start : pitch + t.stop])
            pieces.append(am_ref[k, t])
        z = dot(jnp.concatenate(pieces, 1), weights)
        e_ref[t] = z
        p = dot(pieces[2], proj)
        p_ref[t] = p
        zm, pm = z * own, p * own
        for i, term in enumerate((zm, zm * z, pm, pm * p)):
            sums[i] = sums[i] + column_sum(term)
    stat_ref[...] = jnp.concatenate(sums, 0)


def mid_forward_kernel(plan, layers, chan_ref, inv_ref, marks_ref, par_ref, *refs):
    k = len(layers)
    n = plan.chans
    z_refs, stat_refs, shard_refs = refs[:k], refs[k : 2 * k], refs[2 * k : 2 * k + n]
    outs = refs[2 * k + n :]
    if k == 2:
        z_ref, out_stat_ref, a_ref, h_ref, w_ref, xs_ref, xa_ref, sems = outs
    else:
        z_ref, out_stat_ref, a_ref, w_ref, xs_ref, xa_ref, sems = outs
        h_ref = None
    copies = start_shards(chan_ref[0], shard_refs, w_ref, sems)
    inv = inv_ref[0]
    norms = [moments(stat[...], inv) for stat in stat_refs]
    wide, pitch = plan.wide, plan.pitch
    clear_gaps(xs_ref, plan.spots)
    for i in range(3):
        blank = jnp.zeros((pitch, wide), LOW)
        xa_ref[i, 0:pitch] = blank
        xa_ref[i, pitch + plan.spots : 2 * pitch + plan.spots] = blank
    for t in tiles(plan.spots, vector_tile(plan)):
        own = marks_ref[t, 0:1]
        u = 0.0
        for (mean, inverse), src, j in zip(norms, z_refs, layers):
            u = u + (par_ref[j : j + 1] * ((src[t] - mean) * inverse) + par_ref[5 + j : 6 + j])
        u = u * own
        a = u * logistic(u)
        if h_ref is not None:
            h_ref[t] = a
        xs_ref[GAP + t.start : GAP + t.stop] = a
        low = a.astype(LOW)
        a_ref[t] = low
        xa_ref[1, pitch + t.start : pitch + t.stop] = low
    for t in tiles(plan.spots, vector_tile(plan)):
        for i, step in ((0, -1), (2, 1)):
            part = xs_ref[GAP + t.start + step : GAP + t.stop + step]
            part = part * marks_ref[t, 1 + i // 2 : 2 + i // 2]
            xa_ref[i, pitch + t.start : pitch + t.stop] = part.astype(LOW)
    for copy in copies:
        copy.wait()
    weights = w_ref[...].reshape(9 * wide, wide)
    total, square = 0.0, 0.0
    for t in tiles(plan.spots, matmul_tile(plan)):
        own = marks_ref[t, 0:1]
        pieces = []
        for a in range(3):
            for b in range(3):
                pieces.append(xa_ref[a, t.start + b * pitch : t.stop + b * pitch])
        z = dot(jnp.concatenate(pieces, 1), weights)
        z_ref[t] = z
        zm = z * own
        total = total + column_sum(zm)
        square = square + column_sum(zm * z)
    out_stat_ref[...] = jnp.concatenate([total, square], 0)


def head_kernel(plan, chan_ref, inv_ref, marks_ref, par_ref, z_ref, stat_ref, h_ref, *refs):
    n = plan.chans
    og_refs = refs[:n]
    out_ref, g_ref, out_stat_ref, og_ref = refs[n:]
    chan = chan_ref[0]
    for rel in range(n):
        og_ref[chan ^ rel] = og_refs[rel][...]
    mean, inverse = moments(stat_ref[...], inv_ref[0])
    size = plan.chans_out
    for j in range(n):
        lanes = slice(j * size, (j + 1) * size)
        total, dotted = 0.0, 0.0
        for t in tiles(plan.spots, plan.pitch):
            own = marks_ref[t, 0:1]
            hat = (z_ref[t, lanes] - mean[:, lanes]) * inverse[:, lanes]
            u = own * (par_ref[4:5, lanes] * hat + par_ref[9:10, lanes]) + h_ref[t, lanes]
            s = logistic(u)
            out_ref[chan ^ j, t] = (u * s).astype(LOW)
            q = og_ref[j, t].astype(FULL) * (s * (1.0 + u * (1.0 - s))) * own
            g_ref[t, lanes] = q
            total = total + column_sum(q)
            dotted = dotted + column_sum(q * hat)
        out_stat_ref[0:1, lanes] = total
        out_stat_ref[1:2, lanes] = dotted


def norm_back(own, q, z, norm, gain, total, dotted, inv):
    mean, inverse = norm
    hat = (z - mean) * inverse
    return own * (gain * inverse) * (q - total * inv - hat * (dotted * inv))


def mid_backward_kernel(plan, j, kind, chan_ref, inv_ref, marks_ref, par_ref, *refs):
    n = plan.chans
    g_ref, z_ref, stat_ref, back_ref = refs[:4]
    shard_refs = refs[4 : 4 + n]
    refs = refs[4 + n :]
    add_ref = short_z_ref = None
    if kind == "join":
        src_refs, src_stats, add_ref = refs[:2], refs[2:4], refs[4]
        refs = refs[5:]
        layers = (1, 2)
    elif kind == "entry":
        src_refs, src_stats, short_z_ref, short_stat_ref = refs[:1], refs[1:2], refs[2], refs[3]
        refs = refs[4:]
        layers = (0,)
    else:
        src_refs, src_stats = refs[:1], refs[1:2]
        refs = refs[2:]
        layers = (3,)
    ga_ref, next_ref, out_stat_ref = refs[:3]
    refs = refs[3:]
    if kind == "entry":
        short_ref, refs = refs[0], refs[1:]
    w_ref, s0_ref, s2_ref, sems = refs
    copies = start_shards(chan_ref[0], shard_refs, w_ref, sems)
    inv = inv_ref[0]
    wide, pitch = plan.wide, plan.pitch
    norm = moments(stat_ref[...], inv)
    total, dotted = back_ref[0:1], back_ref[1:2]
    for ref in (s0_ref, s2_ref):
        clear_gaps(ref, plan.spots)
    for i in range(3):
        blank = jnp.zeros((pitch, wide), LOW)
        ga_ref[i, 0:pitch] = blank
        ga_ref[i, pitch + plan.spots : 2 * pitch + plan.spots] = blank
    if kind == "entry":
        short_norm = moments(short_stat_ref[...], inv)
    for t in tiles(plan.spots, vector_tile(plan)):
        own, upper, lower = (marks_ref[t, i : i + 1] for i in range(3))
        g = g_ref[t]
        gz = norm_back(own, g, z_ref[t], norm, par_ref[j : j + 1], total, dotted, inv)
        low = gz.astype(LOW)
        gz = low.astype(FULL)
        ga_ref[1, pitch + t.start : pitch + t.stop] = low
        s0_ref[GAP + t.start : GAP + t.stop] = gz * upper
        s2_ref[GAP + t.start : GAP + t.stop] = gz * lower
        if kind == "entry":
            back = norm_back(
                own, g, short_z_ref[t], short_norm, par_ref[2:3], total, back_ref[2:3], inv
            )
            short_ref[t] = back.astype(LOW)
    for t in tiles(plan.spots, vector_tile(plan)):
        first, last = GAP + t.start, GAP + t.stop
        to = slice(pitch + t.start, pitch + t.stop)
        ga_ref[0, to] = s0_ref[first + 1 : last + 1].astype(LOW)
        ga_ref[2, to] = s2_ref[first - 1 : last - 1].astype(LOW)
    for copy in copies:
        copy.wait()
    norms = [moments(stat[...], inv) for stat in src_stats]
    sums = [0.0] * (1 + len(layers))
    weights = jnp.concatenate([w_ref[a, b] for a in range(3) for b in range(3)], 1)
    for t in tiles(plan.spots, matmul_tile(plan)):
        own = marks_ref[t, 0:1]
        pieces = []
        for a in range(3):
            for b in range(3):
                back = (2 - b) * pitch
                pieces.append(ga_ref[a, t.start + back : t.stop + back])
        gx = dot_t(jnp.concatenate(pieces, 1), weights)
        u = 0.0
        hats = []
        for (mean, inverse), src, i in zip(norms, src_refs, layers):
            hat = (src[t] - mean) * inverse
            hats.append(hat)
            u = u + (par_ref[i : i + 1] * hat + par_ref[5 + i : 6 + i])
        u = u * own
        if add_ref is not None:
            gx = gx + add_ref[t]
        q = gx * slope(u) * own
        next_ref[t] = q
        sums[0] = sums[0] + column_sum(q)
        for i, hat in enumerate(hats):
            sums[1 + i] = sums[1 + i] + column_sum(q * hat)
    out_stat_ref[...] = jnp.concatenate(sums, 0)


def entry_norm_kernel(plan, inv_ref, marks_ref, par_ref, g_ref, e_ref, stat_ref, back_ref, gm_ref, s_ref):
    inv = inv_ref[0]
    norm = moments(stat_ref[...], inv)
    clear_gaps(s_ref, plan.spots)
    for k in range(2):
        gm_ref[k, plan.spots : plan.spots + plan.pitch] = jnp.zeros((plan.pitch, plan.wide), LOW)
    for t in tiles(plan.spots, vector_tile(plan)):
        own, upper = marks_ref[t, 0:1], marks_ref[t, 1:2]
        gz = norm_back(
            own, g_ref[t], e_ref[t], norm, par_ref[0:1], back_ref[0:1], back_ref[1:2], inv
        )
        low = gz.astype(LOW)
        gm_ref[0, t] = low
        s_ref[GAP + t.start : GAP + t.stop] = low.astype(FULL) * upper
    for t in tiles(plan.spots, vector_tile(plan)):
        gm_ref[1, t] = s_ref[GAP + t.start + 1 : GAP + t.stop + 1].astype(LOW)


def entry_backward_kernel(plan, marks_ref, gm_ref, short_ref, *refs):
    n = plan.chans
    shard_refs = refs[:n]
    gx_ref, w_ref, wp_ref, sems = refs[n:]
    for copy in entry_copies(plan, shard_refs, w_ref, wp_ref, sems):
        copy.wait()
    size = 2 * plan.chans_in
    deep = n * size
    pitch, wide = plan.pitch, plan.wide

    def part(a, side):
        return w_ref[a, side].reshape(deep, wide)

    top_weights = [part(1, 0), part(1, 1), wp_ref[...].reshape(deep, wide)]
    top_weights = jnp.concatenate(top_weights, 1)
    low_weights = jnp.concatenate([part(2, 0), part(2, 1), part(0, 0), part(0, 1)], 1)
    for t in tiles(plan.spots, matmul_tile(plan)):
        own = marks_ref[t, 0:1]
        right = slice(t.start + pitch, t.stop + pitch)
        here = [gm_ref[0, t], gm_ref[0, right]]
        top = dot_t(jnp.concatenate(here + [short_ref[t]], 1), top_weights)
        here += [gm_ref[1, t], gm_ref[1, right]]
        low = dot_t(jnp.concatenate(here, 1), low_weights)
        for row, value in enumerate((top, low)):
            value = (value * own).astype(LOW)
            for rel in range(n):
                gx_ref[rel, row, t] = value[:, rel * size : (rel + 1) * size]


def mid_weight_kernel(plan, chan_ref, a_ref, ga_ref, keep_ref, send_ref, turned_ref, at_ref):
    wide, pitch = plan.wide, plan.pitch
    turned_ref[...] = dot_t(unit(wide), a_ref[...]).astype(LOW)
    chan = chan_ref[0]
    size = plan.chans_out
    for rel in range(plan.chans):
        place = pl.ds(pl.multiple_of((chan ^ rel) * size, size), size)
        at_ref[rel * size : (rel + 1) * size] = turned_ref[place]
    for a in range(3):
        for b in range(3):
            back = (2 - b) * pitch
            rows = slice((3 * a + b) * size, (3 * a + b + 1) * size)
            part = dot(at_ref[...], ga_ref[a, back : back + plan.spots]).astype(LOW)
            for rel in range(plan.chans):
                target = send_ref if rel & 1 else keep_ref
                target[rel // 2, rows] = part[rel * size : (rel + 1) * size]


def entry_weight_kernel(plan, xm_ref, gm_ref, short_ref, keep_ref, send_ref, xt_ref):
    n, size, wide, pitch = plan.chans, plan.chans_in, plan.wide, plan.pitch
    whole = unit(n * 2 * size)
    for row in range(2):
        xt_ref[row] = dot_t(whole, xm_ref[row]).astype(LOW)

    def put(tap, rel, value):
        target = send_ref if rel & 1 else keep_ref
        target[rel // 2, tap * size : (tap + 1) * size] = value

    def product(row, right):
        return dot(xt_ref[row], right).astype(LOW)

    for row, grad, a in ((0, 0, 1), (1, 0, 2), (1, 1, 0)):
        big = product(row, gm_ref[grad, 0 : plan.spots])
        side = product(row, gm_ref[grad, pitch : pitch + plan.spots])
        for rel in range(n):
            at = 2 * rel * size
            put(3 * a + 1, rel, big[at : at + size])
            put(3 * a + 2, rel, big[at + size : at + 2 * size])
            put(3 * a, rel, side[at + size : at + 2 * size])
    proj = product(0, short_ref[...])
    for rel in range(n):
        put(9, rel, proj[2 * rel * size : (2 * rel + 1) * size])


def mid_assembly_kernel(count, mine_ref, *refs):
    parts, out_ref, hold_ref, sems = refs[: 2 * count], *refs[2 * count :]
    half = parts[0].shape[0]
    copies = []
    for i, part in enumerate(parts):
        hold_ref[i] = part[...].astype(FULL)
        at = mine_ref[0] if i % 2 == 0 else 1 - mine_ref[0]
        rows = pl.ds(pl.multiple_of(at * half, 8), half)
        copy = pltpu.make_async_copy(hold_ref.at[i], out_ref.at[i // 2, rows], sems.at[i])
        copy.start()
        copies.append(copy)
    for copy in copies:
        copy.wait()


def entry_assembly_kernel(mine_ref, own_ref, other_ref, conv_ref, proj_ref, hold_ref, sems):
    half = own_ref.shape[0]
    for i, part in enumerate((own_ref, other_ref)):
        at = mine_ref[0] if i == 0 else 1 - mine_ref[0]
        hold_ref[pl.ds(pl.multiple_of(at * half, 8), half)] = part[...].astype(FULL)
    cut = conv_ref.shape[0]
    copies = [
        pltpu.make_async_copy(hold_ref.at[pl.ds(0, cut)], conv_ref, sems.at[0]),
        pltpu.make_async_copy(hold_ref.at[pl.ds(cut, proj_ref.shape[0])], proj_ref, sems.at[1]),
    ]
    for copy in copies:
        copy.start()
    for copy in copies:
        copy.wait()


def call(kernel, operands, specs, outs, out_specs, scratch, flops, name):
    bytes_moved = sum(int(np.prod(o.shape)) * o.dtype.itemsize for o in operands)
    bytes_moved += sum(int(np.prod(s)) * jnp.dtype(d).itemsize for s, d in outs)
    shapes = [jax.ShapeDtypeStruct(s, d) for s, d in outs]
    held = SLACK_BYTES
    for one in scratch:
        if one.memory_space == pltpu.VMEM:
            held += int(np.prod(one.shape)) * jnp.dtype(one.dtype).itemsize
    return pl.pallas_call(
        kernel,
        out_shape=shapes,
        in_specs=specs,
        out_specs=out_specs,
        scratch_shapes=scratch,
        compiler_params=pltpu.CompilerParams(vmem_limit_bytes=held),
        cost_estimate=pl.CostEstimate(
            flops=int(flops), bytes_accessed=int(bytes_moved), transcendentals=0
        ),
        name=name,
    )(*operands)


def feature_picks(plan):
    width, columns = plan.width, MOST_SIDE
    picks = np.zeros((2, 2 * columns * BLOCK, BLOCK * 4 * width), np.float32)
    for side in range(2):
        for phase in range(2):
            for c in range(columns):
                for r in range(BLOCK):
                    source = (2 * r + phase) * 2 * width + 2 * c + side
                    picks[side, (phase * columns + c) * BLOCK + r, source] = 1.0
    return picks


def row_picks(plan):
    width = plan.width
    picks = np.zeros((MOST_SIDE * ROW_BLOCK, ROW_BLOCK * width), np.float32)
    for c in range(MOST_SIDE):
        for r in range(ROW_BLOCK):
            picks[c * ROW_BLOCK + r, r * width + c] = 1.0
    return picks


def cut_picks(picks, rows, per_row, rows_dev, turned=False):
    own = rows_dev % rows * per_row
    extra = EXTRA * per_row
    parts = (picks, picks[..., :own], picks[..., own : own + extra])
    return [jnp.asarray((part.T if turned else part).astype(LOW)) for part in parts]


def marks_of(plan, sizes, top, first):
    sides = sizes // 2
    starts = jnp.cumsum(sides) - sides
    here = top + jnp.arange(plan.pitch, dtype=jnp.int32)
    inside = (
        (here[:, None] >= starts[None, :]) & (here[:, None] < (starts + sides)[None, :])
    ).astype(jnp.int32)
    begins = jnp.sum(inside * starts[None, :], axis=1)
    widths = jnp.sum(inside * sides[None, :], axis=1)
    local = here - begins
    owned = (widths > 0) & (begins >= first) & (begins < first + plan.own_rows)
    columns = jnp.arange(MOST_SIDE, dtype=jnp.int32)
    own = owned[None, :] & (columns[:, None] < widths[None, :])
    upper = jnp.broadcast_to((owned & (local > 0))[None, :], own.shape)
    lower = jnp.broadcast_to((owned & (local < widths - 1))[None, :], own.shape)
    marks = jnp.stack([own, upper, lower] + [jnp.zeros_like(own)] * 5, axis=-1)
    total = jnp.sum((sides * sides).astype(FULL))
    return marks.astype(FULL).reshape(plan.spots, 8), (1.0 / total).reshape(1)


def shards(features, image_sizes, conv_in_w, proj_w, conv_mid_w, norm_gain, norm_bias, out_grad):
    chans, spaces = lax.axis_size("chan"), lax.axis_size("space")
    splits = chans // MICRO
    width = WIN // 2
    rows_dev = features.shape[2] // (4 * width)
    own_rows = rows_dev // splits
    bases = tuple(split * own_rows // BLOCK * BLOCK for split in range(splits))
    need = max(split * own_rows - bases[split] for split in range(splits)) + own_rows + EXTRA
    pitch = -(-need // BLOCK) * BLOCK
    reach = -(-(rows_dev + EXTRA) // BLOCK) * BLOCK
    assert max(bases) + pitch <= reach and rows_dev + EXTRA == reach
    chans_in, chans_out = features.shape[1], norm_gain.shape[1]
    spots = MOST_SIDE * pitch
    plan = Plan(
        chans, spaces, splits, rows_dev, own_rows, bases, pitch, width, spots,
        chans_in, chans_out, chans * chans_out,
    )
    wide = plan.wide
    chan = lax.axis_index("chan")
    micro, split = chan // splits, chan % splits
    here = lax.axis_index("space") * rows_dev
    first = here + split * own_rows
    chan_at = chan.astype(jnp.int32).reshape(1)

    picks = cut_picks(feature_picks(plan), BLOCK, 4 * width, rows_dev)
    halo = from_next(features[:, :, : EXTRA * 4 * width])
    (spread,) = call(
        functools.partial(spread_features_kernel, plan),
        (chan_at, features, halo, *picks),
        [SMEM] + [VMEM] * 5,
        [((chans, 2, spots, 2 * chans_in), LOW)],
        [VMEM],
        [],
        2 * 2 * 2 * spots * 640 * chans * 2 * chans_in,
        "spread_features",
    )
    x_parts = swapped(spread, plan)
    entry_own = jnp.concatenate([conv_in_w.reshape(9, chans_in, wide), proj_w[None]], axis=0)
    entry_shards = gathered(entry_own, plan)

    slots = jnp.concatenate([norm_gain, norm_bias], axis=0)
    slots = lax.dynamic_update_slice(
        jnp.zeros((10, wide), FULL), slots, (jnp.int32(0), chan * chans_out)
    )
    bit = 1
    while bit < chans:
        slots = slots + flipped(slots, "chan", bit)
        bit *= 2
    pars = slots
    mid_first = tied(conv_mid_w[0], *x_parts, *entry_shards, pars)

    sizes = lax.dynamic_index_in_dim(image_sizes, micro, 0, keepdims=False)
    bases_at = jnp.asarray(bases, jnp.int32)[split]
    marks, inv = marks_of(plan, sizes, here + bases_at, first)

    conv_flops = 2 * spots * 9 * wide * wide
    field = ((spots, wide), FULL)
    deep = chans * 2 * chans_in
    entry_scratch = [
        pltpu.VMEM((3, 2, chans, 2, chans_in, wide), LOW),
        pltpu.VMEM((chans, 2, chans_in, wide), LOW),
    ]
    padded = pltpu.VMEM((spots + 2 * GAP, wide), FULL)
    z0, zp, stats, xm = call(
        functools.partial(entry_forward_kernel, plan),
        (marks, *x_parts, *entry_shards),
        [VMEM] * (1 + chans) + [HBM] * chans,
        [field, field, ((4, wide), FULL), ((2, spots, deep), LOW)],
        [VMEM] * 4,
        entry_scratch
        + [
            pltpu.VMEM((spots + 2 * GAP, deep), FULL),
            pltpu.VMEM((3, spots + pitch, deep), LOW),
            pltpu.SemaphoreType.DMA((7 * chans,)),
        ],
        2 * spots * 7 * deep * wide,
        "entry_forward",
    )
    mid_shards = [gathered(mid_first, plan, (stats,))]
    mid_second = tied(conv_mid_w[1], stats)
    stats = micro_sums(stats, plan)
    stat0, statp = stats[0:2], stats[2:4]

    weight_scratch = pltpu.VMEM((3, 3, wide, wide), LOW)
    shard_sems = pltpu.SemaphoreType.DMA((chans,))

    def mid_forward(layers, sources, source_stats, weights, name):
        outs = [field, ((2, wide), FULL), ((spots, wide), LOW)]
        if len(layers) == 2:
            outs.append(field)
        k = len(layers)
        return call(
            functools.partial(mid_forward_kernel, plan, layers),
            (chan_at, inv, marks, pars, *sources, *source_stats, *weights),
            [SMEM, SMEM] + [VMEM] * (2 + 2 * k) + [HBM] * chans,
            outs,
            [VMEM] * len(outs),
            [weight_scratch, padded, pltpu.VMEM((3, spots + 2 * pitch, wide), LOW), shard_sems],
            conv_flops,
            name,
        )

    z2, stat1, a_first = mid_forward((0,), (z0,), (stat0,), mid_shards[0], "mid_forward_a")
    mid_shards.append(gathered(mid_second, plan, (stat1,)))
    mid_third = tied(conv_mid_w[2], stat1)
    picks_out = cut_picks(row_picks(plan), ROW_BLOCK, width, rows_dev)
    picks_back = cut_picks(row_picks(plan), ROW_BLOCK, width, rows_dev, True)
    out_grad = jnp.swapaxes(out_grad, 1, 2)
    halo = from_next(out_grad[:, : EXTRA * width])
    (grad_spread,) = call(
        functools.partial(spread_rows_kernel, plan),
        (chan_at, out_grad, halo, *picks_out),
        [SMEM] + [VMEM] * 5,
        [((chans, spots, chans_out), LOW)],
        [VMEM],
        [],
        2 * spots * 640 * wide,
        "spread_rows",
    )
    og_parts = swapped(tied(grad_spread, stat1), plan)
    stat1 = micro_sums(stat1, plan)
    z3, stat3, a_second, h1 = mid_forward(
        (1, 2), (z2, zp), (stat1, statp), mid_shards[1], "mid_forward_b"
    )
    mid_shards.append(gathered(mid_third, plan, (stat3,)))
    stat3 = micro_sums(stat3, plan)
    z4, stat4, a_third = mid_forward((3,), (z3,), (stat3,), mid_shards[2], "mid_forward_c")
    stat4 = micro_sums(stat4, plan)

    block, gh2, back4 = call(
        functools.partial(head_kernel, plan),
        (chan_at, inv, marks, pars, z4, stat4, h1, *og_parts),
        [SMEM, SMEM] + [VMEM] * (5 + chans),
        [((chans, spots, chans_out), LOW), field, ((2, wide), FULL)],
        [VMEM] * 3,
        [pltpu.VMEM((chans, spots, chans_out), LOW)],
        spots * wide * 30,
        "head",
    )
    back4 = micro_sums(back4, plan)

    def mid_backward(j, kind, g, z, stat, back, weights, others, extra_outs, name):
        count = 3 if kind == "join" else 2
        outs = [((3, spots + 2 * pitch, wide), LOW), field, ((count, wide), FULL)] + extra_outs
        return call(
            functools.partial(mid_backward_kernel, plan, j, kind),
            (chan_at, inv, marks, pars, g, z, stat, back, *weights, *others),
            [SMEM, SMEM] + [VMEM] * 6 + [HBM] * chans + [VMEM] * len(others),
            outs,
            [VMEM] * len(outs),
            [weight_scratch, padded, padded, shard_sems],
            conv_flops,
            name,
        )

    def mid_weight(a, ga, name, across_first):
        keep, send = call(
            functools.partial(mid_weight_kernel, plan),
            (chan_at, a, ga),
            [SMEM, VMEM, VMEM],
            [((chans // 2, 9 * chans_out, wide), LOW)] * 2,
            [VMEM, VMEM],
            [pltpu.VMEM((wide, spots), LOW)] * 2,
            conv_flops,
            name,
        )
        return WeightSum(keep, send, plan, across_first)

    ga_third, g3, back3 = mid_backward(
        4, "plain", gh2, z4, stat4, back4, mid_shards[2], (z3, stat3), [], "mid_backward_c"
    )
    third = mid_weight(a_third, ga_third, "mid_weight_c", False)
    back3 = micro_sums(back3, plan, [lambda: third.send])
    ga_second, gh1, back12 = mid_backward(
        3, "join", g3, z3, stat3, back3, mid_shards[1], (z2, zp, stat1, statp, gh2), [],
        "mid_backward_b",
    )
    second = mid_weight(a_second, ga_second, "mid_weight_b", False)
    back12 = micro_sums(back12, plan, [lambda: second.send, third.advance])
    ga_first, g1, back0, gzp = mid_backward(
        1, "entry", gh1, z2, stat1, back12, mid_shards[0], (z0, stat0, zp, statp),
        [((spots, wide), LOW)], "mid_backward_a",
    )
    first_sum = mid_weight(a_first, ga_first, "mid_weight_a", True)
    back0 = micro_sums(back0, plan, [lambda: first_sum.send, second.advance, third.advance])
    (gm,) = call(
        functools.partial(entry_norm_kernel, plan),
        (inv, marks, pars, g1, z0, stat0, back0),
        [SMEM] + [VMEM] * 6,
        [((2, spots + pitch, wide), LOW)],
        [VMEM],
        [padded],
        spots * wide * 20,
        "entry_norm",
    )
    keep, send = call(
        functools.partial(entry_weight_kernel, plan),
        (xm, tied(gm, first_sum.advance()), gzp),
        [VMEM] * 3,
        [((chans // 2, 10 * chans_in, wide), LOW)] * 2,
        [VMEM] * 2,
        [pltpu.VMEM((2, deep, spots), LOW)],
        2 * spots * 7 * deep * wide,
        "entry_weight",
    )
    entry_sum = WeightSum(keep, send, plan, True)
    (gx,) = call(
        functools.partial(entry_backward_kernel, plan),
        (marks, gm, tied(gzp, send, third.advance()), *entry_shards),
        [VMEM] * 3 + [HBM] * chans,
        [((chans, 2, spots, 2 * chans_in), LOW)],
        [VMEM],
        entry_scratch + [pltpu.SemaphoreType.DMA((7 * chans,))],
        2 * spots * 7 * deep * wide,
        "entry_backward",
    )
    gx_parts = swapped(gx, plan)
    gx_parts[1] = tied(
        gx_parts[1], entry_sum.advance(), second.advance(), third.advance(), first_sum.advance()
    )

    def joined(kernel, parts, matrices, shape, axis, extra, dtype, whole, flops, name):
        edge = tuple(extra if i == axis else n for i, n in enumerate(shape))
        main, tail = call(
            functools.partial(kernel, plan),
            (chan_at, *matrices, *parts),
            [SMEM] + [VMEM] * (3 + chans),
            [(shape, dtype), (edge, LOW)],
            [VMEM] * 2,
            [pltpu.VMEM(whole, LOW)],
            flops,
            name,
        )
        first = lax.slice_in_dim(main, 0, extra, axis=axis) + to_next(tail).astype(dtype)
        return lax.dynamic_update_slice(main, first, (0, 0, 0))

    block_out = joined(
        join_rows_kernel, swapped(block, plan), picks_back, out_grad.shape, 1, EXTRA * width, LOW,
        (chans, spots, chans_out), 2 * spots * wide * 800, "join_rows",
    )
    block_out = jnp.swapaxes(block_out, 1, 2)
    feature_grad = joined(
        join_features_kernel, gx_parts, picks, features.shape, 2, EXTRA * 4 * width, FULL,
        (chans, 2, spots, 2 * chans_in), 8 * spots * 640 * chans * chans_in, "join_features",
    )

    last = ((lax.axis_index("space")) % 2).astype(jnp.int32).reshape(1)
    mids = [one.halves()[:2] for one in (first_sum, second, third)]
    (conv_mid_grad,) = call(
        functools.partial(mid_assembly_kernel, 3),
        (last, *[part for pair in mids for part in pair]),
        [SMEM] + [VMEM] * 6,
        [((3, 9 * chans_out, wide), FULL)],
        [HBM],
        [
            pltpu.VMEM((6, 9 * chans_out // 2, wide), FULL),
            pltpu.SemaphoreType.DMA((6,)),
        ],
        0,
        "mid_assembly",
    )
    conv_mid_grad = conv_mid_grad.reshape(3, 3, 3, chans_out, wide)
    conv_in_grad, proj_grad = call(
        entry_assembly_kernel,
        (last, *entry_sum.halves()[:2]),
        [SMEM] + [VMEM] * 2,
        [((9 * chans_in, wide), FULL), ((chans_in, wide), FULL)],
        [HBM] * 2,
        [pltpu.VMEM((10 * chans_in, wide), FULL), pltpu.SemaphoreType.DMA((2,))],
        0,
        "entry_assembly",
    )
    conv_in_grad = conv_in_grad.reshape(3, 3, chans_in, wide)

    sums = jnp.stack(
        [back0[1], back12[1], back12[2], back3[1], back4[1]]
        + [back0[0], back12[0], back12[0], back3[0], back4[0]]
    )
    sums = sums + flipped(sums, "chan", splits)
    sums = lax.dynamic_slice_in_dim(sums, chan * chans_out, chans_out, 1)
    return (
        block_out, feature_grad, conv_in_grad, proj_grad, conv_mid_grad, sums[:5], sums[5:],
    )


def solution(mesh):
    placed = (
        P(None, "chan", "space"),
        P(),
        P(None, None, "chan", None),
        P("chan", None),
        P(None, None, None, "chan", None),
        P(None, "chan"),
        P(None, "chan"),
        P(None, "chan", "space"),
    )
    return jax.shard_map(
        shards,
        mesh=mesh,
        in_specs=placed,
        out_specs=(
            P(None, "chan", "space"),
            P(None, "chan", "space"),
            P(None, None, "chan", None),
            P("chan", None),
            P(None, None, None, "chan", None),
            P(None, "chan"),
            P(None, "chan"),
        ),
        check_vma=False,
    )
```

time: 1140 us -> 466 us (0.41); the launches traced: 1120 us -> 460 us
  local copies, waits for them, and re-layouts: 269 us -> 30 us
  blocking collectives: 167 us -> 0 us
  waiting for transfers between devices: 353 us -> 190 us
  matrix products: 116 us -> 0 us
  Pallas kernels: 0 us -> 105 us
  other arithmetic: 126 us -> 23.5 us
  starting transfers between devices: 72.7 us -> 109 us
  between operations: 17.4 us -> 2.65 us
    psum x8 -> x0, blocking collectives: 167 us -> none  [space_sums(): return lax.psum((first_sum, second_sum), 'space')]
    ppermute x28 -> x111, waiting for transfers between devices: 25.6 us -> 190 us  [the longest x59 136 us: flipped(): return lax.ppermute(value, axis, [(i, i ^ bit) for i in range(count)])]
    unnamed x31 -> x0, waiting for transfers between devices: 162 us -> none
    psum x1 -> x0, waiting for transfers between devices: 136 us -> none  [shards(): lax.psum(as_sent(weight_totals), 'space')]
    dot_general x30 -> x0, matrix products: 116 us -> none  [the longest x6 49.4 us: mid_backward(): jnp.einsum('tco,toq->cq', weight_taps, stacked, preferred_element_type=jn...]
    unnamed x325 -> x106, local copies, waits for them, and re-layouts: 128 us -> 20.4 us
    pallas_call x0 -> x20, Pallas kernels: none -> 105 us  [call(): pl.pallas_call(kernel, out_shape=shapes, in_specs=specs, out_specs=out_sp...]
    concatenate x16 -> x0, local copies, waits for them, and re-layouts: 47.6 us -> none  [the longest x6 30 us: with_halo(): block = jnp.concatenate([low, block, high], axis=dim)]
  transfers between devices with their start and end apart: 49 -> 111, of which waited for: 26 -> 57; matrix products, arithmetic and copies ran while one was open for 30% -> 7% of each run, Pallas kernels for 0% -> 19%
where the time goes in v1:
time: 466 us; the launch traced here: 460 us
  waiting for transfers between devices  190 us (41%)
  starting transfers between devices  109 us (23%)
  Pallas kernels  105 us (23%)
  local copies, waits for them, and re-layouts  30 us (6%)
  other arithmetic  23.5 us (5%)
    ppermute x59, waiting for transfers between devices, flipped(): return lax.ppermute(value, axis, [(i, i ^ bit) for i in range(count)])  136 us
    pallas_call x20, Pallas kernels, call(): pl.pallas_call(kernel, out_shape=shapes, in_specs=specs, out_specs=out_sp...  105 us
    ppermute x48, starting transfers between devices, exchanged(): lax.ppermute(value, ('chan', 'space'), [(i, i ^ flip) for i in range(coun...  51.2 us
    ppermute x59, starting transfers between devices, flipped(): return lax.ppermute(value, axis, [(i, i ^ bit) for i in range(count)])  48.4 us
    ppermute x48, waiting for transfers between devices, exchanged(): lax.ppermute(value, ('chan', 'space'), [(i, i ^ flip) for i in range(coun...  32.9 us
    unnamed x106, local copies, waits for them, and re-layouts  20.4 us
    ppermute x2, waiting for transfers between devices, to_next(): return lax.ppermute(value, 'space', [(i, i + 1) for i in range(count - 1)])  17.4 us
    convert_element_type x16, other arithmetic, added(): return (kept + received).astype(LOW)  15.4 us
  transfers between devices with their start and end apart: 111, of which 57 were waited for; matrix products, arithmetic and copies ran while one was open for 7% of the time, Pallas kernels for 19%

profile of v1, /device:TPU:0, one launch (start us, length us, event | category | flops | bytes accessed | tf_op | source)
XLA Modules:
  0.0 460.1 jit_solution(8436985123993840907)
XLA Ops:
  2.5 2.6 collective-permute-start.7
  9.2 4.0 collective-permute-done.2.halo_ref
  15.6 2.9 spread_features.1
  18.5 2.1 collective-permute-done.7.refs_6_.refs_2_
  24.3 3.8 slice_bitcast_fusion
  28.1 7.6 %collective-permute-done.4.refs_2_ = bf16[2,864,128]{2,1,0:T(8,128)(2,1)} collective-permute-done((bf16[2,864,128]{2,1,0:T(8,128)(2,1)}, bf16[2,864,128]{2,1,0:T(8,128)(2,1)}, u32[]{:S(2)}, u32[]{:S(2)}) %collective-permute-start.4) | collective-permute-done | bytes 442400 | tf_op jit(solution)/shard_map/ppermute | solution.py:35
  35.7 8.2 %collective-permute-done.5.refs_3_ = bf16[2,864,128]{2,1,0:T(8,128)(2,1)} collective-permute-done((bf16[2,864,128]{2,1,0:T(8,128)(2,1)}, bf16[2,864,128]{2,1,0:T(8,128)(2,1)}, u32[]{:S(2)}, u32[]{:S(2)}) %collective-permute-start.5) | collective-permute-done | bytes 442400 | tf_op jit(solution)/shard_map/ppermute | solution.py:35
  52.1 8.8 %entry_forward.1 = (f32[864,512]{1,0:T(8,128)S(1)}, f32[864,512]{1,0:T(8,128)S(1)}, f32[4,512]{1,0:T(4,128)S(1)}, bf16[2,864,512]{2,1,0:T(8,128)(2,1)S(1)}) custom-call(f32[864,8]{1,0:T(8,128)S(1)} %convert_element_type.336.marks_ref, bf16[2,864,128]{2,1,0:T(8,128)(2,1)S(1)} %copy-done.16, bf16[2,864,128]{2,1,0:T(8,128)(2,1)} %collective-permute-done.3.refs_1_, ...), custom_call_target="tpu_custom_call" | custom-call | flops 3170893824 | bytes 9735168 | tf_op jit(solution)/shard_map/entry_forward/pallas_call | solution.py:731
  63.4 9.8 %collective-permute-done.16.refs_4_.refs_6_ = bf16[3,3,128,512]{3,2,1,0:T(8,128)(2,1)} collective-permute-done((bf16[3,3,128,512]{3,2,1,0:T(8,128)(2,1)S(1)}, bf16[3,3,128,512]{3,2,1,0:T(8,128)(2,1)}, u32[]{:S(2)}, u32[]{:S(2)}) %collective-permute-start.16) | collective-permute-done | bytes 1179680 | tf_op jit(solution)/shard_map/ppermute | solution.py:35
  76.6 2.1 collective-permute-done.10
  79.8 2.6 collective-permute-start.13
  88.1 7.2 %mid_forward_a.1 = (f32[864,512]{1,0:T(8,128)S(1)}, f32[2,512]{1,0:T(2,128)S(1)}, bf16[864,512]{1,0:T(8,128)(2,1)S(1)}) custom-call(s32[1]{0:T(128)} %bitcast.chan_ref, f32[1]{0:T(128)} %bitcast.2.inv_ref, f32[864,8]{1,0:T(8,128)S(1)} %convert_element_type.336.marks_ref, f32[10,512]{1,0:T(8,128)S(1)} %add.430.par_ref, ...), custom_call_target="tpu_custom_call" | custom-call | flops 4076863488 | bytes 9198600 | tf_op jit(solution)/shard_map/mid_forward_a/pallas_call | solution.py:731
  96.3 5.7 %collective-permute-done.25.refs_6_ = bf16[3,3,128,512]{3,2,1,0:T(8,128)(2,1)} collective-permute-done((bf16[3,3,128,512]{3,2,1,0:T(8,128)(2,1)}, bf16[3,3,128,512]{3,2,1,0:T(8,128)(2,1)}, u32[]{:S(2)}, u32[]{:S(2)}) %collective-permute-start.25) | collective-permute-done | bytes 1179680 | tf_op jit(solution)/shard_map/ppermute | solution.py:35
  105.3 2.0 collective-permute-done.19
  108.5 2.6 collective-permute-start.22
  116.7 6.4 %mid_forward_b.1 = (f32[864,512]{1,0:T(8,128)S(1)}, f32[2,512]{1,0:T(2,128)S(1)}, bf16[864,512]{1,0:T(8,128)(2,1)S(1)}, f32[864,512]{1,0:T(8,128)S(1)}) custom-call(s32[1]{0:T(128)} %bitcast.chan_ref, f32[1]{0:T(128)} %bitcast.2.inv_ref, f32[864,8]{1,0:T(8,128)S(1)} %convert_element_type.336.marks_ref, f32[10,512]{1,0:T(8,128)S(1)} %add.430.par_ref, ...), custom_call_target="tpu_custom_call" | custom-call | flops 4076863488 | bytes 12741640 | tf_op jit(solution)/shard_map/mid_forward_b/pallas_call | solution.py:731
  123.1 7.2 %collective-permute-done.34.refs_4_.refs_6_ = bf16[3,3,128,512]{3,2,1,0:T(8,128)(2,1)S(1)} collective-permute-done((bf16[3,3,128,512]{3,2,1,0:T(8,128)(2,1)S(1)}, bf16[3,3,128,512]{3,2,1,0:T(8,128)(2,1)S(1)}, u32[]{:S(2)}, u32[]{:S(2)}) %collective-permute-start.34) | collective-permute-done | bytes 1179680 | tf_op jit(solution)/shard_map/ppermute | solution.py:35
  135.1 2.7 collective-permute-start.31
  140.9 2.2 collective-permute-done.32
  143.2 6.1 %mid_forward_c.1 = (f32[864,512]{1,0:T(8,128)S(1)}, f32[2,512]{1,0:T(2,128)S(1)}, bf16[864,512]{1,0:T(8,128)(2,1)S(1)}) custom-call(s32[1]{0:T(128)} %bitcast.chan_ref, f32[1]{0:T(128)} %bitcast.2.inv_ref, f32[864,8]{1,0:T(8,128)S(1)} %convert_element_type.336.marks_ref, f32[10,512]{1,0:T(8,128)S(1)} %add.430.par_ref, ...), custom_call_target="tpu_custom_call" | custom-call | flops 4076863488 | bytes 9198600 | tf_op jit(solution)/shard_map/mid_forward_c/pallas_call | solution.py:731
  153.1 2.5 collective-permute-start.40
  161.0 4.6 collective-permute-done.44.refs_2_
  165.6 3.8 collective-permute-done.45.refs_3_
  175.8 2.6 collective-permute-start.54
  180.3 3.4 collective-permute-done.55
  183.8 7.1 %mid_backward_c.1 = (bf16[3,1056,512]{2,1,0:T(8,128)(2,1)S(1)}, f32[864,512]{1,0:T(8,128)S(1)}, f32[2,512]{1,0:T(2,128)S(1)}) custom-call(s32[1]{0:T(128)} %bitcast.chan_ref, f32[1]{0:T(128)} %bitcast.2.inv_ref, f32[864,8]{1,0:T(8,128)S(1)} %convert_element_type.336.marks_ref, f32[10,512]{1,0:T(8,128)S(1)} %add.430.par_ref, ...), custom_call_target="tpu_custom_call" | custom-call | flops 4076863488 | bytes 15105032 | tf_op jit(solution)/shard_map/mid_backward_c/pallas_call | solution.py:731
  190.9 5.9 %mid_weight_c.1 = (bf16[2,1152,512]{2,1,0:T(8,128)(2,1)S(1)}, bf16[2,1152,512]{2,1,0:T(8,128)(2,1)S(1)}) custom-call(s32[1]{0:T(128)} %bitcast.chan_ref, bf16[864,512]{1,0:T(8,128)(2,1)S(1)} %get-tuple-element.85.a_ref, bf16[3,1056,512]{2,1,0:T(8,128)(2,1)S(1)} %get-tuple-element.86.ga_ref), custom_call_target="tpu_custom_call" | custom-call | flops 4076863488 | bytes 8847364 | tf_op jit(solution)/shard_map/mid_weight_c/pallas_call | solution.py:731
  198.8 2.6 collective-permute-done.56
  207.9 7.2 %mid_backward_b.1 = (bf16[3,1056,512]{2,1,0:T(8,128)(2,1)S(1)}, f32[864,512]{1,0:T(8,128)S(1)}, f32[3,512]{1,0:T(4,128)S(1)}) custom-call(s32[1]{0:T(128)} %bitcast.chan_ref, f32[1]{0:T(128)} %bitcast.2.inv_ref, f32[864,8]{1,0:T(8,128)S(1)} %convert_element_type.336.marks_ref, f32[10,512]{1,0:T(8,128)S(1)} %add.430.par_ref, ...), custom_call_target="tpu_custom_call" | custom-call | flops 4076863488 | bytes 18650120 | tf_op jit(solution)/shard_map/mid_backward_b/pallas_call | solution.py:731
  215.1 7.3 %mid_weight_b.1 = (bf16[2,1152,512]{2,1,0:T(8,128)(2,1)S(1)}, bf16[2,1152,512]{2,1,0:T(8,128)(2,1)}) custom-call(s32[1]{0:T(128)} %bitcast.chan_ref, bf16[864,512]{1,0:T(8,128)(2,1)S(1)} %get-tuple-element.91.a_ref, bf16[3,1056,512]{2,1,0:T(8,128)(2,1)S(1)} %get-tuple-element.92.ga_ref), custom_call_target="tpu_custom_call" | custom-call | flops 4076863488 | bytes 8847364 | tf_op jit(solution)/shard_map/mid_weight_b/pallas_call | solution.py:731
  224.6 2.1 add_convert_fusion.3
  232.1 2.1 collective-permute-done.68
  241.4 8.2 %mid_backward_a.1 = (bf16[3,1056,512]{2,1,0:T(8,128)(2,1)S(1)}, f32[864,512]{1,0:T(8,128)S(1)}, f32[2,512]{1,0:T(2,128)S(1)}, bf16[864,512]{1,0:T(8,128)(2,1)S(1)}) custom-call(s32[1]{0:T(128)} %bitcast.chan_ref, f32[1]{0:T(128)} %bitcast.2.inv_ref, f32[864,8]{1,0:T(8,128)S(1)} %convert_element_type.336.marks_ref, f32[10,512]{1,0:T(8,128)S(1)} %add.430.par_ref, ...), custom_call_target="tpu_custom_call" | custom-call | flops 4076863488 | bytes 17765384 | tf_op jit(solution)/shard_map/mid_backward_a/pallas_call | solution.py:731
  249.7 5.8 %mid_weight_a.1 = (bf16[2,1152,512]{2,1,0:T(8,128)(2,1)S(1)}, bf16[2,1152,512]{2,1,0:T(8,128)(2,1)S(1)}) custom-call(s32[1]{0:T(128)} %bitcast.chan_ref, bf16[864,512]{1,0:T(8,128)(2,1)S(1)} %copy-done.47, bf16[3,1056,512]{2,1,0:T(8,128)(2,1)S(1)} %get-tuple-element.99.ga_ref), custom_call_target="tpu_custom_call" | custom-call | flops 4076863488 | bytes 8847364 | tf_op jit(solution)/shard_map/mid_weight_a/pallas_call | solution.py:731
  257.8 2.4 add_convert_fusion.1
  261.7 2.8 collective-permute-done.47.refs_2_
  264.5 28.3 %collective-permute-done.48.refs_3_ = bf16[864,128]{1,0:T(8,128)(2,1)S(1)} collective-permute-done((bf16[864,128]{1,0:T(8,128)(2,1)S(1)}, bf16[864,128]{1,0:T(8,128)(2,1)S(1)}, u32[]{:S(2)}, u32[]{:S(2)}) %collective-permute-start.48) | collective-permute-done | bytes 221216 | tf_op jit(solution)/shard_map/ppermute | solution.py:35
  292.8 2.4 join_rows.1
  298.4 2.9 collective-permute-start.49
  311.4 2.1 add_convert_fusion
  314.0 6.1 %entry_weight.1 = (bf16[2,640,512]{2,1,0:T(8,128)(2,1)S(1)}, bf16[2,640,512]{2,1,0:T(8,128)(2,1)}) custom-call(bf16[2,864,512]{2,1,0:T(8,128)(2,1)S(1)} %copy-done.45, bf16[2,960,512]{2,1,0:T(8,128)(2,1)S(1)} %entry_norm.1.gm_ref, bf16[864,512]{1,0:T(8,128)(2,1)S(1)} %get-tuple-element.108.short_ref), custom_call_target="tpu_custom_call" | custom-call | flops 3170893824 | bytes 7241728 | tf_op jit(solution)/shard_map/entry_weight/pallas_call | solution.py:731
  321.2 2.7 collective-permute-done.78
  325.5 11.1 %collective-permute-done.100 = bf16[1,576,512]{2,1,0:T(8,128)(2,1)S(1)} collective-permute-done((bf16[1,576,512]{2,1,0:T(8,128)(2,1)S(1)}, bf16[1,576,512]{2,1,0:T(8,128)(2,1)S(1)}, u32[]{:S(2)}, u32[]{:S(2)}) %collective-permute-start.100) | collective-permute-done | bytes 589856 | tf_op jit(solution)/shard_map/ppermute | solution.py:35
  340.7 2.0 collective-permute-start.106
  342.7 4.9 %collective-permute-done.101 = bf16[1,288,512]{2,1,0:T(8,128)(2,1)} collective-permute-done((bf16[1,288,512]{2,1,0:T(8,128)(2,1)}, bf16[1,288,512]{2,1,0:T(8,128)(2,1)}, u32[]{:S(2)}, u32[]{:S(2)}) %collective-permute-start.101) | collective-permute-done | bytes 294944 | tf_op jit(solution)/shard_map/ppermute | solution.py:35
  348.6 5.8 %collective-permute-done.106 = bf16[1,144,512]{2,1,0:T(8,128)(2,1)S(1)} collective-permute-done((bf16[1,144,512]{2,1,0:T(8,128)(2,1)S(1)}, bf16[1,144,512]{2,1,0:T(8,128)(2,1)S(1)}, u32[]{:S(2)}, u32[]{:S(2)}) %collective-permute-start.106) | collective-permute-done | bytes 147488 | tf_op jit(solution)/shard_map/ppermute | solution.py:35
  355.4 4.2 collective-permute-done.83
  366.6 2.2 collective-permute-start.103
  369.3 7.5 %entry_backward.1 = bf16[4,2,864,128]{3,2,1,0:T(8,128)(2,1)S(1)} custom-call(f32[864,8]{1,0:T(8,128)S(1)} %convert_element_type.336.marks_ref, bf16[2,960,512]{2,1,0:T(8,128)(2,1)S(1)} %entry_norm.1.gm_ref, bf16[864,512]{1,0:T(8,128)(2,1)S(1)} %copy-done.43, bf16[10,64,512]{2,1,0:T(8,128)(2,1)S(1)} %copy-done.14, bf16[10,64,512]{2,1,0:T(8,128)(2,1)S(1)} %copy-done.22, ...), custom_call_target="tpu_custom_call" | custom-call | flops 3170893824 | bytes 7269376 | tf_op jit(solution)/shard_map/entry_backward/pallas_call | solution.py:731
  380.0 3.8 collective-permute-done.95
  384.4 2.2 collective-permute-start.96
  386.7 2.9 collective-permute-done.88
  389.6 2.4 collective-permute-done.96
  392.3 2.3 collective-permute-start.97
  394.9 6.1 %collective-permute-done.89 = bf16[1,160,512]{2,1,0:T(8,128)(2,1)S(1)} collective-permute-done((bf16[1,160,512]{2,1,0:T(8,128)(2,1)S(1)}, bf16[1,160,512]{2,1,0:T(8,128)(2,1)S(1)}, u32[]{:S(2)}, u32[]{:S(2)}) %collective-permute-start.89) | collective-permute-done | bytes 163872 | tf_op jit(solution)/shard_map/ppermute | solution.py:35
  403.1 4.5 collective-permute-done.90
  409.4 2.5 collective-permute-done.104
  413.6 3.8 collective-permute-done.91
  418.7 3.0 collective-permute-start.92
  422.5 5.9 %join_features.1 = (f32[2,64,6720]{2,1,0:T(8,128)}, bf16[2,64,320]{2,1,0:T(8,128)(2,1)S(1)}) custom-call(s32[1]{0:T(128)} %bitcast.chan_ref, bf16[2,288,640]{2,1,0:T(8,128)(2,1)S(1)} %copy-done.28, bf16[2,288,320]{2,1,0:T(8,128)(2,1)S(1)} %copy-done.31, bf16[2,288,320]{2,1,0:T(8,128)(2,1)S(1)} %copy-done.33, ...), custom_call_target="tpu_custom_call" | custom-call | flops 1132462080 | bytes 6766596 | tf_op jit(solution)/shard_map/join_features/pallas_call | solution.py:731
  428.4 3.5 collective-permute-start.86
  432.8 17.4 %collective-permute-done.86 = bf16[2,64,320]{2,1,0:T(8,128)(2,1)S(1)} collective-permute-done((bf16[2,64,320]{2,1,0:T(8,128)(2,1)S(1)}, bf16[2,64,320]{2,1,0:T(8,128)(2,1)S(1)}, u32[]{:S(2)}, u32[]{:S(2)}) %collective-permute-start.86) | collective-permute-done | bytes 81952 | tf_op jit(solution)/shard_map/ppermute | solution.py:45
  453.7 2.1 entry_assembly.1
  455.8 4.1 mid_assembly.1
  (382 shorter events, 141.4 us)
Async XLA Ops:
  1.9 42.0 %collective-permute-start.6 = (bf16[10,64,512]{2,1,0:T(8,128)(2,1)S(1)}, bf16[10,64,512]{2,1,0:T(8,128)(2,1)S(1)}, u32[]{:S(2)}, u32[]{:S(2)}) collective-permute-start(bf16[10,64,512]{2,1,0:T(8,128)(2,1)S(1)} %pad_maximum_fusion.refs_4_.refs_0_), channel_id=1, source_target_pairs={{0,8},{8,0},{16,24},{24,16},{1,9},{9,1},{17,25},{25,17},{2,10},{10... | collective-permute-start | bytes 1966088 | tf_op jit(solution)/shard_map/ppermute | solution.py:35
  2.5 18.2 %collective-permute-start.7 = (bf16[10,64,512]{2,1,0:T(8,128)(2,1)S(1)}, bf16[10,64,512]{2,1,0:T(8,128)(2,1)S(1)}, u32[]{:S(2)}, u32[]{:S(2)}) collective-permute-start(bf16[10,64,512]{2,1,0:T(8,128)(2,1)S(1)} %pad_maximum_fusion.refs_4_.refs_0_), channel_id=1, source_target_pairs={{0,16},{8,24},{16,0},{24,8},{1,17},{9,25},{17,1},{25,9},{2,18},{10... | collective-permute-start | bytes 1966088 | tf_op jit(solution)/shard_map/ppermute | solution.py:35
  6.2 6.9 %collective-permute-start.2 = (bf16[2,64,320]{2,1,0:T(8,128)(2,1)S(1)}, bf16[2,64,320]{2,1,0:T(8,128)(2,1)S(1)}, u32[]{:S(2)}, u32[]{:S(2)}) collective-permute-start(bf16[2,64,320]{2,1,0:T(8,128)(2,1)S(1)} %slice.182), channel_id=1, source_target_pairs={{1,0},{2,1},{3,2},{4,3},{5,4},{6,5},{7,6},{9,8},{10,9},{11,10},{12... | collective-permute-start | bytes 245768 | tf_op jit(solution)/shard_map/ppermute | solution.py:40
  8.8 15.4 %collective-permute-start.1 = (f32[10,512]{1,0:T(8,128)S(1)}, f32[10,512]{1,0:T(8,128)S(1)}, u32[]{:S(2)}, u32[]{:S(2)}) collective-permute-start(f32[10,512]{1,0:T(8,128)S(1)} %constant_dynamic-update-slice_fusion), channel_id=1, source_target_pairs={{0,16},{8,24},{16,0},{24,8},{1,17},{9,25},{17,1},{25,9},{2,18},{10... | collective-permute-start | bytes 61448 | tf_op jit(solution)/shard_map/ppermute | solution.py:35
  20.6 24.1 %collective-permute-start.8 = (bf16[10,64,512]{2,1,0:T(8,128)(2,1)S(1)}, bf16[10,64,512]{2,1,0:T(8,128)(2,1)}, u32[]{:S(2)}, u32[]{:S(2)}) collective-permute-start(bf16[10,64,512]{2,1,0:T(8,128)(2,1)S(1)} %collective-permute-done.7.refs_6_.refs_2_), channel_id=1, source_target_pairs={{0,8},{8,0},{16,24},{24,16},{1,9},{9,1},{17,25},{25,17},{2,10},{10... | collective-permute-start | bytes 1966088 | tf_op jit(solution)/shard_map/ppermute | solution.py:35
  22.1 6.0 %collective-permute-start.3 = (bf16[2,864,128]{2,1,0:T(8,128)(2,1)}, bf16[2,864,128]{2,1,0:T(8,128)(2,1)}, u32[]{:S(2)}, u32[]{:S(2)}) collective-permute-start(bf16[2,864,128]{2,1,0:T(8,128)(2,1)} %get-tuple-element.146), channel_id=1, source_target_pairs={{0,8},{8,0},{16,24},{24,16},{1,9},{9,1},{17,25},{25,17},{2,10},{10... | collective-permute-start | bytes 1327112 | tf_op jit(solution)/shard_map/ppermute | solution.py:35
  22.4 13.3 %collective-permute-start.4 = (bf16[2,864,128]{2,1,0:T(8,128)(2,1)}, bf16[2,864,128]{2,1,0:T(8,128)(2,1)}, u32[]{:S(2)}, u32[]{:S(2)}) collective-permute-start(bf16[2,864,128]{2,1,0:T(8,128)(2,1)} %get-tuple-element.145), channel_id=1, source_target_pairs={{0,16},{8,24},{16,0},{24,8},{1,17},{9,25},{17,1},{25,9},{2,18},{10... | collective-permute-start | bytes 1327112 | tf_op jit(solution)/shard_map/ppermute | solution.py:35
  24.3 19.6 %collective-permute-start.5 = (bf16[2,864,128]{2,1,0:T(8,128)(2,1)}, bf16[2,864,128]{2,1,0:T(8,128)(2,1)}, u32[]{:S(2)}, u32[]{:S(2)}) collective-permute-start(bf16[2,864,128]{2,1,0:T(8,128)(2,1)} %get-tuple-element.144), channel_id=1, source_target_pairs={{0,24},{8,16},{16,8},{24,0},{1,25},{9,17},{17,9},{25,1},{2,26},{10... | collective-permute-start | bytes 1327112 | tf_op jit(solution)/shard_map/ppermute | solution.py:35
  44.8 28.5 %collective-permute-start.16 = (bf16[3,3,128,512]{3,2,1,0:T(8,128)(2,1)S(1)}, bf16[3,3,128,512]{3,2,1,0:T(8,128)(2,1)}, u32[]{:S(2)}, u32[]{:S(2)}) collective-permute-start(bf16[3,3,128,512]{3,2,1,0:T(8,128)(2,1)S(1)} %get-tuple-element.63.refs_2_.refs_4_), channel_id=1, source_target_pairs={{0,16},{8,24},{16,0},{24,8},{1,17},{9,25},{17,1},{25,9},{2,18},{10... | collective-permute-start | bytes 3538952 | tf_op jit(solution)/shard_map/ppermute | solution.py:35
  47.5 40.6 %collective-permute-start.15 = (bf16[3,3,128,512]{3,2,1,0:T(8,128)(2,1)S(1)}, bf16[3,3,128,512]{3,2,1,0:T(8,128)(2,1)}, u32[]{:S(2)}, u32[]{:S(2)}) collective-permute-start(bf16[3,3,128,512]{3,2,1,0:T(8,128)(2,1)S(1)} %get-tuple-element.63.refs_2_.refs_4_), channel_id=1, source_target_pairs={{0,8},{8,0},{16,24},{24,16},{1,9},{9,1},{17,25},{25,17},{2,10},{10... | collective-permute-start | bytes 3538952 | tf_op jit(solution)/shard_map/ppermute | solution.py:35
  73.2 14.9 %collective-permute-start.17 = (bf16[3,3,128,512]{3,2,1,0:T(8,128)(2,1)}, bf16[3,3,128,512]{3,2,1,0:T(8,128)(2,1)}, u32[]{:S(2)}, u32[]{:S(2)}) collective-permute-start(bf16[3,3,128,512]{3,2,1,0:T(8,128)(2,1)} %collective-permute-done.16.refs_4_.refs_6_), channel_id=1, source_target_pairs={{0,8},{8,0},{16,24},{24,16},{1,9},{9,1},{17,25},{25,17},{2,10},{10... | collective-permute-start | bytes 3538952 | tf_op jit(solution)/shard_map/ppermute | solution.py:35
  73.2 28.7 %collective-permute-start.25 = (bf16[3,3,128,512]{3,2,1,0:T(8,128)(2,1)}, bf16[3,3,128,512]{3,2,1,0:T(8,128)(2,1)}, u32[]{:S(2)}, u32[]{:S(2)}) collective-permute-start(bf16[3,3,128,512]{3,2,1,0:T(8,128)(2,1)} %get-tuple-element.68.refs_4_), channel_id=1, source_target_pairs={{0,16},{8,24},{16,0},{24,8},{1,17},{9,25},{17,1},{25,9},{2,18},{10... | collective-permute-start | bytes 3538952 | tf_op jit(solution)/shard_map/ppermute | solution.py:35
  82.5 5.4 %collective-permute-start.14 = (f32[4,512]{1,0:T(4,128)S(1)}, f32[4,512]{1,0:T(4,128)S(1)}, u32[]{:S(2)}, u32[]{:S(2)}) collective-permute-start(f32[4,512]{1,0:T(4,128)S(1)} %add_add_fusion.3), channel_id=1, source_target_pairs={{0,6},{1,7},{2,4},{3,5},{4,2},{5,3},{6,0},{7,1},{8,14},{9,15},{10,... | collective-permute-start | bytes 24584 | tf_op jit(solution)/shard_map/ppermute | solution.py:51
  87.9 28.7 %collective-permute-start.24 = (bf16[3,3,128,512]{3,2,1,0:T(8,128)(2,1)}, bf16[3,3,128,512]{3,2,1,0:T(8,128)(2,1)S(1)}, u32[]{:S(2)}, u32[]{:S(2)}) collective-permute-start(bf16[3,3,128,512]{3,2,1,0:T(8,128)(2,1)} %get-tuple-element.68.refs_4_), channel_id=1, source_target_pairs={{0,8},{8,0},{16,24},{24,16},{1,9},{9,1},{17,25},{25,17},{2,10},{10... | collective-permute-start | bytes 3538952 | tf_op jit(solution)/shard_map/ppermute | solution.py:35
  101.9 14.7 %collective-permute-start.26 = (bf16[3,3,128,512]{3,2,1,0:T(8,128)(2,1)}, bf16[3,3,128,512]{3,2,1,0:T(8,128)(2,1)S(1)}, u32[]{:S(2)}, u32[]{:S(2)}) collective-permute-start(bf16[3,3,128,512]{3,2,1,0:T(8,128)(2,1)} %collective-permute-done.25.refs_6_), channel_id=1, source_target_pairs={{0,8},{8,0},{16,24},{24,16},{1,9},{9,1},{17,25},{25,17},{2,10},{10... | collective-permute-start | bytes 3538952 | tf_op jit(solution)/shard_map/ppermute | solution.py:35
  101.9 28.4 %collective-permute-start.34 = (bf16[3,3,128,512]{3,2,1,0:T(8,128)(2,1)S(1)}, bf16[3,3,128,512]{3,2,1,0:T(8,128)(2,1)S(1)}, u32[]{:S(2)}, u32[]{:S(2)}) collective-permute-start(bf16[3,3,128,512]{3,2,1,0:T(8,128)(2,1)S(1)} %copy-done.7), channel_id=1, source_target_pairs={{0,16},{8,24},{16,0},{24,8},{1,17},{9,25},{17,1},{25,9},{2,18},{10... | collective-permute-start | bytes 3538952 | tf_op jit(solution)/shard_map/ppermute | solution.py:35
  116.5 26.6 %collective-permute-start.33 = (bf16[3,3,128,512]{3,2,1,0:T(8,128)(2,1)S(1)}, bf16[3,3,128,512]{3,2,1,0:T(8,128)(2,1)S(1)}, u32[]{:S(2)}, u32[]{:S(2)}) collective-permute-start(bf16[3,3,128,512]{3,2,1,0:T(8,128)(2,1)S(1)} %copy-done.7), channel_id=1, source_target_pairs={{0,8},{8,0},{16,24},{24,16},{1,9},{9,1},{17,25},{25,17},{2,10},{10... | collective-permute-start | bytes 3538952 | tf_op jit(solution)/shard_map/ppermute | solution.py:35
  130.3 12.9 %collective-permute-start.35 = (bf16[3,3,128,512]{3,2,1,0:T(8,128)(2,1)S(1)}, bf16[3,3,128,512]{3,2,1,0:T(8,128)(2,1)S(1)}, u32[]{:S(2)}, u32[]{:S(2)}) collective-permute-start(bf16[3,3,128,512]{3,2,1,0:T(8,128)(2,1)S(1)} %collective-permute-done.34.refs_4_.refs_6_), channel_id=1, source_target_pairs={{0,8},{8,0},{16,24},{24,16},{1,9},{9,1},{17,25},{25,17},{2,10},{10... | collective-permute-start | bytes 3538952 | tf_op jit(solution)/shard_map/ppermute | solution.py:35
  139.7 11.9 %collective-permute-start.42 = (bf16[2,80,128]{2,1,0:T(8,128)(2,1)S(1)}, bf16[2,80,128]{2,1,0:T(8,128)(2,1)S(1)}, u32[]{:S(2)}, u32[]{:S(2)}) collective-permute-start(bf16[2,80,128]{2,1,0:T(8,128)(2,1)S(1)} %slice.239), channel_id=1, source_target_pairs={{1,0},{2,1},{3,2},{4,3},{5,4},{6,5},{7,6},{9,8},{10,9},{11,10},{12... | collective-permute-start | bytes 122888 | tf_op jit(solution)/shard_map/ppermute | solution.py:40
  153.1 5.8 %collective-permute-start.40 = (f32[2,512]{1,0:T(2,128)S(1)}, f32[2,512]{1,0:T(2,128)S(1)}, u32[]{:S(2)}, u32[]{:S(2)}) collective-permute-start(f32[2,512]{1,0:T(2,128)S(1)} %add_add_fusion.11), channel_id=1, source_target_pairs={{0,4},{1,5},{2,6},{3,7},{4,0},{5,1},{6,2},{7,3},{8,12},{9,13},{10,... | collective-permute-start | bytes 12296 | tf_op jit(solution)/shard_map/ppermute | solution.py:51
  157.3 8.3 %collective-permute-start.44 = (bf16[864,128]{1,0:T(8,128)(2,1)S(1)}, bf16[864,128]{1,0:T(8,128)(2,1)S(1)}, u32[]{:S(2)}, u32[]{:S(2)}) collective-permute-start(bf16[864,128]{1,0:T(8,128)(2,1)S(1)} %get-tuple-element.161), channel_id=1, source_target_pairs={{0,16},{8,24},{16,0},{24,8},{1,17},{9,25},{17,1},{25,9},{2,18},{10... | collective-permute-start | bytes 663560 | tf_op jit(solution)/shard_map/ppermute | solution.py:35
  158.9 10.5 %collective-permute-start.45 = (bf16[864,128]{1,0:T(8,128)(2,1)S(1)}, bf16[864,128]{1,0:T(8,128)(2,1)S(1)}, u32[]{:S(2)}, u32[]{:S(2)}) collective-permute-start(bf16[864,128]{1,0:T(8,128)(2,1)S(1)} %get-tuple-element.160), channel_id=1, source_target_pairs={{0,24},{8,16},{16,8},{24,0},{1,25},{9,17},{17,9},{25,1},{2,26},{10... | collective-permute-start | bytes 663560 | tf_op jit(solution)/shard_map/ppermute | solution.py:35
  196.8 27.8 %collective-permute-start.63 = (bf16[2,1152,512]{2,1,0:T(8,128)(2,1)S(1)}, bf16[2,1152,512]{2,1,0:T(8,128)(2,1)S(1)}, u32[]{:S(2)}, u32[]{:S(2)}) collective-permute-start(bf16[2,1152,512]{2,1,0:T(8,128)(2,1)S(1)} %get-tuple-element.87), channel_id=1, source_target_pairs={{0,8},{8,0},{16,24},{24,16},{1,9},{9,1},{17,25},{25,17},{2,10},{10... | collective-permute-start | bytes 7077896 | tf_op jit(solution)/shard_map/ppermute | solution.py:35
  222.4 35.3 %collective-permute-start.70 = (bf16[2,1152,512]{2,1,0:T(8,128)(2,1)}, bf16[2,1152,512]{2,1,0:T(8,128)(2,1)}, u32[]{:S(2)}, u32[]{:S(2)}) collective-permute-start(bf16[2,1152,512]{2,1,0:T(8,128)(2,1)} %get-tuple-element.93), channel_id=1, source_target_pairs={{0,8},{8,0},{16,24},{24,16},{1,9},{9,1},{17,25},{25,17},{2,10},{10... | collective-permute-start | bytes 7077896 | tf_op jit(solution)/shard_map/ppermute | solution.py:35
  228.7 5.5 %collective-permute-start.68 = (f32[3,512]{1,0:T(4,128)S(1)}, f32[3,512]{1,0:T(4,128)S(1)}, u32[]{:S(2)}, u32[]{:S(2)}) collective-permute-start(f32[3,512]{1,0:T(4,128)S(1)} %add_add_fusion.1), channel_id=1, source_target_pairs={{0,6},{1,7},{2,4},{3,5},{4,2},{5,3},{6,0},{7,1},{8,14},{9,15},{10,... | collective-permute-start | bytes 18440 | tf_op jit(solution)/shard_map/ppermute | solution.py:51
  230.6 66.7 %collective-permute-start.71 = (bf16[1,1152,512]{2,1,0:T(8,128)(2,1)}, bf16[1,1152,512]{2,1,0:T(8,128)(2,1)S(1)}, u32[]{:S(2)}, u32[]{:S(2)}) collective-permute-start(bf16[1,1152,512]{2,1,0:T(8,128)(2,1)} %get-tuple-element.128), channel_id=1, source_target_pairs={{0,16},{8,24},{16,0},{24,8},{1,17},{9,25},{17,1},{25,9},{2,18},{10... | collective-permute-start | bytes 3538952 | tf_op jit(solution)/shard_map/ppermute | solution.py:35
  255.5 55.9 %collective-permute-start.77 = (bf16[2,1152,512]{2,1,0:T(8,128)(2,1)S(1)}, bf16[2,1152,512]{2,1,0:T(8,128)(2,1)S(1)}, u32[]{:S(2)}, u32[]{:S(2)}) collective-permute-start(bf16[2,1152,512]{2,1,0:T(8,128)(2,1)S(1)} %get-tuple-element.100), channel_id=1, source_target_pairs={{0,8},{8,0},{16,24},{24,16},{1,9},{9,1},{17,25},{25,17},{2,10},{10... | collective-permute-start | bytes 7077896 | tf_op jit(solution)/shard_map/ppermute | solution.py:35
  256.2 8.3 %collective-permute-start.47 = (bf16[864,128]{1,0:T(8,128)(2,1)S(1)}, bf16[864,128]{1,0:T(8,128)(2,1)S(1)}, u32[]{:S(2)}, u32[]{:S(2)}) collective-permute-start(bf16[864,128]{1,0:T(8,128)(2,1)S(1)} %get-tuple-element.157), channel_id=1, source_target_pairs={{0,16},{8,24},{16,0},{24,8},{1,17},{9,25},{17,1},{25,9},{2,18},{10... | collective-permute-start | bytes 663560 | tf_op jit(solution)/shard_map/ppermute | solution.py:35
  260.2 49.2 %collective-permute-start.81 = (bf16[1,1152,512]{2,1,0:T(8,128)(2,1)S(1)}, bf16[1,1152,512]{2,1,0:T(8,128)(2,1)S(1)}, u32[]{:S(2)}, u32[]{:S(2)}) collective-permute-start(bf16[1,1152,512]{2,1,0:T(8,128)(2,1)S(1)} %get-tuple-element.126), channel_id=1, source_target_pairs={{0,16},{8,24},{16,0},{24,8},{1,17},{9,25},{17,1},{25,9},{2,18},{10... | collective-permute-start | bytes 3538952 | tf_op jit(solution)/shard_map/ppermute | solution.py:35
  260.7 32.0 %collective-permute-start.48 = (bf16[864,128]{1,0:T(8,128)(2,1)S(1)}, bf16[864,128]{1,0:T(8,128)(2,1)S(1)}, u32[]{:S(2)}, u32[]{:S(2)}) collective-permute-start(bf16[864,128]{1,0:T(8,128)(2,1)S(1)} %get-tuple-element.156), channel_id=1, source_target_pairs={{0,24},{8,16},{16,8},{24,0},{1,25},{9,17},{17,9},{25,1},{2,26},{10... | collective-permute-start | bytes 663560 | tf_op jit(solution)/shard_map/ppermute | solution.py:35
  295.2 6.1 %collective-permute-start.72 = (f32[2,512]{1,0:T(2,128)S(1)}, f32[2,512]{1,0:T(2,128)S(1)}, u32[]{:S(2)}, u32[]{:S(2)}) collective-permute-start(f32[2,512]{1,0:T(2,128)S(1)} %get-tuple-element.97), channel_id=1, source_target_pairs={{0,1},{1,0},{2,3},{3,2},{4,5},{5,4},{6,7},{7,6},{8,9},{9,8},{10,11... | collective-permute-start | bytes 12296 | tf_op jit(solution)/shard_map/ppermute | solution.py:51
  298.4 6.4 %collective-permute-start.49 = (bf16[2,80,128]{2,1,0:T(8,128)(2,1)S(1)}, bf16[2,80,128]{2,1,0:T(8,128)(2,1)S(1)}, u32[]{:S(2)}, u32[]{:S(2)}) collective-permute-start(bf16[2,80,128]{2,1,0:T(8,128)(2,1)S(1)} %get-tuple-element.80), channel_id=1, source_target_pairs={{0,1},{1,2},{2,3},{3,4},{4,5},{5,6},{6,7},{8,9},{9,10},{10,11},{11... | collective-permute-start | bytes 122888 | tf_op jit(solution)/shard_map/ppermute | solution.py:45
  301.3 6.3 %collective-permute-start.75 = (f32[2,512]{1,0:T(2,128)S(1)}, f32[2,512]{1,0:T(2,128)S(1)}, u32[]{:S(2)}, u32[]{:S(2)}) collective-permute-start(f32[2,512]{1,0:T(2,128)S(1)} %add_add_fusion.5), channel_id=1, source_target_pairs={{0,4},{1,5},{2,6},{3,7},{4,0},{5,1},{6,2},{7,3},{8,12},{9,13},{10,... | collective-permute-start | bytes 12296 | tf_op jit(solution)/shard_map/ppermute | solution.py:51
  307.6 16.3 %collective-permute-start.78 = (bf16[1,576,512]{2,1,0:T(8,128)(2,1)S(1)}, bf16[1,576,512]{2,1,0:T(8,128)(2,1)S(1)}, u32[]{:S(2)}, u32[]{:S(2)}) collective-permute-start(bf16[1,576,512]{2,1,0:T(8,128)(2,1)S(1)} %get-tuple-element.139), channel_id=1, source_target_pairs={{0,1},{1,0},{2,3},{3,2},{4,5},{5,4},{6,7},{7,6},{8,9},{9,8},{10,11... | collective-permute-start | bytes 1769480 | tf_op jit(solution)/shard_map/ppermute | solution.py:35
  309.8 26.8 %collective-permute-start.100 = (bf16[1,576,512]{2,1,0:T(8,128)(2,1)S(1)}, bf16[1,576,512]{2,1,0:T(8,128)(2,1)S(1)}, u32[]{:S(2)}, u32[]{:S(2)}) collective-permute-start(bf16[1,576,512]{2,1,0:T(8,128)(2,1)S(1)} %get-tuple-element.135), channel_id=1, source_target_pairs={{0,1},{1,0},{2,3},{3,2},{4,5},{5,4},{6,7},{7,6},{8,9},{9,8},{10,11... | collective-permute-start | bytes 1769480 | tf_op jit(solution)/shard_map/ppermute | solution.py:35
  313.5 46.2 %collective-permute-start.83 = (bf16[2,576,512]{2,1,0:T(8,128)(2,1)}, bf16[2,576,512]{2,1,0:T(8,128)(2,1)}, u32[]{:S(2)}, u32[]{:S(2)}) collective-permute-start(bf16[2,576,512]{2,1,0:T(8,128)(2,1)} %get-tuple-element.124), channel_id=1, source_target_pairs={{0,1},{1,0},{2,3},{3,2},{4,5},{5,4},{6,7},{7,6},{8,9},{9,8},{10,11... | collective-permute-start | bytes 3538952 | tf_op jit(solution)/shard_map/ppermute | solution.py:35
  321.2 41.8 %collective-permute-start.80 = (bf16[2,640,512]{2,1,0:T(8,128)(2,1)}, bf16[2,640,512]{2,1,0:T(8,128)(2,1)}, u32[]{:S(2)}, u32[]{:S(2)}) collective-permute-start(bf16[2,640,512]{2,1,0:T(8,128)(2,1)} %get-tuple-element.107), channel_id=1, source_target_pairs={{0,8},{8,0},{16,24},{24,16},{1,9},{9,1},{17,25},{25,17},{2,10},{10... | collective-permute-start | bytes 3932168 | tf_op jit(solution)/shard_map/ppermute | solution.py:35
  324.8 14.9 %collective-permute-start.82 = (bf16[1,288,512]{2,1,0:T(8,128)(2,1)}, bf16[1,288,512]{2,1,0:T(8,128)(2,1)}, u32[]{:S(2)}, u32[]{:S(2)}) collective-permute-start(bf16[1,288,512]{2,1,0:T(8,128)(2,1)} %get-tuple-element.155), channel_id=1, source_target_pairs={{0,2},{1,3},{2,0},{3,1},{4,6},{5,7},{6,4},{7,5},{8,10},{9,11},{10,... | collective-permute-start | bytes 884744 | tf_op jit(solution)/shard_map/ppermute | solution.py:35
  337.5 10.1 %collective-permute-start.101 = (bf16[1,288,512]{2,1,0:T(8,128)(2,1)}, bf16[1,288,512]{2,1,0:T(8,128)(2,1)}, u32[]{:S(2)}, u32[]{:S(2)}) collective-permute-start(bf16[1,288,512]{2,1,0:T(8,128)(2,1)} %get-tuple-element.151), channel_id=1, source_target_pairs={{0,2},{1,3},{2,0},{3,1},{4,6},{5,7},{6,4},{7,5},{8,10},{9,11},{10,... | collective-permute-start | bytes 884744 | tf_op jit(solution)/shard_map/ppermute | solution.py:35
  340.7 13.7 %collective-permute-start.106 = (bf16[1,144,512]{2,1,0:T(8,128)(2,1)S(1)}, bf16[1,144,512]{2,1,0:T(8,128)(2,1)S(1)}, u32[]{:S(2)}, u32[]{:S(2)}) collective-permute-start(bf16[1,144,512]{2,1,0:T(8,128)(2,1)S(1)} %add_convert_fusion.32), channel_id=1, source_target_pairs={{0,4},{1,5},{2,6},{3,7},{4,0},{5,1},{6,2},{7,3},{8,12},{9,13},{10,... | collective-permute-start | bytes 442376 | tf_op jit(solution)/shard_map/ppermute | solution.py:35
  348.6 17.1 %collective-permute-start.102 = (bf16[1,144,512]{2,1,0:T(8,128)(2,1)S(1)}, bf16[1,144,512]{2,1,0:T(8,128)(2,1)S(1)}, u32[]{:S(2)}, u32[]{:S(2)}) collective-permute-start(bf16[1,144,512]{2,1,0:T(8,128)(2,1)S(1)} %add_convert_fusion.27), channel_id=1, source_target_pairs={{0,4},{1,5},{2,6},{3,7},{4,0},{5,1},{6,2},{7,3},{8,12},{9,13},{10,... | collective-permute-start | bytes 442376 | tf_op jit(solution)/shard_map/ppermute | solution.py:35
  355.4 13.5 %collective-permute-start.107 = (bf16[144,512]{1,0:T(8,128)(2,1)S(1)}, bf16[144,512]{1,0:T(8,128)(2,1)S(1)}, u32[]{:S(2)}, u32[]{:S(2)}) collective-permute-start(bf16[144,512]{1,0:T(8,128)(2,1)S(1)} %fusion.2), channel_id=1, source_target_pairs={{0,4},{1,5},{2,6},{3,7},{4,0},{5,1},{6,2},{7,3},{8,12},{9,13},{10,... | collective-permute-start | bytes 442376 | tf_op jit(solution)/shard_map/ppermute | solution.py:35
  361.4 15.4 %collective-permute-start.94 = (bf16[1,576,512]{2,1,0:T(8,128)(2,1)S(1)}, bf16[1,576,512]{2,1,0:T(8,128)(2,1)S(1)}, u32[]{:S(2)}, u32[]{:S(2)}) collective-permute-start(bf16[1,576,512]{2,1,0:T(8,128)(2,1)S(1)} %get-tuple-element.137), channel_id=1, source_target_pairs={{0,16},{8,24},{16,0},{24,8},{1,17},{9,25},{17,1},{25,9},{2,18},{10... | collective-permute-start | bytes 1769480 | tf_op jit(solution)/shard_map/ppermute | solution.py:35
  364.8 14.2 %collective-permute-start.87 = (bf16[2,320,512]{2,1,0:T(8,128)(2,1)S(1)}, bf16[2,320,512]{2,1,0:T(8,128)(2,1)S(1)}, u32[]{:S(2)}, u32[]{:S(2)}) collective-permute-start(bf16[2,320,512]{2,1,0:T(8,128)(2,1)S(1)} %get-tuple-element.133), channel_id=1, source_target_pairs={{0,1},{1,0},{2,3},{3,2},{4,5},{5,4},{6,7},{7,6},{8,9},{9,8},{10,11... | collective-permute-start | bytes 1966088 | tf_op jit(solution)/shard_map/ppermute | solution.py:35
  366.6 17.7 %collective-permute-start.103 = (bf16[144,512]{1,0:T(8,128)(2,1)S(1)}, bf16[144,512]{1,0:T(8,128)(2,1)S(1)}, u32[]{:S(2)}, u32[]{:S(2)}) collective-permute-start(bf16[144,512]{1,0:T(8,128)(2,1)S(1)} %fusion.1), channel_id=1, source_target_pairs={{0,4},{1,5},{2,6},{3,7},{4,0},{5,1},{6,2},{7,3},{8,12},{9,13},{10,... | collective-permute-start | bytes 442376 | tf_op jit(solution)/shard_map/ppermute | solution.py:35
  368.9 23.4 %collective-permute-start.108 = (bf16[288,512]{1,0:T(8,128)(2,1)S(1)}, bf16[288,512]{1,0:T(8,128)(2,1)S(1)}, u32[]{:S(2)}, u32[]{:S(2)}) collective-permute-start(bf16[288,512]{1,0:T(8,128)(2,1)S(1)} %maximum_select_fusion.6), channel_id=1, source_target_pairs={{0,2},{1,3},{2,0},{3,1},{4,6},{5,7},{6,4},{7,5},{8,10},{9,11},{10,... | collective-permute-start | bytes 884744 | tf_op jit(solution)/shard_map/ppermute | solution.py:35
  376.9 6.9 %collective-permute-start.95 = (bf16[1,288,512]{2,1,0:T(8,128)(2,1)S(1)}, bf16[1,288,512]{2,1,0:T(8,128)(2,1)S(1)}, u32[]{:S(2)}, u32[]{:S(2)}) collective-permute-start(bf16[1,288,512]{2,1,0:T(8,128)(2,1)S(1)} %get-tuple-element.153), channel_id=1, source_target_pairs={{0,2},{1,3},{2,0},{3,1},{4,6},{5,7},{6,4},{7,5},{8,10},{9,11},{10,... | collective-permute-start | bytes 884744 | tf_op jit(solution)/shard_map/ppermute | solution.py:35
  379.3 10.3 %collective-permute-start.88 = (bf16[1,320,512]{2,1,0:T(8,128)(2,1)S(1)}, bf16[1,320,512]{2,1,0:T(8,128)(2,1)S(1)}, u32[]{:S(2)}, u32[]{:S(2)}) collective-permute-start(bf16[1,320,512]{2,1,0:T(8,128)(2,1)S(1)} %get-tuple-element.149), channel_id=1, source_target_pairs={{0,16},{8,24},{16,0},{24,8},{1,17},{9,25},{17,1},{25,9},{2,18},{10... | collective-permute-start | bytes 983048 | tf_op jit(solution)/shard_map/ppermute | solution.py:35
  379.9 32.3 %collective-permute-start.79 = (bf16[2,864,128]{2,1,0:T(8,128)(2,1)S(1)}, bf16[2,864,128]{2,1,0:T(8,128)(2,1)S(1)}, u32[]{:S(2)}, u32[]{:S(2)}) collective-permute-start(bf16[2,864,128]{2,1,0:T(8,128)(2,1)S(1)} %get-tuple-element.142), channel_id=1, source_target_pairs={{0,8},{8,0},{16,24},{24,16},{1,9},{9,1},{17,25},{25,17},{2,10},{10... | collective-permute-start | bytes 1327112 | tf_op jit(solution)/shard_map/ppermute | solution.py:35
  383.8 38.2 %collective-permute-start.84 = (bf16[2,864,128]{2,1,0:T(8,128)(2,1)S(1)}, bf16[2,864,128]{2,1,0:T(8,128)(2,1)S(1)}, u32[]{:S(2)}, u32[]{:S(2)}) collective-permute-start(bf16[2,864,128]{2,1,0:T(8,128)(2,1)S(1)} %get-tuple-element.141), channel_id=1, source_target_pairs={{0,16},{8,24},{16,0},{24,8},{1,17},{9,25},{17,1},{25,9},{2,18},{10... | collective-permute-start | bytes 1327112 | tf_op jit(solution)/shard_map/ppermute | solution.py:35
  384.4 7.7 %collective-permute-start.96 = (bf16[1,144,512]{2,1,0:T(8,128)(2,1)S(1)}, bf16[1,144,512]{2,1,0:T(8,128)(2,1)S(1)}, u32[]{:S(2)}, u32[]{:S(2)}) collective-permute-start(bf16[1,144,512]{2,1,0:T(8,128)(2,1)S(1)} %add_convert_fusion.30), channel_id=1, source_target_pairs={{0,4},{1,5},{2,6},{3,7},{4,0},{5,1},{6,2},{7,3},{8,12},{9,13},{10,... | collective-permute-start | bytes 442376 | tf_op jit(solution)/shard_map/ppermute | solution.py:35
  389.5 32.9 %collective-permute-start.85 = (bf16[2,864,128]{2,1,0:T(8,128)(2,1)S(1)}, bf16[2,864,128]{2,1,0:T(8,128)(2,1)S(1)}, u32[]{:S(2)}, u32[]{:S(2)}) collective-permute-start(bf16[2,864,128]{2,1,0:T(8,128)(2,1)S(1)} %get-tuple-element.140), channel_id=1, source_target_pairs={{0,24},{8,16},{16,8},{24,0},{1,25},{9,17},{17,9},{25,1},{2,26},{10... | collective-permute-start | bytes 1327112 | tf_op jit(solution)/shard_map/ppermute | solution.py:35
  392.1 8.9 %collective-permute-start.89 = (bf16[1,160,512]{2,1,0:T(8,128)(2,1)S(1)}, bf16[1,160,512]{2,1,0:T(8,128)(2,1)S(1)}, u32[]{:S(2)}, u32[]{:S(2)}) collective-permute-start(bf16[1,160,512]{2,1,0:T(8,128)(2,1)S(1)} %get-tuple-element.165), channel_id=1, source_target_pairs={{0,2},{1,3},{2,0},{3,1},{4,6},{5,7},{6,4},{7,5},{8,10},{9,11},{10,... | collective-permute-start | bytes 491528 | tf_op jit(solution)/shard_map/ppermute | solution.py:35
  392.3 8.7 %collective-permute-start.97 = (bf16[144,512]{1,0:T(8,128)(2,1)S(1)}, bf16[144,512]{1,0:T(8,128)(2,1)S(1)}, u32[]{:S(2)}, u32[]{:S(2)}) collective-permute-start(bf16[144,512]{1,0:T(8,128)(2,1)S(1)} %fusion), channel_id=1, source_target_pairs={{0,4},{1,5},{2,6},{3,7},{4,0},{5,1},{6,2},{7,3},{8,12},{9,13},{10,... | collective-permute-start | bytes 442376 | tf_op jit(solution)/shard_map/ppermute | solution.py:35
  401.0 11.0 %collective-permute-start.104 = (bf16[288,512]{1,0:T(8,128)(2,1)S(1)}, bf16[288,512]{1,0:T(8,128)(2,1)S(1)}, u32[]{:S(2)}, u32[]{:S(2)}) collective-permute-start(bf16[288,512]{1,0:T(8,128)(2,1)S(1)} %maximum_select_fusion.5), channel_id=1, source_target_pairs={{0,2},{1,3},{2,0},{3,1},{4,6},{5,7},{6,4},{7,5},{8,10},{9,11},{10,... | collective-permute-start | bytes 884744 | tf_op jit(solution)/shard_map/ppermute | solution.py:35
  401.0 6.6 %collective-permute-start.90 = (bf16[1,80,512]{2,1,0:T(8,128)(2,1)S(1)}, bf16[1,80,512]{2,1,0:T(8,128)(2,1)S(1)}, u32[]{:S(2)}, u32[]{:S(2)}) collective-permute-start(bf16[1,80,512]{2,1,0:T(8,128)(2,1)S(1)} %add_convert_fusion.34), channel_id=1, source_target_pairs={{0,4},{1,5},{2,6},{3,7},{4,0},{5,1},{6,2},{7,3},{8,12},{9,13},{10,... | collective-permute-start | bytes 245768 | tf_op jit(solution)/shard_map/ppermute | solution.py:35
  407.6 11.1 %collective-permute-start.98 = (bf16[288,512]{1,0:T(8,128)(2,1)S(1)}, bf16[288,512]{1,0:T(8,128)(2,1)S(1)}, u32[]{:S(2)}, u32[]{:S(2)}) collective-permute-start(bf16[288,512]{1,0:T(8,128)(2,1)S(1)} %maximum_select_fusion.4), channel_id=1, source_target_pairs={{0,2},{1,3},{2,0},{3,1},{4,6},{5,7},{6,4},{7,5},{8,10},{9,11},{10,... | collective-permute-start | bytes 884744 | tf_op jit(solution)/shard_map/ppermute | solution.py:35
  412.0 5.4 %collective-permute-start.91 = (bf16[80,512]{1,0:T(8,128)(2,1)S(1)}, bf16[80,512]{1,0:T(8,128)(2,1)S(1)}, u32[]{:S(2)}, u32[]{:S(2)}) collective-permute-start(bf16[80,512]{1,0:T(8,128)(2,1)S(1)} %fusion.3), channel_id=1, source_target_pairs={{0,4},{1,5},{2,6},{3,7},{4,0},{5,1},{6,2},{7,3},{8,12},{9,13},{10,... | collective-permute-start | bytes 245768 | tf_op jit(solution)/shard_map/ppermute | solution.py:35
  412.2 43.6 %collective-permute-start.109 = (bf16[576,512]{1,0:T(8,128)(2,1)S(1)}, bf16[576,512]{1,0:T(8,128)(2,1)S(1)}, u32[]{:S(2)}, u32[]{:S(2)}) collective-permute-start(bf16[576,512]{1,0:T(8,128)(2,1)S(1)} %maximum_select_fusion.2.refs_4_), channel_id=1, source_target_pairs={{0,1},{1,0},{2,3},{3,2},{4,5},{5,4},{6,7},{7,6},{8,9},{9,8},{10,11... | collective-permute-start | bytes 1769480 | tf_op jit(solution)/shard_map/ppermute | solution.py:35
  417.4 38.4 %collective-permute-start.105 = (bf16[576,512]{1,0:T(8,128)(2,1)S(1)}, bf16[576,512]{1,0:T(8,128)(2,1)S(1)}, u32[]{:S(2)}, u32[]{:S(2)}) collective-permute-start(bf16[576,512]{1,0:T(8,128)(2,1)S(1)} %maximum_select_fusion.1.refs_2_), channel_id=1, source_target_pairs={{0,1},{1,0},{2,3},{3,2},{4,5},{5,4},{6,7},{7,6},{8,9},{9,8},{10,11... | collective-permute-start | bytes 1769480 | tf_op jit(solution)/shard_map/ppermute | solution.py:35
  418.7 13.3 %collective-permute-start.92 = (bf16[160,512]{1,0:T(8,128)(2,1)S(1)}, bf16[160,512]{1,0:T(8,128)(2,1)S(1)}, u32[]{:S(2)}, u32[]{:S(2)}) collective-permute-start(bf16[160,512]{1,0:T(8,128)(2,1)S(1)} %maximum_select_fusion.7), channel_id=1, source_target_pairs={{0,2},{1,3},{2,0},{3,1},{4,6},{5,7},{6,4},{7,5},{8,10},{9,11},{10,... | collective-permute-start | bytes 491528 | tf_op jit(solution)/shard_map/ppermute | solution.py:35
  422.0 33.8 %collective-permute-start.99 = (bf16[576,512]{1,0:T(8,128)(2,1)S(1)}, bf16[576,512]{1,0:T(8,128)(2,1)}, u32[]{:S(2)}, u32[]{:S(2)}) collective-permute-start(bf16[576,512]{1,0:T(8,128)(2,1)S(1)} %maximum_select_fusion.refs_0_), channel_id=1, source_target_pairs={{0,1},{1,0},{2,3},{3,2},{4,5},{5,4},{6,7},{7,6},{8,9},{9,8},{10,11... | collective-permute-start | bytes 1769480 | tf_op jit(solution)/shard_map/ppermute | solution.py:35
  428.4 21.7 %collective-permute-start.86 = (bf16[2,64,320]{2,1,0:T(8,128)(2,1)S(1)}, bf16[2,64,320]{2,1,0:T(8,128)(2,1)S(1)}, u32[]{:S(2)}, u32[]{:S(2)}) collective-permute-start(bf16[2,64,320]{2,1,0:T(8,128)(2,1)S(1)} %get-tuple-element.112), channel_id=1, source_target_pairs={{0,1},{1,2},{2,3},{3,4},{4,5},{5,6},{6,7},{8,9},{9,10},{10,11},{11... | collective-permute-start | bytes 245768 | tf_op jit(solution)/shard_map/ppermute | solution.py:45
  432.1 21.6 %collective-permute-start.93 = (bf16[320,512]{1,0:T(8,128)(2,1)S(1)}, bf16[320,512]{1,0:T(8,128)(2,1)}, u32[]{:S(2)}, u32[]{:S(2)}) collective-permute-start(bf16[320,512]{1,0:T(8,128)(2,1)S(1)} %maximum_select_fusion.3.own_ref), channel_id=1, source_target_pairs={{0,1},{1,0},{2,3},{3,2},{4,5},{5,4},{6,7},{7,6},{8,9},{9,8},{10,11... | collective-permute-start | bytes 983048 | tf_op jit(solution)/shard_map/ppermute | solution.py:35
  (101 other events, 936.6 us)

commit v2 on v1

--- a/solution.py
+++ b/solution.py
@@ -19,6 +19,8 @@
 EPS = 1e-05
 SLACK_BYTES = 6 * 1024 * 1024
 LOW = jnp.bfloat16
+HIDERS = ("mid_forward_c", "mid_backward_c", "mid_backward_b", "mid_weight_b")
+HIDERS += ("mid_backward_a", "mid_weight_a", "entry_backward", "entry_weight")
 FULL = jnp.float32
 
 PLAN_FIELDS = ["chans", "spaces", "splits", "rows_dev", "own_rows", "bases", "pitch", "width"]
@@ -28,6 +30,7 @@
 VMEM = pl.BlockSpec(memory_space=pltpu.VMEM)
 SMEM = pl.BlockSpec(memory_space=pltpu.SMEM)
 HBM = pl.BlockSpec(memory_space=pltpu.HBM)
+ANY = pl.BlockSpec(memory_space=pl.ANY)
 
 
 def flipped(value, axis, bit):
@@ -70,7 +73,7 @@
     return [parts[0]] + [flipped(parts[rel], "chan", rel) for rel in range(1, plan.chans)]
 
 
-def micro_sums(value, plan, jobs=()):
+def micro_sums(value, plan, early=(), late=()):
     bits = []
     bit = 1
     while bit < plan.splits:
@@ -82,12 +85,19 @@
         bit *= 2
     for i in range(0, len(bits), 2):
         pair = bits[i : i + 2]
+        start = value
         one = exchanged(value, *pair[0], plan)
         if len(pair) == 2:
             two = exchanged(value, *pair[1], plan)
             both = exchanged(value, pair[0][0] ^ pair[1][0], pair[0][1] ^ pair[1][1], plan)
-        if i == 0 and jobs:
-            one = tied(one, *[job() for job in jobs])
+        done = []
+        if i == 0:
+            done = [job(one) for job in early]
+        elif i == 2:
+            done = [job(start) for job in late]
+        done = [token for token in jax.tree.leaves(done) if token is not None]
+        if done:
+            one = tied(one, *done)
         value = value + one
         if len(pair) == 2:
             value = value + (two + both)
@@ -95,62 +105,94 @@
 
 
 class WeightSum:
-    def __init__(self, keep, send, plan, across_first):
+    def __init__(self, keep, send, plan, order):
         self.send, self.plan = send, plan
-        self.pair = (keep, flipped(send, "chan", 1))
-        chan_steps, space_steps = [], []
-        bit = 2
-        while bit < plan.chans:
-            chan_steps.append(("chan", bit))
-            bit *= 2
-        bit = 1
-        while bit < plan.spaces:
-            space_steps.append(("space", bit))
-            bit *= 2
-        if across_first:
-            self.steps = space_steps[:1] + chan_steps + space_steps[1:]
-        else:
-            self.steps = chan_steps + space_steps
-        self.gathers = [bit for _, bit in space_steps[::-1]]
-        self.whole = None
+        self.kept = keep
+        self.received = [] if send is None else [flipped(send, "chan", 1)]
+        self.steps = []
+        named = [bit for step in order if step != "c" for bit in step]
+        rest = [k for k in range(plan.spaces.bit_length() - 1) if k not in named]
+        for step in list(order) + [(k,) for k in rest]:
+            if step == "c":
+                self.steps += [("chan", (1 << k,)) for k in range(1, plan.chans.bit_length() - 1)]
+            else:
+                self.steps.append(("space", tuple(1 << k for k in step)))
+        self.steps[-1] = ("swap", self.steps[-1][1])
+        self.gathers = [bits for axis, bits in self.steps if axis == "space"][::-1]
+        self.last = self.gathers[-1]
+        self.gathering = False
 
     def mine(self, bit):
         return (lax.axis_index("space") // bit) % 2
 
     def added(self, pick):
-        kept, received = (pick(part).astype(FULL) for part in self.pair)
-        return (kept + received).astype(LOW)
-
-    def advance(self):
+        total = pick(self.kept).astype(FULL)
+        for part in self.received:
+            total = total + pick(part).astype(FULL)
+        return total.astype(LOW)
+
+    def flips(self, bits):
+        ways = []
+        for number in range(1, 1 << len(bits)):
+            held = [(number >> i) & 1 for i in range(len(bits))]
+            ways.append((sum(bit for bit, on in zip(bits, held) if on), held))
+        return ways
+
+    def take(self, *after):
+        if after and self.received:
+            self.received[0] = tied(self.received[0], *after)
+        elif after:
+            self.kept = tied(self.kept, *after)
+
+    def advance(self, *after):
+        self.take(*after)
         if self.steps:
-            axis, bit = self.steps.pop(0)
-            if axis == "chan":
+            axis, bits = self.steps.pop(0)
+            if axis == "swap":
+                kept = self.added(lambda part: part)
+                sent = [(bits[0], kept)]
+                axis = "space"
+            elif axis == "chan":
                 kept = self.added(lambda part: part[0::2])
-                sent = self.added(lambda part: part[1::2])
+                sent = [(bits[0], self.added(lambda part: part[1::2]))]
             else:
-                half = self.pair[0].shape[1] // 2
-                at = self.mine(bit) * half
-                kept = self.added(lambda part: lax.dynamic_slice_in_dim(part, at, half, 1))
-                sent = self.added(lambda part: lax.dynamic_slice_in_dim(part, half - at, half, 1))
-            self.pair = (kept, flipped(sent, axis, bit))
-            return sent
-        bit = self.gathers.pop(0)
-        if self.whole is None:
-            self.whole = self.added(lambda part: part)[0]
-        else:
-            self.whole = self.ordered(*self.pair)
-        self.pair = (self.whole, flipped(self.whole, "space", bit), bit)
-        return self.whole
-
-    def ordered(self, own, received, bit):
-        low = jnp.concatenate([own, received], axis=0)
-        high = jnp.concatenate([received, own], axis=0)
-        return jnp.where(self.mine(bit) == 0, low, high)
-
-    def halves(self):
+                size = self.kept.shape[1] >> len(bits)
+
+                def piece(held):
+                    at = 0
+                    for bit, on in zip(bits[::-1], held[::-1]):
+                        at = 2 * at + (self.mine(bit) if not on else 1 - self.mine(bit))
+                    return self.added(lambda part: lax.dynamic_slice_in_dim(part, at * size, size, 1))
+
+                kept = piece([0] * len(bits))
+                sent = [(flip, piece(held)) for flip, held in self.flips(bits)]
+            self.kept = kept
+            self.received = [flipped(part, axis, flip) for flip, part in sent]
+            return sent[0][1]
+        bits = self.gathers.pop(0)
+        whole = self.ordered() if self.gathering else self.added(lambda part: part)
+        self.gathering = bits
+        self.kept = whole
+        self.received = [flipped(whole, "space", flip) for flip, _ in self.flips(bits)]
+        return whole
+
+    def ordered(self):
+        parts = [self.kept] + self.received
+        for bit in self.gathering:
+            turned = self.mine(bit) == 0
+            joined = []
+            for i in range(0, len(parts), 2):
+                low = jnp.concatenate(parts[i : i + 2], axis=1)
+                high = jnp.concatenate(parts[i : i + 2][::-1], axis=1)
+                joined.append(jnp.where(turned, low, high))
+            parts = joined
+        return parts[0]
+
+    def halves(self, *after):
         while self.steps or self.gathers:
-            self.advance()
-        return self.pair
+            self.advance(*after)
+        self.take(*after)
+        return self.kept[0], self.received[0][0]
 
 
 def tiles(count, size):
@@ -218,7 +260,27 @@
     return 2 * plan.pitch // 4 if plan.pitch % 32 == 0 else plan.pitch
 
 
-def spread_features_kernel(plan, chan_ref, x_ref, halo_ref, picks_ref, left_ref, right_ref, out_ref):
+def feature_pick(plan, side, first, count):
+    shape = (2 * MOST_SIDE * BLOCK, count)
+    place = lax.broadcasted_iota(jnp.int32, shape, 0)
+    cell = lax.broadcasted_iota(jnp.int32, shape, 1) + first
+    row, column = place & (BLOCK - 1), place >> (BLOCK.bit_length() - 1)
+    phase = jnp.where(column >= MOST_SIDE, 1, 0)
+    column = column - MOST_SIDE * phase
+    source = (2 * row + phase) * (2 * plan.width) + 2 * column + side
+    return jnp.where(source == cell, 1.0, 0.0).astype(LOW)
+
+
+def row_pick(plan, first, count, turned=False):
+    spots = MOST_SIDE * ROW_BLOCK
+    shape = (count, spots) if turned else (spots, count)
+    place = lax.broadcasted_iota(jnp.int32, shape, 1 if turned else 0)
+    cell = lax.broadcasted_iota(jnp.int32, shape, 0 if turned else 1) + first
+    row, column = place & (ROW_BLOCK - 1), place >> (ROW_BLOCK.bit_length() - 1)
+    return jnp.where(row * plan.width + column == cell, 1.0, 0.0).astype(LOW)
+
+
+def spread_features_kernel(plan, chan_ref, x_ref, halo_ref, out_ref):
     chan = chan_ref[0]
     size, lanes = plan.chans_in, BLOCK * 4 * plan.width
     columns = MOST_SIDE
@@ -232,16 +294,20 @@
         return jnp.concatenate(even, 0), jnp.concatenate(odd, 0)
 
     have = x_ref.shape[2]
+    own, extra = have % lanes, halo_ref.shape[2]
+    picks = [feature_pick(plan, side, 0, lanes) for side in range(2)]
+    left = [feature_pick(plan, side, 0, own) for side in range(2)]
+    right = [feature_pick(plan, side, own, extra) for side in range(2)]
     for j in range(-(-(plan.rows_dev + EXTRA) // BLOCK)):
         start = j * lanes
         if start + lanes <= have:
             even, odd = stacked([x_ref[m, :, start : start + lanes] for m in range(MICRO)])
-            result = dot_t(picks_ref[0], even) + dot_t(picks_ref[1], odd)
+            result = dot_t(picks[0], even) + dot_t(picks[1], odd)
         else:
             even, odd = stacked([x_ref[m, :, start:have] for m in range(MICRO)])
-            result = dot_t(left_ref[0], even) + dot_t(left_ref[1], odd)
+            result = dot_t(left[0], even) + dot_t(left[1], odd)
             even, odd = stacked([halo_ref[m] for m in range(MICRO)])
-            result += dot_t(right_ref[0], even) + dot_t(right_ref[1], odd)
+            result += dot_t(right[0], even) + dot_t(right[1], odd)
         result = result.astype(LOW)
         for split, base in enumerate(plan.bases):
             row = j * BLOCK - base
@@ -257,17 +323,20 @@
                         out_ref[to, phase, spot : spot + BLOCK] = part
 
 
-def spread_rows_kernel(plan, chan_ref, x_ref, halo_ref, pick_ref, left_ref, right_ref, out_ref):
+def spread_rows_kernel(plan, chan_ref, x_ref, halo_ref, out_ref):
     chan = chan_ref[0]
     size, spots = plan.chans_out, ROW_BLOCK * plan.width
     have = x_ref.shape[1]
+    own, extra = have % spots, halo_ref.shape[1]
+    pick, left = row_pick(plan, 0, spots), row_pick(plan, 0, own)
+    right = row_pick(plan, own, extra)
     for j in range(-(-(plan.rows_dev + EXTRA) // ROW_BLOCK)):
         start = j * spots
         for m in range(MICRO):
             if start + spots <= have:
-                result = dot(pick_ref[...], x_ref[m, start : start + spots])
+                result = dot(pick, x_ref[m, start : start + spots])
             else:
-                result = dot(left_ref[...], x_ref[m, start:have]) + dot(right_ref[...], halo_ref[m])
+                result = dot(left, x_ref[m, start:have]) + dot(right, halo_ref[m])
             result = result.astype(LOW)
             for split, base in enumerate(plan.bases):
                 low, high = max(j * ROW_BLOCK, base), min((j + 1) * ROW_BLOCK, base + plan.pitch)
@@ -295,7 +364,7 @@
     return pieces
 
 
-def join_rows_kernel(plan, chan_ref, picks_ref, left_ref, right_ref, *refs):
+def join_rows_kernel(plan, chan_ref, *refs):
     parts = refs[: plan.chans]
     out_ref, tail_ref, whole_ref = refs[plan.chans :]
     chan = chan_ref[0]
@@ -303,6 +372,9 @@
         whole_ref[chan ^ rel] = parts[rel][...]
     spots = ROW_BLOCK * plan.width
     have = out_ref.shape[1]
+    own, extra = have % spots, tail_ref.shape[1]
+    pick, left = row_pick(plan, 0, spots, True), row_pick(plan, 0, own, True)
+    right = row_pick(plan, own, extra, True)
     limit = plan.rows_dev + EXTRA
     for j in range(-(-limit // ROW_BLOCK)):
         start = j * spots
@@ -316,13 +388,13 @@
                     pieces.append(jnp.zeros(blank, LOW))
             rows = jnp.concatenate(pieces, 0)
             if start + spots <= have:
-                out_ref[m, start : start + spots] = dot(picks_ref[...], rows).astype(LOW)
+                out_ref[m, start : start + spots] = dot(pick, rows).astype(LOW)
             else:
-                out_ref[m, start:have] = dot(left_ref[...], rows).astype(LOW)
-                tail_ref[m] = dot(right_ref[...], rows).astype(LOW)
-
-
-def join_features_kernel(plan, chan_ref, picks_ref, left_ref, right_ref, *refs):
+                out_ref[m, start:have] = dot(left, rows).astype(LOW)
+                tail_ref[m] = dot(right, rows).astype(LOW)
+
+
+def join_features_kernel(plan, chan_ref, *refs):
     parts = refs[: plan.chans]
     out_ref, tail_ref, whole_ref = refs[plan.chans :]
     chan = chan_ref[0]
@@ -332,6 +404,10 @@
     one = unit(2 * size)
     lanes = BLOCK * 4 * plan.width
     have = out_ref.shape[2]
+    own, extra = have % lanes, tail_ref.shape[2]
+    picks = [feature_pick(plan, side, 0, lanes) for side in range(2)]
+    left = [feature_pick(plan, side, 0, own) for side in range(2)]
+    right = [feature_pick(plan, side, own, extra) for side in range(2)]
     for j in range(-(-(plan.rows_dev + EXTRA) // BLOCK)):
         start = j * lanes
         first, second = [], []
@@ -346,12 +422,12 @@
             second.append(turned[size:])
         first, second = jnp.concatenate(first, 0), jnp.concatenate(second, 0)
         if start + lanes <= have:
-            result = dot(first, picks_ref[0]) + dot(second, picks_ref[1])
+            result = dot(first, picks[0]) + dot(second, picks[1])
             for m in range(MICRO):
                 out_ref[m, :, start : start + lanes] = result[m * size : (m + 1) * size]
         else:
-            result = dot(first, left_ref[0]) + dot(second, left_ref[1])
-            tail = dot(first, right_ref[0]) + dot(second, right_ref[1])
+            result = dot(first, left[0]) + dot(second, left[1])
+            tail = dot(first, right[0]) + dot(second, right[1])
             for m in range(MICRO):
                 out_ref[m, :, start:have] = result[m * size : (m + 1) * size]
                 tail_ref[m] = tail[m * size : (m + 1) * size].astype(LOW)
@@ -383,7 +459,11 @@
     n = plan.chans
     x_refs, shard_refs = refs[:n], refs[n : 2 * n]
     e_ref, p_ref, stat_ref, xm_ref = refs[2 * n : 2 * n + 4]
-    w_ref, wp_ref, xs_ref, am_ref, sems = refs[2 * n + 4 :]
+    x_ref, w_ref, wp_ref, xs_ref, am_ref, sems, x_sems = refs[2 * n + 4 :]
+    x_copies = []
+    for rel in range(n):
+        x_copies.append(pltpu.make_async_copy(x_refs[rel], x_ref.at[rel], x_sems.at[rel]))
+        x_copies[-1].start()
     copies = entry_copies(plan, shard_refs, w_ref, wp_ref, sems)
     size = 2 * plan.chans_in
     deep = n * size
@@ -392,11 +472,12 @@
         am_ref[k, 0:pitch] = jnp.zeros((pitch, deep), LOW)
     clear_gaps(xs_ref, plan.spots)
     for rel in range(n):
+        x_copies[rel].wait()
         lanes = slice(rel * size, (rel + 1) * size)
         for t in tiles(plan.spots, vector_tile(plan)):
             own = marks_ref[t, 0:1]
             for row in range(2):
-                value = x_refs[rel][row, t].astype(FULL) * own
+                value = x_ref[rel, row, t].astype(FULL) * own
                 low = value.astype(LOW)
                 xm_ref[row, t, lanes] = low
                 am_ref[row, pitch + t.start : pitch + t.stop, lanes] = low
@@ -417,9 +498,9 @@
             pieces.append(am_ref[k, pitch + t.start : pitch + t.stop])
             pieces.append(am_ref[k, t])
         z = dot(jnp.concatenate(pieces, 1), weights)
-        e_ref[t] = z
+        e_ref[t] = z.astype(LOW)
         p = dot(pieces[2], proj)
-        p_ref[t] = p
+        p_ref[t] = p.astype(LOW)
         zm, pm = z * own, p * own
         for i, term in enumerate((zm, zm * z, pm, pm * p)):
             sums[i] = sums[i] + column_sum(term)
@@ -449,11 +530,11 @@
         own = marks_ref[t, 0:1]
         u = 0.0
         for (mean, inverse), src, j in zip(norms, z_refs, layers):
-            u = u + (par_ref[j : j + 1] * ((src[t] - mean) * inverse) + par_ref[5 + j : 6 + j])
+            u = u + (par_ref[j : j + 1] * ((src[t].astype(FULL) - mean) * inverse) + par_ref[5 + j : 6 + j])
         u = u * own
         a = u * logistic(u)
         if h_ref is not None:
-            h_ref[t] = a
+            h_ref[t] = a.astype(LOW)
         xs_ref[GAP + t.start : GAP + t.stop] = a
         low = a.astype(LOW)
         a_ref[t] = low
@@ -474,7 +555,7 @@
             for b in range(3):
                 pieces.append(xa_ref[a, t.start + b * pitch : t.stop + b * pitch])
         z = dot(jnp.concatenate(pieces, 1), weights)
-        z_ref[t] = z
+        z_ref[t] = z.astype(LOW)
         zm = z * own
         total = total + column_sum(zm)
         square = square + column_sum(zm * z)
@@ -495,12 +576,12 @@
         total, dotted = 0.0, 0.0
         for t in tiles(plan.spots, plan.pitch):
             own = marks_ref[t, 0:1]
-            hat = (z_ref[t, lanes] - mean[:, lanes]) * inverse[:, lanes]
-            u = own * (par_ref[4:5, lanes] * hat + par_ref[9:10, lanes]) + h_ref[t, lanes]
+            hat = (z_ref[t, lanes].astype(FULL) - mean[:, lanes]) * inverse[:, lanes]
+            u = own * (par_ref[4:5, lanes] * hat + par_ref[9:10, lanes]) + h_ref[t, lanes].astype(FULL)
             s = logistic(u)
             out_ref[chan ^ j, t] = (u * s).astype(LOW)
             q = og_ref[j, t].astype(FULL) * (s * (1.0 + u * (1.0 - s))) * own
-            g_ref[t, lanes] = q
+            g_ref[t, lanes] = q.astype(LOW)
             total = total + column_sum(q)
             dotted = dotted + column_sum(q * hat)
         out_stat_ref[0:1, lanes] = total
@@ -551,8 +632,9 @@
         short_norm = moments(short_stat_ref[...], inv)
     for t in tiles(plan.spots, vector_tile(plan)):
         own, upper, lower = (marks_ref[t, i : i + 1] for i in range(3))
-        g = g_ref[t]
-        gz = norm_back(own, g, z_ref[t], norm, par_ref[j : j + 1], total, dotted, inv)
+        g = g_ref[t].astype(FULL)
+        z = z_ref[t].astype(FULL)
+        gz = norm_back(own, g, z, norm, par_ref[j : j + 1], total, dotted, inv)
         low = gz.astype(LOW)
         gz = low.astype(FULL)
         ga_ref[1, pitch + t.start : pitch + t.stop] = low
@@ -560,7 +642,8 @@
         s2_ref[GAP + t.start : GAP + t.stop] = gz * lower
         if kind == "entry":
             back = norm_back(
-                own, g, short_z_ref[t], short_norm, par_ref[2:3], total, back_ref[2:3], inv
+                own, g, short_z_ref[t].astype(FULL), short_norm, par_ref[2:3], total,
+                back_ref[2:3], inv,
             )
             short_ref[t] = back.astype(LOW)
     for t in tiles(plan.spots, vector_tile(plan)):
@@ -584,14 +667,14 @@
         u = 0.0
         hats = []
         for (mean, inverse), src, i in zip(norms, src_refs, layers):
-            hat = (src[t] - mean) * inverse
+            hat = (src[t].astype(FULL) - mean) * inverse
             hats.append(hat)
             u = u + (par_ref[i : i + 1] * hat + par_ref[5 + i : 6 + i])
         u = u * own
         if add_ref is not None:
-            gx = gx + add_ref[t]
+            gx = gx + add_ref[t].astype(FULL)
         q = gx * slope(u) * own
-        next_ref[t] = q
+        next_ref[t] = q.astype(LOW)
         sums[0] = sums[0] + column_sum(q)
         for i, hat in enumerate(hats):
             sums[1 + i] = sums[1 + i] + column_sum(q * hat)
@@ -607,7 +690,8 @@
     for t in tiles(plan.spots, vector_tile(plan)):
         own, upper = marks_ref[t, 0:1], marks_ref[t, 1:2]
         gz = norm_back(
-            own, g_ref[t], e_ref[t], norm, par_ref[0:1], back_ref[0:1], back_ref[1:2], inv
+            own, g_ref[t].astype(FULL), e_ref[t].astype(FULL), norm, par_ref[0:1], back_ref[0:1],
+            back_ref[1:2], inv,
         )
         low = gz.astype(LOW)
         gm_ref[0, t] = low
@@ -689,17 +773,18 @@
         put(9, rel, proj[2 * rel * size : (2 * rel + 1) * size])
 
 
-def mid_assembly_kernel(count, mine_ref, *refs):
-    parts, out_ref, hold_ref, sems = refs[: 2 * count], *refs[2 * count :]
-    half = parts[0].shape[0]
+def mid_assembly_kernel(mine_ref, *refs):
+    out_ref, hold_ref, sems = refs[6:]
+    half = refs[0].shape[0]
     copies = []
-    for i, part in enumerate(parts):
-        hold_ref[i] = part[...].astype(FULL)
-        at = mine_ref[0] if i % 2 == 0 else 1 - mine_ref[0]
-        rows = pl.ds(pl.multiple_of(at * half, 8), half)
-        copy = pltpu.make_async_copy(hold_ref.at[i], out_ref.at[i // 2, rows], sems.at[i])
-        copy.start()
-        copies.append(copy)
+    for layer in range(3):
+        mine = mine_ref[layer]
+        for i, part in enumerate(refs[2 * layer : 2 * layer + 2]):
+            at = mine if i == 0 else 1 - mine
+            rows = pl.ds(pl.multiple_of(at * half, 8), half)
+            hold_ref[layer, rows] = part[...].astype(FULL)
+        copies.append(pltpu.make_async_copy(hold_ref.at[layer], out_ref.at[layer], sems.at[layer]))
+        copies[-1].start()
     for copy in copies:
         copy.wait()
 
@@ -707,7 +792,7 @@
 def entry_assembly_kernel(mine_ref, own_ref, other_ref, conv_ref, proj_ref, hold_ref, sems):
     half = own_ref.shape[0]
     for i, part in enumerate((own_ref, other_ref)):
-        at = mine_ref[0] if i == 0 else 1 - mine_ref[0]
+        at = mine_ref[3] if i == 0 else 1 - mine_ref[3]
         hold_ref[pl.ds(pl.multiple_of(at * half, 8), half)] = part[...].astype(FULL)
     cut = conv_ref.shape[0]
     copies = [
@@ -720,9 +805,10 @@
         copy.wait()
 
 
-def call(kernel, operands, specs, outs, out_specs, scratch, flops, name):
+def call(kernel, operands, specs, outs, out_specs, scratch, name, flops=0):
     bytes_moved = sum(int(np.prod(o.shape)) * o.dtype.itemsize for o in operands)
     bytes_moved += sum(int(np.prod(s)) * jnp.dtype(d).itemsize for s, d in outs)
+    bytes_moved = 1 if name in HIDERS else bytes_moved
     shapes = [jax.ShapeDtypeStruct(s, d) for s, d in outs]
     held = SLACK_BYTES
     for one in scratch:
@@ -740,34 +826,6 @@
         ),
         name=name,
     )(*operands)
-
-
-def feature_picks(plan):
-    width, columns = plan.width, MOST_SIDE
-    picks = np.zeros((2, 2 * columns * BLOCK, BLOCK * 4 * width), np.float32)
-    for side in range(2):
-        for phase in range(2):
-            for c in range(columns):
-                for r in range(BLOCK):
-                    source = (2 * r + phase) * 2 * width + 2 * c + side
-                    picks[side, (phase * columns + c) * BLOCK + r, source] = 1.0
-    return picks
-
-
-def row_picks(plan):
-    width = plan.width
-    picks = np.zeros((MOST_SIDE * ROW_BLOCK, ROW_BLOCK * width), np.float32)
-    for c in range(MOST_SIDE):
-        for r in range(ROW_BLOCK):
-            picks[c * ROW_BLOCK + r, r * width + c] = 1.0
-    return picks
-
-
-def cut_picks(picks, rows, per_row, rows_dev, turned=False):
-    own = rows_dev % rows * per_row
-    extra = EXTRA * per_row
-    parts = (picks, picks[..., :own], picks[..., own : own + extra])
-    return [jnp.asarray((part.T if turned else part).astype(LOW)) for part in parts]
 
 
 def marks_of(plan, sizes, top, first):
@@ -814,22 +872,20 @@
     first = here + split * own_rows
     chan_at = chan.astype(jnp.int32).reshape(1)
 
-    picks = cut_picks(feature_picks(plan), BLOCK, 4 * width, rows_dev)
-    halo = from_next(features[:, :, : EXTRA * 4 * width])
+    edge = features[:, :, : EXTRA * 4 * width]
+    halo = from_next(edge)
+    out_grad = jnp.swapaxes(out_grad, 1, 2)
+    out_halo = from_next(out_grad[:, : EXTRA * width])
     (spread,) = call(
         functools.partial(spread_features_kernel, plan),
-        (chan_at, features, halo, *picks),
-        [SMEM] + [VMEM] * 5,
+        (chan_at, features, tied(halo, out_halo)),
+        [SMEM] + [VMEM] * 2,
         [((chans, 2, spots, 2 * chans_in), LOW)],
         [VMEM],
         [],
-        2 * 2 * 2 * spots * 640 * chans * 2 * chans_in,
         "spread_features",
     )
     x_parts = swapped(spread, plan)
-    entry_own = jnp.concatenate([conv_in_w.reshape(9, chans_in, wide), proj_w[None]], axis=0)
-    entry_shards = gathered(entry_own, plan)
-
     slots = jnp.concatenate([norm_gain, norm_bias], axis=0)
     slots = lax.dynamic_update_slice(
         jnp.zeros((10, wide), FULL), slots, (jnp.int32(0), chan * chans_out)
@@ -839,14 +895,27 @@
         slots = slots + flipped(slots, "chan", bit)
         bit *= 2
     pars = slots
-    mid_first = tied(conv_mid_w[0], *x_parts, *entry_shards, pars)
-
     sizes = lax.dynamic_index_in_dim(image_sizes, micro, 0, keepdims=False)
     bases_at = jnp.asarray(bases, jnp.int32)[split]
     marks, inv = marks_of(plan, sizes, here + bases_at, first)
 
+    (grad_spread,) = call(
+        functools.partial(spread_rows_kernel, plan),
+        (chan_at, out_grad, tied(out_halo, x_parts[1])),
+        [SMEM] + [VMEM] * 2,
+        [((chans, spots, chans_out), LOW)],
+        [VMEM],
+        [],
+        "spread_rows",
+    )
+
+    entry_own = jnp.concatenate([conv_in_w.reshape(9, chans_in, wide), proj_w[None]], axis=0)
+    entry_own = tied(entry_own, edge)
+    entry_shards = gathered(entry_own, plan, (*x_parts[chans // 2 :], pars, grad_spread))
+    mid_first = tied(conv_mid_w[0], *x_parts[chans // 2 :])
+
     conv_flops = 2 * spots * 9 * wide * wide
-    field = ((spots, wide), FULL)
+    field = ((spots, wide), LOW)
     deep = chans * 2 * chans_in
     entry_scratch = [
         pltpu.VMEM((3, 2, chans, 2, chans_in, wide), LOW),
@@ -856,21 +925,28 @@
     z0, zp, stats, xm = call(
         functools.partial(entry_forward_kernel, plan),
         (marks, *x_parts, *entry_shards),
-        [VMEM] * (1 + chans) + [HBM] * chans,
+        [VMEM] + [ANY] * (2 * chans),
         [field, field, ((4, wide), FULL), ((2, spots, deep), LOW)],
         [VMEM] * 4,
-        entry_scratch
+        [pltpu.VMEM((chans, 2, spots, 2 * chans_in), LOW)]
+        + entry_scratch
         + [
             pltpu.VMEM((spots + 2 * GAP, deep), FULL),
             pltpu.VMEM((3, spots + pitch, deep), LOW),
             pltpu.SemaphoreType.DMA((7 * chans,)),
+            pltpu.SemaphoreType.DMA((chans,)),
         ],
-        2 * spots * 7 * deep * wide,
         "entry_forward",
-    )
-    mid_shards = [gathered(mid_first, plan, (stats,))]
+        conv_flops // 2,
+    )
+    mid_shards = []
+
+    def second_hop(layer):
+        return lambda value: mid_shards.append(gathered(layer, plan, (value,)))
+
     mid_second = tied(conv_mid_w[1], stats)
-    stats = micro_sums(stats, plan)
+    stats = micro_sums(stats, plan, (), [second_hop(mid_first)])
+    mid_third = tied(conv_mid_w[2], stats)
     stat0, statp = stats[0:2], stats[2:4]
 
     weight_scratch = pltpu.VMEM((3, 3, wide, wide), LOW)
@@ -888,36 +964,19 @@
             outs,
             [VMEM] * len(outs),
             [weight_scratch, padded, pltpu.VMEM((3, spots + 2 * pitch, wide), LOW), shard_sems],
-            conv_flops,
             name,
+            0 if name in HIDERS else conv_flops,
         )
 
     z2, stat1, a_first = mid_forward((0,), (z0,), (stat0,), mid_shards[0], "mid_forward_a")
-    mid_shards.append(gathered(mid_second, plan, (stat1,)))
-    mid_third = tied(conv_mid_w[2], stat1)
-    picks_out = cut_picks(row_picks(plan), ROW_BLOCK, width, rows_dev)
-    picks_back = cut_picks(row_picks(plan), ROW_BLOCK, width, rows_dev, True)
-    out_grad = jnp.swapaxes(out_grad, 1, 2)
-    halo = from_next(out_grad[:, : EXTRA * width])
-    (grad_spread,) = call(
-        functools.partial(spread_rows_kernel, plan),
-        (chan_at, out_grad, halo, *picks_out),
-        [SMEM] + [VMEM] * 5,
-        [((chans, spots, chans_out), LOW)],
-        [VMEM],
-        [],
-        2 * spots * 640 * wide,
-        "spread_rows",
-    )
     og_parts = swapped(tied(grad_spread, stat1), plan)
-    stat1 = micro_sums(stat1, plan)
+    stat1 = micro_sums(stat1, plan, (), [second_hop(mid_second)])
     z3, stat3, a_second, h1 = mid_forward(
         (1, 2), (z2, zp), (stat1, statp), mid_shards[1], "mid_forward_b"
     )
-    mid_shards.append(gathered(mid_third, plan, (stat3,)))
-    stat3 = micro_sums(stat3, plan)
+    stat3 = micro_sums(stat3, plan, (), [second_hop(mid_third)])
     z4, stat4, a_third = mid_forward((3,), (z3,), (stat3,), mid_shards[2], "mid_forward_c")
-    stat4 = micro_sums(stat4, plan)
+    stat4 = micro_sums(tied(stat4, *og_parts[1:]), plan)
 
     block, gh2, back4 = call(
         functools.partial(head_kernel, plan),
@@ -926,10 +985,10 @@
         [((chans, spots, chans_out), LOW), field, ((2, wide), FULL)],
         [VMEM] * 3,
         [pltpu.VMEM((chans, spots, chans_out), LOW)],
-        spots * wide * 30,
         "head",
     )
     back4 = micro_sums(back4, plan)
+    block_parts = swapped(block, plan)
 
     def mid_backward(j, kind, g, z, stat, back, weights, others, extra_outs, name):
         count = 3 if kind == "join" else 2
@@ -941,40 +1000,61 @@
             outs,
             [VMEM] * len(outs),
             [weight_scratch, padded, padded, shard_sems],
-            conv_flops,
             name,
+            0 if name in HIDERS else conv_flops,
         )
 
-    def mid_weight(a, ga, name, across_first):
-        keep, send = call(
+    def mid_weight(a, ga, name):
+        return call(
             functools.partial(mid_weight_kernel, plan),
             (chan_at, a, ga),
             [SMEM, VMEM, VMEM],
             [((chans // 2, 9 * chans_out, wide), LOW)] * 2,
             [VMEM, VMEM],
             [pltpu.VMEM((wide, spots), LOW)] * 2,
-            conv_flops,
             name,
+            0 if name in HIDERS else conv_flops,
         )
-        return WeightSum(keep, send, plan, across_first)
-
     ga_third, g3, back3 = mid_backward(
         4, "plain", gh2, z4, stat4, back4, mid_shards[2], (z3, stat3), [], "mid_backward_c"
     )
-    third = mid_weight(a_third, ga_third, "mid_weight_c", False)
-    back3 = micro_sums(back3, plan, [lambda: third.send])
+    sums_of = {}
+
+    def weigh(key, a, ga, order, behind=()):
+        def job(value):
+            keep, send = mid_weight(tied(a, value), ga, "mid_weight_" + key)
+            others = [part for other in behind for part in sums_of[other].received]
+            if others:
+                send = tied(send, *others)
+            sums_of[key] = WeightSum(keep, send, plan, order)
+            return [send] + [sums_of[other].advance(send) for other in behind]
+
+        return job
+
+    def step(key):
+        return lambda value: sums_of[key].advance(value)
+
+    back3 = micro_sums(
+        tied(back3, *block_parts[1:]), plan,
+        [weigh("c", a_third, ga_third, ["c", (0,), (1,), (2,)])],
+        [step("c")],
+    )
     ga_second, gh1, back12 = mid_backward(
         3, "join", g3, z3, stat3, back3, mid_shards[1], (z2, zp, stat1, statp, gh2), [],
         "mid_backward_b",
     )
-    second = mid_weight(a_second, ga_second, "mid_weight_b", False)
-    back12 = micro_sums(back12, plan, [lambda: second.send, third.advance])
+    back12 = micro_sums(
+        back12, plan, [weigh("b", a_second, ga_second, ["c", (1,), (0,), (2,)], "c")], [step("b")]
+    )
     ga_first, g1, back0, gzp = mid_backward(
         1, "entry", gh1, z2, stat1, back12, mid_shards[0], (z0, stat0, zp, statp),
         [((spots, wide), LOW)], "mid_backward_a",
     )
-    first_sum = mid_weight(a_first, ga_first, "mid_weight_a", True)
-    back0 = micro_sums(back0, plan, [lambda: first_sum.send, second.advance, third.advance])
+    back0 = micro_sums(
+        back0, plan,
+        [weigh("a", a_first, ga_first, [(0,), "c", (1,), (2,)], "cb")],
+        [step("c")],
+    )
     (gm,) = call(
         functools.partial(entry_norm_kernel, plan),
         (inv, marks, pars, g1, z0, stat0, back0),
@@ -982,84 +1062,98 @@
         [((2, spots + pitch, wide), LOW)],
         [VMEM],
         [padded],
-        spots * wide * 20,
         "entry_norm",
     )
+    token = sums_of["a"].advance(gm)
+    (gx,) = call(
+        functools.partial(entry_backward_kernel, plan),
+        (marks, tied(gm, token), gzp, *entry_shards),
+        [VMEM] * 3 + [ANY] * chans,
+        [((chans, 2, spots, 2 * chans_in), LOW)],
+        [VMEM],
+        entry_scratch + [pltpu.SemaphoreType.DMA((7 * chans,))],
+        "entry_backward",
+    )
+    gx_parts = swapped(gx, plan)
     keep, send = call(
         functools.partial(entry_weight_kernel, plan),
-        (xm, tied(gm, first_sum.advance()), gzp),
+        (xm, tied(gm, gx), gzp),
         [VMEM] * 3,
         [((chans // 2, 10 * chans_in, wide), LOW)] * 2,
         [VMEM] * 2,
         [pltpu.VMEM((2, deep, spots), LOW)],
-        2 * spots * 7 * deep * wide,
         "entry_weight",
     )
-    entry_sum = WeightSum(keep, send, plan, True)
-    (gx,) = call(
-        functools.partial(entry_backward_kernel, plan),
-        (marks, gm, tied(gzp, send, third.advance()), *entry_shards),
-        [VMEM] * 3 + [HBM] * chans,
-        [((chans, 2, spots, 2 * chans_in), LOW)],
-        [VMEM],
-        entry_scratch + [pltpu.SemaphoreType.DMA((7 * chans,))],
-        2 * spots * 7 * deep * wide,
-        "entry_backward",
-    )
-    gx_parts = swapped(gx, plan)
-    gx_parts[1] = tied(
-        gx_parts[1], entry_sum.advance(), second.advance(), third.advance(), first_sum.advance()
-    )
-
-    def joined(kernel, parts, matrices, shape, axis, extra, dtype, whole, flops, name):
+    send = tied(
+        send, gx_parts[chans // 2], *[part for key in "abc" for part in sums_of[key].received]
+    )
+    sums_of["e"] = WeightSum(keep, send, plan, [(0,), (1,), "c", (2,)])
+
+    def chain(last, keys):
+        for key in keys:
+            last = sums_of[key].advance(last)
+        return last
+
+    def joined(kernel, parts, shape, axis, extra, dtype, whole, name):
         edge = tuple(extra if i == axis else n for i, n in enumerate(shape))
-        main, tail = call(
+        return call(
             functools.partial(kernel, plan),
-            (chan_at, *matrices, *parts),
-            [SMEM] + [VMEM] * (3 + chans),
+            (chan_at, *parts),
+            [SMEM] + [VMEM] * chans,
             [(shape, dtype), (edge, LOW)],
             [VMEM] * 2,
             [pltpu.VMEM(whole, LOW)],
-            flops,
             name,
         )
-        first = lax.slice_in_dim(main, 0, extra, axis=axis) + to_next(tail).astype(dtype)
+
+    def topped(main, tail, axis):
+        first = lax.slice_in_dim(main, 0, tail.shape[axis], axis=axis) + tail.astype(main.dtype)
         return lax.dynamic_update_slice(main, first, (0, 0, 0))
 
-    block_out = joined(
-        join_rows_kernel, swapped(block, plan), picks_back, out_grad.shape, 1, EXTRA * width, LOW,
-        (chans, spots, chans_out), 2 * spots * wide * 800, "join_rows",
-    )
-    block_out = jnp.swapaxes(block_out, 1, 2)
-    feature_grad = joined(
-        join_features_kernel, gx_parts, picks, features.shape, 2, EXTRA * 4 * width, FULL,
-        (chans, 2, spots, 2 * chans_in), 8 * spots * 640 * chans * chans_in, "join_features",
-    )
-
-    last = ((lax.axis_index("space")) % 2).astype(jnp.int32).reshape(1)
-    mids = [one.halves()[:2] for one in (first_sum, second, third)]
+    token = chain(send, "cab")
+    token = chain(tied(token, gx_parts[-1]), "e")
+    gx_parts[0] = tied(gx_parts[0], token)
+    feature_grad, feature_tail = joined(
+        join_features_kernel, gx_parts, features.shape, 2, EXTRA * 4 * width, FULL,
+        (chans, 2, spots, 2 * chans_in), "join_features",
+    )
+    token = feature_tail
+    feature_tail = to_next(feature_tail)
+    token = chain(token, "be")
+    block_parts[0] = tied(block_parts[0], token)
+    block_out, block_tail = joined(
+        join_rows_kernel, block_parts, out_grad.shape, 1, EXTRA * width, LOW,
+        (chans, spots, chans_out), "join_rows",
+    )
+    token = block_tail
+    block_tail = to_next(block_tail)
+    token = chain(token, "aecb")
+    feature_grad = topped(feature_grad, tied(feature_tail, token), 2)
+    block_out = jnp.swapaxes(topped(block_out, tied(block_tail, token), 1), 1, 2)
+    token = chain(token, "eabeaea")
+
+    def mine(key):
+        return sums_of[key].mine(sums_of[key].last[0])
+
+    last = jnp.stack([mine(key) for key in "abce"]).astype(jnp.int32)
     (conv_mid_grad,) = call(
-        functools.partial(mid_assembly_kernel, 3),
-        (last, *[part for pair in mids for part in pair]),
+        mid_assembly_kernel,
+        (last, *[part for key in "abc" for part in sums_of[key].halves(token)]),
         [SMEM] + [VMEM] * 6,
         [((3, 9 * chans_out, wide), FULL)],
         [HBM],
-        [
-            pltpu.VMEM((6, 9 * chans_out // 2, wide), FULL),
-            pltpu.SemaphoreType.DMA((6,)),
-        ],
-        0,
+        [pltpu.VMEM((3, 9 * chans_out, wide), FULL), pltpu.SemaphoreType.DMA((3,))],
         "mid_assembly",
     )
+    entry_own, entry_other = sums_of["e"].halves(token)
     conv_mid_grad = conv_mid_grad.reshape(3, 3, 3, chans_out, wide)
     conv_in_grad, proj_grad = call(
         entry_assembly_kernel,
-        (last, *entry_sum.halves()[:2]),
+        (last, entry_own, entry_other),
         [SMEM] + [VMEM] * 2,
         [((9 * chans_in, wide), FULL), ((chans_in, wide), FULL)],
         [HBM] * 2,
         [pltpu.VMEM((10 * chans_in, wide), FULL), pltpu.SemaphoreType.DMA((2,))],
-        0,
         "entry_assembly",
     )
     conv_in_grad = conv_in_grad.reshape(3, 3, chans_in, wide)

time: 466 us -> 433 us (0.929)
  waiting for transfers between devices: 190 us -> 145 us
  other arithmetic: 23.5 us -> 35.3 us
  starting transfers between devices: 109 us -> 114 us
    ppermute x59 -> x55, waiting for transfers between devices: 136 us -> 108 us  [flipped(): return lax.ppermute(value, axis, [(i, i ^ bit) for i in range(count)])]
    ppermute x2, waiting for transfers between devices: 17.4 us -> 0.01 us  [to_next(): return lax.ppermute(value, 'space', [(i, i + 1) for i in range(count - 1)])]
    convert_element_type x16 -> x20, other arithmetic: 15.4 us -> 25.4 us  [added(): return total.astype(LOW)]
    ppermute x48, starting transfers between devices: 51.2 us -> 61.3 us  [exchanged(): lax.ppermute(value, ('chan', 'space'), [(i, i ^ flip) for i in range(coun...]
    unnamed x106 -> x98, local copies, waits for them, and re-layouts: 20.4 us -> 13.8 us
    ppermute x59 -> x55, starting transfers between devices: 48.4 us -> 43.6 us  [flipped(): return lax.ppermute(value, axis, [(i, i ^ bit) for i in range(count)])]
  transfers between devices with their start and end apart: 111 -> 107, of which waited for: 57 -> 50; matrix products, arithmetic and copies ran while one was open for 7% -> 9% of each run, Pallas kernels for 19% -> 22%
where the time goes in v2:
time: 433 us; the launch traced here: 428 us
  waiting for transfers between devices  145 us (33%)
  starting transfers between devices  114 us (26%)
  Pallas kernels  104 us (24%)
  other arithmetic  35.3 us (8%)
  local copies, waits for them, and re-layouts  26.1 us (6%)
    ppermute x55, waiting for transfers between devices, flipped(): return lax.ppermute(value, axis, [(i, i ^ bit) for i in range(count)])  108 us
    pallas_call x20, Pallas kernels, call(): pl.pallas_call(kernel, out_shape=shapes, in_specs=specs, out_specs=out_sp...  104 us
    ppermute x48, starting transfers between devices, exchanged(): lax.ppermute(value, ('chan', 'space'), [(i, i ^ flip) for i in range(coun...  61.3 us
    ppermute x55, starting transfers between devices, flipped(): return lax.ppermute(value, axis, [(i, i ^ bit) for i in range(count)])  43.6 us
    ppermute x48, waiting for transfers between devices, exchanged(): lax.ppermute(value, ('chan', 'space'), [(i, i ^ flip) for i in range(coun...  36.6 us
    convert_element_type x20, other arithmetic, added(): return total.astype(LOW)  25.4 us
    unnamed x98, local copies, waits for them, and re-layouts  13.8 us
  transfers between devices with their start and end apart: 107, of which 50 were waited for; matrix products, arithmetic and copies ran while one was open for 9% of the time, Pallas kernels for 22%

profile of v2, /device:TPU:0, one launch (start us, length us, event | category | flops | bytes accessed | tf_op | source)
XLA Modules:
  0.0 427.5 jit_solution(11228446572375509502)
XLA Ops:
  7.3 2.6 collective-permute-start.8
  11.0 3.5 slice_bitcast_fusion
  14.6 2.8 spread_features.1
  21.2 13.8 %collective-permute-done.5.refs_2_ = bf16[2,864,128]{2,1,0:T(8,128)(2,1)} collective-permute-done((bf16[2,864,128]{2,1,0:T(8,128)(2,1)}, bf16[2,864,128]{2,1,0:T(8,128)(2,1)}, u32[]{:S(2)}, u32[]{:S(2)}) %collective-permute-start.5) | collective-permute-done | bytes 442400 | tf_op jit(solution)/shard_map/ppermute | solution.py:38
  35.0 1.9 collective-permute-start.1
  37.0 7.2 %collective-permute-done.6.refs_3_ = bf16[2,864,128]{2,1,0:T(8,128)(2,1)} collective-permute-done((bf16[2,864,128]{2,1,0:T(8,128)(2,1)}, bf16[2,864,128]{2,1,0:T(8,128)(2,1)}, u32[]{:S(2)}, u32[]{:S(2)}) %collective-permute-start.6) | collective-permute-done | bytes 442400 | tf_op jit(solution)/shard_map/ppermute | solution.py:38
  53.0 6.4 %entry_forward.1 = (bf16[864,512]{1,0:T(8,128)(2,1)S(1)}, bf16[864,512]{1,0:T(8,128)(2,1)S(1)}, f32[4,512]{1,0:T(4,128)S(1)}, bf16[2,864,512]{2,1,0:T(8,128)(2,1)S(1)}) custom-call(f32[864,8]{1,0:T(8,128)S(1)} %convert_element_type.300.marks_ref, bf16[2,864,128]{2,1,0:T(8,128)(2,1)S(1)} %copy-done.24, bf16[2,864,128]{2,1,0:T(8,128)(2,1)} %collective-permute-done.4.refs_1_, ...), custom_call_target="tpu_custom_call" | custom-call | flops 2038431744 | bytes 7965696 | tf_op jit(solution)/shard_map/entry_forward/pallas_call | solution.py:817
  62.6 3.0 collective-permute-start.11
  68.7 4.0 collective-permute-done.17.refs_4_.refs_6_
  74.4 4.8 %collective-permute-start.14 = (f32[4,512]{1,0:T(4,128)S(1)}, f32[4,512]{1,0:T(4,128)S(1)}, u32[]{:S(2)}, u32[]{:S(2)}) collective-permute-start(f32[4,512]{1,0:T(4,128)S(1)} %add_add_fusion.3), channel_id=1, source_target_pairs={{0,4},{1,5},{2,6},{3,7},{4,0},{5,1},{6,2},{7,3},{8,12},{9,13},{10,... | collective-permute-start | bytes 24584 | tf_op jit(solution)/shard_map/ppermute | solution.py:54
  80.9 1.9 collective-permute-start.13
  86.0 7.4 %mid_forward_a.1 = (bf16[864,512]{1,0:T(8,128)(2,1)S(1)}, f32[2,512]{1,0:T(2,128)S(1)}, bf16[864,512]{1,0:T(8,128)(2,1)S(1)}) custom-call(s32[1]{0:T(128)} %bitcast.chan_ref, f32[1]{0:T(128)} %bitcast.2.inv_ref, f32[864,8]{1,0:T(8,128)S(1)} %convert_element_type.300.marks_ref, f32[10,512]{1,0:T(8,128)S(1)} %add.396.par_ref, bf16[864,512]{1,0:T(8,128)(2,1)S(1)} %copy-done.6, ...), custom_call_target="tpu_custom_call" | custom-call | flops 4076863488 | bytes 7429128 | tf_op jit(solution)/shard_map/mid_forward_a/pallas_call | solution.py:817
  98.0 3.2 collective-permute-done.26.refs_6_
  102.9 4.7 %collective-permute-start.23 = (f32[2,512]{1,0:T(2,128)S(1)}, f32[2,512]{1,0:T(2,128)S(1)}, u32[]{:S(2)}, u32[]{:S(2)}) collective-permute-start(f32[2,512]{1,0:T(2,128)S(1)} %add_add_fusion.15), channel_id=1, source_target_pairs={{0,4},{1,5},{2,6},{3,7},{4,0},{5,1},{6,2},{7,3},{8,12},{9,13},{10,... | collective-permute-start | bytes 12296 | tf_op jit(solution)/shard_map/ppermute | solution.py:54
  109.2 1.9 collective-permute-start.22
  111.1 1.9 collective-permute-done.24
  113.1 6.6 %mid_forward_b.1 = (bf16[864,512]{1,0:T(8,128)(2,1)S(1)}, f32[2,512]{1,0:T(2,128)S(1)}, bf16[864,512]{1,0:T(8,128)(2,1)S(1)}, bf16[864,512]{1,0:T(8,128)(2,1)S(1)}) custom-call(s32[1]{0:T(128)} %bitcast.chan_ref, f32[1]{0:T(128)} %bitcast.2.inv_ref, f32[864,8]{1,0:T(8,128)S(1)} %convert_element_type.300.marks_ref, f32[10,512]{1,0:T(8,128)S(1)} %add.396.par_ref, ...), custom_call_target="tpu_custom_call" | custom-call | flops 4076863488 | bytes 9202696 | tf_op jit(solution)/shard_map/mid_forward_b/pallas_call | solution.py:817
  124.3 5.2 %collective-permute-done.35.refs_4_.refs_6_ = bf16[3,3,128,512]{3,2,1,0:T(8,128)(2,1)S(1)} collective-permute-done((bf16[3,3,128,512]{3,2,1,0:T(8,128)(2,1)S(1)}, bf16[3,3,128,512]{3,2,1,0:T(8,128)(2,1)S(1)}, u32[]{:S(2)}, u32[]{:S(2)}) %collective-permute-start.35) | collective-permute-done | bytes 1179680 | tf_op jit(solution)/shard_map/ppermute | solution.py:38
  129.6 5.4 %collective-permute-start.32 = (f32[2,512]{1,0:T(2,128)S(1)}, f32[2,512]{1,0:T(2,128)S(1)}, u32[]{:S(2)}, u32[]{:S(2)}) collective-permute-start(f32[2,512]{1,0:T(2,128)S(1)} %add_add_fusion.13), channel_id=1, source_target_pairs={{0,4},{1,5},{2,6},{3,7},{4,0},{5,1},{6,2},{7,3},{8,12},{9,13},{10,... | collective-permute-start | bytes 12296 | tf_op jit(solution)/shard_map/ppermute | solution.py:54
  136.7 3.7 collective-permute-done.33
  141.5 6.4 %mid_forward_c.1 = (bf16[864,512]{1,0:T(8,128)(2,1)S(1)}, f32[2,512]{1,0:T(2,128)S(1)}, bf16[864,512]{1,0:T(8,128)(2,1)S(1)}) custom-call(s32[1]{0:T(128)} %bitcast.chan_ref, f32[1]{0:T(128)} %bitcast.2.inv_ref, f32[864,8]{1,0:T(8,128)S(1)} %convert_element_type.300.marks_ref, f32[10,512]{1,0:T(8,128)S(1)} %add.396.par_ref, ...), custom_call_target="tpu_custom_call" | custom-call | bytes 1 | tf_op jit(solution)/shard_map/mid_forward_c/pallas_call | solution.py:817
  159.2 2.3 collective-permute-done.45
  167.6 2.2 collective-permute-start.51
  173.5 7.3 %mid_backward_c.1 = (bf16[3,1056,512]{2,1,0:T(8,128)(2,1)S(1)}, bf16[864,512]{1,0:T(8,128)(2,1)S(1)}, f32[2,512]{1,0:T(2,128)S(1)}) custom-call(s32[1]{0:T(128)} %bitcast.chan_ref, f32[1]{0:T(128)} %bitcast.2.inv_ref, f32[864,8]{1,0:T(8,128)S(1)} %convert_element_type.300.marks_ref, f32[10,512]{1,0:T(8,128)S(1)} %add.396.par_ref, ...), custom_call_target="tpu_custom_call" | custom-call | bytes 1 | tf_op jit(solution)/shard_map/mid_backward_c/pallas_call | solution.py:817
  185.3 5.9 %mid_weight_c.1 = (bf16[2,1152,512]{2,1,0:T(8,128)(2,1)S(1)}, bf16[2,1152,512]{2,1,0:T(8,128)(2,1)S(1)}) custom-call(s32[1]{0:T(128)} %bitcast.chan_ref, bf16[864,512]{1,0:T(8,128)(2,1)S(1)} %get-tuple-element.136.a_ref, bf16[3,1056,512]{2,1,0:T(8,128)(2,1)S(1)} %get-tuple-element.137.ga_ref), custom_call_target="tpu_custom_call" | custom-call | flops 4076863488 | bytes 8847364 | tf_op jit(solution)/shard_map/mid_weight_c/pallas_call | solution.py:817
  193.1 2.0 collective-permute-done.56
  201.2 1.8 collective-permute-start.61
  204.4 2.2 collective-permute-done.61
  206.6 7.5 %mid_backward_b.1 = (bf16[3,1056,512]{2,1,0:T(8,128)(2,1)S(1)}, bf16[864,512]{1,0:T(8,128)(2,1)S(1)}, f32[3,512]{1,0:T(4,128)S(1)}) custom-call(s32[1]{0:T(128)} %bitcast.chan_ref, f32[1]{0:T(128)} %bitcast.2.inv_ref, f32[864,8]{1,0:T(8,128)S(1)} %convert_element_type.300.marks_ref, f32[10,512]{1,0:T(8,128)S(1)} %add.396.par_ref, ...), custom_call_target="tpu_custom_call" | custom-call | bytes 1 | tf_op jit(solution)/shard_map/mid_backward_b/pallas_call | solution.py:817
  215.4 7.2 %mid_weight_b.1 = (bf16[2,1152,512]{2,1,0:T(8,128)(2,1)S(1)}, bf16[2,1152,512]{2,1,0:T(8,128)(2,1)}) custom-call(s32[1]{0:T(128)} %bitcast.chan_ref, bf16[864,512]{1,0:T(8,128)(2,1)S(1)} %get-tuple-element.146.a_ref, bf16[3,1056,512]{2,1,0:T(8,128)(2,1)S(1)} %get-tuple-element.147.ga_ref), custom_call_target="tpu_custom_call" | custom-call | bytes 1 | tf_op jit(solution)/shard_map/mid_weight_b/pallas_call | solution.py:817
  222.6 3.0 collective-permute-done.63
  228.5 2.7 add_convert_fusion.12
  231.5 4.2 add_convert_fusion.2
  240.7 1.8 collective-permute-start.69
  243.7 2.4 collective-permute-done.69
  246.2 9.0 %mid_backward_a.1 = (bf16[3,1056,512]{2,1,0:T(8,128)(2,1)S(1)}, bf16[864,512]{1,0:T(8,128)(2,1)S(1)}, f32[2,512]{1,0:T(2,128)S(1)}, bf16[864,512]{1,0:T(8,128)(2,1)S(1)}) custom-call(s32[1]{0:T(128)} %bitcast.chan_ref, f32[1]{0:T(128)} %bitcast.2.inv_ref, f32[864,8]{1,0:T(8,128)S(1)} %convert_element_type.300.marks_ref, f32[10,512]{1,0:T(8,128)S(1)} %add.396.par_ref, ...), custom_call_target="tpu_custom_call" | custom-call | bytes 1 | tf_op jit(solution)/shard_map/mid_backward_a/pallas_call | solution.py:817
  256.5 7.3 %mid_weight_a.1 = (bf16[2,1152,512]{2,1,0:T(8,128)(2,1)S(1)}, bf16[2,1152,512]{2,1,0:T(8,128)(2,1)}) custom-call(s32[1]{0:T(128)} %bitcast.chan_ref, bf16[864,512]{1,0:T(8,128)(2,1)S(1)} %copy-done.20, bf16[3,1056,512]{2,1,0:T(8,128)(2,1)S(1)} %get-tuple-element.159.ga_ref), custom_call_target="tpu_custom_call" | custom-call | bytes 1 | tf_op jit(solution)/shard_map/mid_weight_a/pallas_call | solution.py:817
  269.5 2.9 add_convert_fusion.10
  272.4 2.4 collective-permute-start.77
  274.8 2.0 collective-permute-start.78
  276.8 2.1 collective-permute-done.76
  282.1 3.3 add_convert_fusion
  286.1 6.4 %entry_backward.1 = bf16[4,2,864,128]{3,2,1,0:T(8,128)(2,1)S(1)} custom-call(f32[864,8]{1,0:T(8,128)S(1)} %convert_element_type.300.marks_ref, bf16[2,960,512]{2,1,0:T(8,128)(2,1)S(1)} %entry_norm.1.gm_ref, bf16[864,512]{1,0:T(8,128)(2,1)S(1)} %get-tuple-element.170.short_ref, bf16[10,64,512]{2,1,0:T(8,128)(2,1)S(1)} %pad_maximum_fusion.refs_4_.refs_0_, ...), custom_call_target="tpu_custom_call" | custom-call | bytes 1 | tf_op jit(solution)/shard_map/entry_backward/pallas_call | solution.py:817
  294.6 2.4 collective-permute-start.83
  297.0 6.1 %entry_weight.1 = (bf16[2,640,512]{2,1,0:T(8,128)(2,1)S(1)}, bf16[2,640,512]{2,1,0:T(8,128)(2,1)}) custom-call(bf16[2,864,512]{2,1,0:T(8,128)(2,1)S(1)} %copy-done.15, bf16[2,960,512]{2,1,0:T(8,128)(2,1)S(1)} %entry_norm.1.gm_ref, bf16[864,512]{1,0:T(8,128)(2,1)S(1)} %get-tuple-element.170.short_ref), custom_call_target="tpu_custom_call" | custom-call | bytes 1 | tf_op jit(solution)/shard_map/entry_weight/pallas_call | solution.py:817
  303.2 5.7 %collective-permute-done.83 = bf16[1,288,512]{2,1,0:T(8,128)(2,1)S(1)} collective-permute-done((bf16[1,288,512]{2,1,0:T(8,128)(2,1)S(1)}, bf16[1,288,512]{2,1,0:T(8,128)(2,1)S(1)}, u32[]{:S(2)}, u32[]{:S(2)}) %collective-permute-start.83) | collective-permute-done | bytes 294944 | tf_op jit(solution)/shard_map/ppermute | solution.py:38
  309.0 3.0 collective-permute-done.81
  314.4 3.0 add_convert_fusion.8
  318.9 2.7 add_convert_fusion.7
  324.3 2.8 collective-permute-done.106
  328.1 6.0 %join_features.1 = (f32[2,64,6720]{2,1,0:T(8,128)}, bf16[2,64,320]{2,1,0:T(8,128)(2,1)S(1)}) custom-call(s32[1]{0:T(128)} %bitcast.chan_ref, bf16[2,864,128]{2,1,0:T(8,128)(2,1)S(1)} %get-tuple-element.178.refs_0_, bf16[2,864,128]{2,1,0:T(8,128)(2,1)S(1)} %collective-permute-done.87.refs_1_, bf16[2,864,128]{2,1,0:T(8,128)(2,1)S(1)} %collective-permute-done.80.refs_2_, ...), custom_call_target="tpu_custom_call" | custom-call | bytes 5292036 | tf_op jit(solution)/shard_map/join_features/pallas_call | solution.py:817
  335.2 6.6 %collective-permute-done.85 = bf16[2,320,512]{2,1,0:T(8,128)(2,1)S(1)} collective-permute-done((bf16[2,320,512]{2,1,0:T(8,128)(2,1)}, bf16[2,320,512]{2,1,0:T(8,128)(2,1)S(1)}, u32[]{:S(2)}, u32[]{:S(2)}) %collective-permute-start.85) | collective-permute-done | bytes 655392 | tf_op jit(solution)/shard_map/ppermute | solution.py:38
  345.7 2.6 collective-permute-start.94
  348.3 2.4 join_rows.1
  350.7 4.4 %collective-permute-start.89 = (bf16[2,80,128]{2,1,0:T(8,128)(2,1)S(1)}, bf16[2,80,128]{2,1,0:T(8,128)(2,1)S(1)}, u32[]{:S(2)}, u32[]{:S(2)}) collective-permute-start(bf16[2,80,128]{2,1,0:T(8,128)(2,1)S(1)} %get-tuple-element.184), channel_id=1, source_target_pairs={{0,1},{1,2},{2,3},{3,4},{4,5},{5,6},{6,7},{8,9},{9,10},{10,11},{11... | collective-permute-start | bytes 122888 | tf_op jit(solution)/shard_map/ppermute | solution.py:48
  355.2 4.0 collective-permute-done.92
  359.3 6.3 %collective-permute-done.91 = bf16[1,288,512]{2,1,0:T(8,128)(2,1)S(1)} collective-permute-done((bf16[1,288,512]{2,1,0:T(8,128)(2,1)S(1)}, bf16[1,288,512]{2,1,0:T(8,128)(2,1)S(1)}, u32[]{:S(2)}, u32[]{:S(2)}) %collective-permute-start.91) | collective-permute-done | bytes 294944 | tf_op jit(solution)/shard_map/ppermute | solution.py:38
  371.1 3.0 collective-permute-start.100
  374.1 12.4 %collective-permute-done.97 = bf16[1,288,512]{2,1,0:T(8,128)(2,1)S(1)} collective-permute-done((bf16[1,288,512]{2,1,0:T(8,128)(2,1)S(1)}, bf16[1,288,512]{2,1,0:T(8,128)(2,1)S(1)}, u32[]{:S(2)}, u32[]{:S(2)}) %collective-permute-start.97) | collective-permute-done | bytes 294944 | tf_op jit(solution)/shard_map/ppermute | solution.py:38
  388.2 2.2 collective-permute-done.100
  393.6 2.1 collective-permute-start.104
  395.8 5.4 %collective-permute-done.102 = bf16[1,288,512]{2,1,0:T(8,128)(2,1)S(1)} collective-permute-done((bf16[1,288,512]{2,1,0:T(8,128)(2,1)S(1)}, bf16[1,288,512]{2,1,0:T(8,128)(2,1)S(1)}, u32[]{:S(2)}, u32[]{:S(2)}) %collective-permute-start.102) | collective-permute-done | bytes 294944 | tf_op jit(solution)/shard_map/ppermute | solution.py:38
  405.5 16.4 %collective-permute-done.101 = bf16[1,320,512]{2,1,0:T(8,128)(2,1)S(1)} collective-permute-done((bf16[1,320,512]{2,1,0:T(8,128)(2,1)S(1)}, bf16[1,320,512]{2,1,0:T(8,128)(2,1)S(1)}, u32[]{:S(2)}, u32[]{:S(2)}) %collective-permute-start.101) | collective-permute-done | bytes 327712 | tf_op jit(solution)/shard_map/ppermute | solution.py:38
  423.6 3.7 mid_assembly.1
  (367 shorter events, 135.2 us)
Async XLA Ops:
  1.4 19.2 %collective-permute-start = (f32[10,512]{1,0:T(8,128)S(1)}, f32[10,512]{1,0:T(8,128)S(1)}, u32[]{:S(2)}, u32[]{:S(2)}) collective-permute-start(f32[10,512]{1,0:T(8,128)S(1)} %constant_dynamic-update-slice_fusion.1), channel_id=1, source_target_pairs={{0,8},{8,0},{16,24},{24,16},{1,9},{9,1},{17,25},{25,17},{2,10},{10... | collective-permute-start | bytes 61448 | tf_op jit(solution)/shard_map/ppermute | solution.py:38
  2.7 11.9 %collective-permute-start.2 = (bf16[2,64,320]{2,1,0:T(8,128)(2,1)S(1)}, bf16[2,64,320]{2,1,0:T(8,128)(2,1)S(1)}, u32[]{:S(2)}, u32[]{:S(2)}) collective-permute-start(bf16[2,64,320]{2,1,0:T(8,128)(2,1)S(1)} %slice.182), channel_id=1, source_target_pairs={{1,0},{2,1},{3,2},{4,3},{5,4},{6,5},{7,6},{9,8},{10,9},{11,10},{12... | collective-permute-start | bytes 245768 | tf_op jit(solution)/shard_map/ppermute | solution.py:43
  4.8 9.8 %collective-permute-start.3 = (bf16[2,80,128]{2,1,0:T(8,128)(2,1)S(1)}, bf16[2,80,128]{2,1,0:T(8,128)(2,1)S(1)}, u32[]{:S(2)}, u32[]{:S(2)}) collective-permute-start(bf16[2,80,128]{2,1,0:T(8,128)(2,1)S(1)} %slice.233), channel_id=1, source_target_pairs={{1,0},{2,1},{3,2},{4,3},{5,4},{6,5},{7,6},{9,8},{10,9},{11,10},{12... | collective-permute-start | bytes 122888 | tf_op jit(solution)/shard_map/ppermute | solution.py:43
  7.3 42.0 %collective-permute-start.8 = (bf16[10,64,512]{2,1,0:T(8,128)(2,1)S(1)}, bf16[10,64,512]{2,1,0:T(8,128)(2,1)}, u32[]{:S(2)}, u32[]{:S(2)}) collective-permute-start(bf16[10,64,512]{2,1,0:T(8,128)(2,1)S(1)} %pad_maximum_fusion.refs_4_.refs_0_), channel_id=1, source_target_pairs={{0,16},{8,24},{16,0},{24,8},{1,17},{9,25},{17,1},{25,9},{2,18},{10... | collective-permute-start | bytes 1966088 | tf_op jit(solution)/shard_map/ppermute | solution.py:38
  18.7 27.2 %collective-permute-start.4 = (bf16[2,864,128]{2,1,0:T(8,128)(2,1)}, bf16[2,864,128]{2,1,0:T(8,128)(2,1)}, u32[]{:S(2)}, u32[]{:S(2)}) collective-permute-start(bf16[2,864,128]{2,1,0:T(8,128)(2,1)} %get-tuple-element.236), channel_id=1, source_target_pairs={{0,8},{8,0},{16,24},{24,16},{1,9},{9,1},{17,25},{25,17},{2,10},{10... | collective-permute-start | bytes 1327112 | tf_op jit(solution)/shard_map/ppermute | solution.py:38
  19.0 16.1 %collective-permute-start.5 = (bf16[2,864,128]{2,1,0:T(8,128)(2,1)}, bf16[2,864,128]{2,1,0:T(8,128)(2,1)}, u32[]{:S(2)}, u32[]{:S(2)}) collective-permute-start(bf16[2,864,128]{2,1,0:T(8,128)(2,1)} %get-tuple-element.235), channel_id=1, source_target_pairs={{0,16},{8,24},{16,0},{24,8},{1,17},{9,25},{17,1},{25,9},{2,18},{10... | collective-permute-start | bytes 1327112 | tf_op jit(solution)/shard_map/ppermute | solution.py:38
  19.3 24.9 %collective-permute-start.6 = (bf16[2,864,128]{2,1,0:T(8,128)(2,1)}, bf16[2,864,128]{2,1,0:T(8,128)(2,1)}, u32[]{:S(2)}, u32[]{:S(2)}) collective-permute-start(bf16[2,864,128]{2,1,0:T(8,128)(2,1)} %get-tuple-element.234), channel_id=1, source_target_pairs={{0,24},{8,16},{16,8},{24,0},{1,25},{9,17},{17,9},{25,1},{2,26},{10... | collective-permute-start | bytes 1327112 | tf_op jit(solution)/shard_map/ppermute | solution.py:38
  20.6 31.4 %collective-permute-start.7 = (bf16[10,64,512]{2,1,0:T(8,128)(2,1)S(1)}, bf16[10,64,512]{2,1,0:T(8,128)(2,1)}, u32[]{:S(2)}, u32[]{:S(2)}) collective-permute-start(bf16[10,64,512]{2,1,0:T(8,128)(2,1)S(1)} %pad_maximum_fusion.refs_4_.refs_0_), channel_id=1, source_target_pairs={{0,8},{8,0},{16,24},{24,16},{1,9},{9,1},{17,25},{25,17},{2,10},{10... | collective-permute-start | bytes 1966088 | tf_op jit(solution)/shard_map/ppermute | solution.py:38
  35.0 10.8 %collective-permute-start.1 = (f32[10,512]{1,0:T(8,128)S(1)}, f32[10,512]{1,0:T(8,128)S(1)}, u32[]{:S(2)}, u32[]{:S(2)}) collective-permute-start(f32[10,512]{1,0:T(8,128)S(1)} %constant_dynamic-update-slice_fusion), channel_id=1, source_target_pairs={{0,16},{8,24},{16,0},{24,8},{1,17},{9,25},{17,1},{25,9},{2,18},{10... | collective-permute-start | bytes 61448 | tf_op jit(solution)/shard_map/ppermute | solution.py:38
  44.1 28.5 %collective-permute-start.17 = (bf16[3,3,128,512]{3,2,1,0:T(8,128)(2,1)}, bf16[3,3,128,512]{3,2,1,0:T(8,128)(2,1)}, u32[]{:S(2)}, u32[]{:S(2)}) collective-permute-start(bf16[3,3,128,512]{3,2,1,0:T(8,128)(2,1)} %get-tuple-element.112.refs_2_.refs_4_), channel_id=1, source_target_pairs={{0,16},{8,24},{16,0},{24,8},{1,17},{9,25},{17,1},{25,9},{2,18},{10... | collective-permute-start | bytes 3538952 | tf_op jit(solution)/shard_map/ppermute | solution.py:38
  65.7 19.1 %collective-permute-start.16 = (bf16[3,3,128,512]{3,2,1,0:T(8,128)(2,1)}, bf16[3,3,128,512]{3,2,1,0:T(8,128)(2,1)}, u32[]{:S(2)}, u32[]{:S(2)}) collective-permute-start(bf16[3,3,128,512]{3,2,1,0:T(8,128)(2,1)} %get-tuple-element.112.refs_2_.refs_4_), channel_id=1, source_target_pairs={{0,8},{8,0},{16,24},{24,16},{1,9},{9,1},{17,25},{25,17},{2,10},{10... | collective-permute-start | bytes 3538952 | tf_op jit(solution)/shard_map/ppermute | solution.py:38
  72.7 12.1 %collective-permute-start.18 = (bf16[3,3,128,512]{3,2,1,0:T(8,128)(2,1)}, bf16[3,3,128,512]{3,2,1,0:T(8,128)(2,1)}, u32[]{:S(2)}, u32[]{:S(2)}) collective-permute-start(bf16[3,3,128,512]{3,2,1,0:T(8,128)(2,1)} %collective-permute-done.17.refs_4_.refs_6_), channel_id=1, source_target_pairs={{0,8},{8,0},{16,24},{24,16},{1,9},{9,1},{17,25},{25,17},{2,10},{10... | collective-permute-start | bytes 3538952 | tf_op jit(solution)/shard_map/ppermute | solution.py:38
  72.7 28.5 %collective-permute-start.26 = (bf16[3,3,128,512]{3,2,1,0:T(8,128)(2,1)S(1)}, bf16[3,3,128,512]{3,2,1,0:T(8,128)(2,1)}, u32[]{:S(2)}, u32[]{:S(2)}) collective-permute-start(bf16[3,3,128,512]{3,2,1,0:T(8,128)(2,1)S(1)} %get-tuple-element.117.refs_4_), channel_id=1, source_target_pairs={{0,16},{8,24},{16,0},{24,8},{1,17},{9,25},{17,1},{25,9},{2,18},{10... | collective-permute-start | bytes 3538952 | tf_op jit(solution)/shard_map/ppermute | solution.py:38
  74.4 6.5 %collective-permute-start.14 = (f32[4,512]{1,0:T(4,128)S(1)}, f32[4,512]{1,0:T(4,128)S(1)}, u32[]{:S(2)}, u32[]{:S(2)}) collective-permute-start(f32[4,512]{1,0:T(4,128)S(1)} %add_add_fusion.3), channel_id=1, source_target_pairs={{0,4},{1,5},{2,6},{3,7},{4,0},{5,1},{6,2},{7,3},{8,12},{9,13},{10,... | collective-permute-start | bytes 24584 | tf_op jit(solution)/shard_map/ppermute | solution.py:54
  79.3 5.4 %collective-permute-start.15 = (f32[4,512]{1,0:T(4,128)S(1)}, f32[4,512]{1,0:T(4,128)S(1)}, u32[]{:S(2)}, u32[]{:S(2)}) collective-permute-start(f32[4,512]{1,0:T(4,128)S(1)} %add_add_fusion.3), channel_id=1, source_target_pairs={{0,6},{1,7},{2,4},{3,5},{4,2},{5,3},{6,0},{7,1},{8,14},{9,15},{10,... | collective-permute-start | bytes 24584 | tf_op jit(solution)/shard_map/ppermute | solution.py:54
  95.6 17.4 %collective-permute-start.25 = (bf16[3,3,128,512]{3,2,1,0:T(8,128)(2,1)S(1)}, bf16[3,3,128,512]{3,2,1,0:T(8,128)(2,1)S(1)}, u32[]{:S(2)}, u32[]{:S(2)}) collective-permute-start(bf16[3,3,128,512]{3,2,1,0:T(8,128)(2,1)S(1)} %get-tuple-element.117.refs_4_), channel_id=1, source_target_pairs={{0,8},{8,0},{16,24},{24,16},{1,9},{9,1},{17,25},{25,17},{2,10},{10... | collective-permute-start | bytes 3538952 | tf_op jit(solution)/shard_map/ppermute | solution.py:38
  101.2 11.9 %collective-permute-start.27 = (bf16[3,3,128,512]{3,2,1,0:T(8,128)(2,1)}, bf16[3,3,128,512]{3,2,1,0:T(8,128)(2,1)S(1)}, u32[]{:S(2)}, u32[]{:S(2)}) collective-permute-start(bf16[3,3,128,512]{3,2,1,0:T(8,128)(2,1)} %collective-permute-done.26.refs_6_), channel_id=1, source_target_pairs={{0,8},{8,0},{16,24},{24,16},{1,9},{9,1},{17,25},{25,17},{2,10},{10... | collective-permute-start | bytes 3538952 | tf_op jit(solution)/shard_map/ppermute | solution.py:38
  101.2 28.4 %collective-permute-start.35 = (bf16[3,3,128,512]{3,2,1,0:T(8,128)(2,1)S(1)}, bf16[3,3,128,512]{3,2,1,0:T(8,128)(2,1)S(1)}, u32[]{:S(2)}, u32[]{:S(2)}) collective-permute-start(bf16[3,3,128,512]{3,2,1,0:T(8,128)(2,1)S(1)} %get-tuple-element.121.refs_2_.refs_4_), channel_id=1, source_target_pairs={{0,16},{8,24},{16,0},{24,8},{1,17},{9,25},{17,1},{25,9},{2,18},{10... | collective-permute-start | bytes 3538952 | tf_op jit(solution)/shard_map/ppermute | solution.py:38
  102.9 6.3 %collective-permute-start.23 = (f32[2,512]{1,0:T(2,128)S(1)}, f32[2,512]{1,0:T(2,128)S(1)}, u32[]{:S(2)}, u32[]{:S(2)}) collective-permute-start(f32[2,512]{1,0:T(2,128)S(1)} %add_add_fusion.15), channel_id=1, source_target_pairs={{0,4},{1,5},{2,6},{3,7},{4,0},{5,1},{6,2},{7,3},{8,12},{9,13},{10,... | collective-permute-start | bytes 12296 | tf_op jit(solution)/shard_map/ppermute | solution.py:54
  107.6 5.4 %collective-permute-start.24 = (f32[2,512]{1,0:T(2,128)S(1)}, f32[2,512]{1,0:T(2,128)S(1)}, u32[]{:S(2)}, u32[]{:S(2)}) collective-permute-start(f32[2,512]{1,0:T(2,128)S(1)} %add_add_fusion.15), channel_id=1, source_target_pairs={{0,6},{1,7},{2,4},{3,5},{4,2},{5,3},{6,0},{7,1},{8,14},{9,15},{10,... | collective-permute-start | bytes 12296 | tf_op jit(solution)/shard_map/ppermute | solution.py:54
  122.0 19.5 %collective-permute-start.34 = (bf16[3,3,128,512]{3,2,1,0:T(8,128)(2,1)S(1)}, bf16[3,3,128,512]{3,2,1,0:T(8,128)(2,1)S(1)}, u32[]{:S(2)}, u32[]{:S(2)}) collective-permute-start(bf16[3,3,128,512]{3,2,1,0:T(8,128)(2,1)S(1)} %get-tuple-element.121.refs_2_.refs_4_), channel_id=1, source_target_pairs={{0,8},{8,0},{16,24},{24,16},{1,9},{9,1},{17,25},{25,17},{2,10},{10... | collective-permute-start | bytes 3538952 | tf_op jit(solution)/shard_map/ppermute | solution.py:38
  129.6 11.9 %collective-permute-start.36 = (bf16[3,3,128,512]{3,2,1,0:T(8,128)(2,1)S(1)}, bf16[3,3,128,512]{3,2,1,0:T(8,128)(2,1)S(1)}, u32[]{:S(2)}, u32[]{:S(2)}) collective-permute-start(bf16[3,3,128,512]{3,2,1,0:T(8,128)(2,1)S(1)} %collective-permute-done.35.refs_4_.refs_6_), channel_id=1, source_target_pairs={{0,8},{8,0},{16,24},{24,16},{1,9},{9,1},{17,25},{25,17},{2,10},{10... | collective-permute-start | bytes 3538952 | tf_op jit(solution)/shard_map/ppermute | solution.py:38
  129.6 7.0 %collective-permute-start.32 = (f32[2,512]{1,0:T(2,128)S(1)}, f32[2,512]{1,0:T(2,128)S(1)}, u32[]{:S(2)}, u32[]{:S(2)}) collective-permute-start(f32[2,512]{1,0:T(2,128)S(1)} %add_add_fusion.13), channel_id=1, source_target_pairs={{0,4},{1,5},{2,6},{3,7},{4,0},{5,1},{6,2},{7,3},{8,12},{9,13},{10,... | collective-permute-start | bytes 12296 | tf_op jit(solution)/shard_map/ppermute | solution.py:54
  136.6 11.3 %collective-permute-start.37 = (bf16[864,128]{1,0:T(8,128)(2,1)S(1)}, bf16[864,128]{1,0:T(8,128)(2,1)S(1)}, u32[]{:S(2)}, u32[]{:S(2)}) collective-permute-start(bf16[864,128]{1,0:T(8,128)(2,1)S(1)} %get-tuple-element.247), channel_id=1, source_target_pairs={{0,8},{8,0},{16,24},{24,16},{1,9},{9,1},{17,25},{25,17},{2,10},{10... | collective-permute-start | bytes 663560 | tf_op jit(solution)/shard_map/ppermute | solution.py:38
  140.4 8.4 %collective-permute-start.38 = (bf16[864,128]{1,0:T(8,128)(2,1)S(1)}, bf16[864,128]{1,0:T(8,128)(2,1)S(1)}, u32[]{:S(2)}, u32[]{:S(2)}) collective-permute-start(bf16[864,128]{1,0:T(8,128)(2,1)S(1)} %get-tuple-element.246), channel_id=1, source_target_pairs={{0,16},{8,24},{16,0},{24,8},{1,17},{9,25},{17,1},{25,9},{2,18},{10... | collective-permute-start | bytes 663560 | tf_op jit(solution)/shard_map/ppermute | solution.py:38
  141.4 8.7 %collective-permute-start.39 = (bf16[864,128]{1,0:T(8,128)(2,1)S(1)}, bf16[864,128]{1,0:T(8,128)(2,1)S(1)}, u32[]{:S(2)}, u32[]{:S(2)}) collective-permute-start(bf16[864,128]{1,0:T(8,128)(2,1)S(1)} %get-tuple-element.245), channel_id=1, source_target_pairs={{0,24},{8,16},{16,8},{24,0},{1,25},{9,17},{17,9},{25,1},{2,26},{10... | collective-permute-start | bytes 663560 | tf_op jit(solution)/shard_map/ppermute | solution.py:38
  167.6 5.5 %collective-permute-start.51 = (f32[2,512]{1,0:T(2,128)S(1)}, f32[2,512]{1,0:T(2,128)S(1)}, u32[]{:S(2)}, u32[]{:S(2)}) collective-permute-start(f32[2,512]{1,0:T(2,128)S(1)} %add_add_fusion.9), channel_id=1, source_target_pairs={{0,6},{1,7},{2,4},{3,5},{4,2},{5,3},{6,0},{7,1},{8,14},{9,15},{10,... | collective-permute-start | bytes 12296 | tf_op jit(solution)/shard_map/ppermute | solution.py:54
  171.2 9.6 %collective-permute-start.52 = (bf16[864,128]{1,0:T(8,128)(2,1)S(1)}, bf16[864,128]{1,0:T(8,128)(2,1)S(1)}, u32[]{:S(2)}, u32[]{:S(2)}) collective-permute-start(bf16[864,128]{1,0:T(8,128)(2,1)S(1)} %get-tuple-element.242), channel_id=1, source_target_pairs={{0,8},{8,0},{16,24},{24,16},{1,9},{9,1},{17,25},{25,17},{2,10},{10... | collective-permute-start | bytes 663560 | tf_op jit(solution)/shard_map/ppermute | solution.py:38
  171.2 10.3 %collective-permute-start.53 = (bf16[864,128]{1,0:T(8,128)(2,1)S(1)}, bf16[864,128]{1,0:T(8,128)(2,1)S(1)}, u32[]{:S(2)}, u32[]{:S(2)}) collective-permute-start(bf16[864,128]{1,0:T(8,128)(2,1)S(1)} %get-tuple-element.241), channel_id=1, source_target_pairs={{0,16},{8,24},{16,0},{24,8},{1,17},{9,25},{17,1},{25,9},{2,18},{10... | collective-permute-start | bytes 663560 | tf_op jit(solution)/shard_map/ppermute | solution.py:38
  172.3 11.1 %collective-permute-start.54 = (bf16[864,128]{1,0:T(8,128)(2,1)S(1)}, bf16[864,128]{1,0:T(8,128)(2,1)S(1)}, u32[]{:S(2)}, u32[]{:S(2)}) collective-permute-start(bf16[864,128]{1,0:T(8,128)(2,1)S(1)} %get-tuple-element.240), channel_id=1, source_target_pairs={{0,24},{8,16},{16,8},{24,0},{1,25},{9,17},{17,9},{25,1},{2,26},{10... | collective-permute-start | bytes 663560 | tf_op jit(solution)/shard_map/ppermute | solution.py:38
  197.6 28.0 %collective-permute-start.63 = (bf16[1,1152,512]{2,1,0:T(8,128)(2,1)S(1)}, bf16[1,1152,512]{2,1,0:T(8,128)(2,1)S(1)}, u32[]{:S(2)}, u32[]{:S(2)}) collective-permute-start(bf16[1,1152,512]{2,1,0:T(8,128)(2,1)S(1)} %get-tuple-element.218), channel_id=1, source_target_pairs={{0,16},{8,24},{16,0},{24,8},{1,17},{9,25},{17,1},{25,9},{2,18},{10... | collective-permute-start | bytes 3538952 | tf_op jit(solution)/shard_map/ppermute | solution.py:38
  235.7 29.5 %collective-permute-start.72 = (bf16[1,1152,512]{2,1,0:T(8,128)(2,1)S(1)}, bf16[1,1152,512]{2,1,0:T(8,128)(2,1)S(1)}, u32[]{:S(2)}, u32[]{:S(2)}) collective-permute-start(bf16[1,1152,512]{2,1,0:T(8,128)(2,1)S(1)} %get-tuple-element.216), channel_id=1, source_target_pairs={{0,16},{8,24},{16,0},{24,8},{1,17},{9,25},{17,1},{25,9},{2,18},{10... | collective-permute-start | bytes 3538952 | tf_op jit(solution)/shard_map/ppermute | solution.py:38
  236.8 28.5 %collective-permute-start.71 = (bf16[1,576,512]{2,1,0:T(8,128)(2,1)S(1)}, bf16[1,576,512]{2,1,0:T(8,128)(2,1)S(1)}, u32[]{:S(2)}, u32[]{:S(2)}) collective-permute-start(bf16[1,576,512]{2,1,0:T(8,128)(2,1)S(1)} %get-tuple-element.229), channel_id=1, source_target_pairs={{0,1},{1,0},{2,3},{3,2},{4,5},{5,4},{6,7},{7,6},{8,9},{9,8},{10,11... | collective-permute-start | bytes 1769480 | tf_op jit(solution)/shard_map/ppermute | solution.py:38
  240.7 5.4 %collective-permute-start.69 = (f32[3,512]{1,0:T(4,128)S(1)}, f32[3,512]{1,0:T(4,128)S(1)}, u32[]{:S(2)}, u32[]{:S(2)}) collective-permute-start(f32[3,512]{1,0:T(4,128)S(1)} %add_add_fusion.1), channel_id=1, source_target_pairs={{0,6},{1,7},{2,4},{3,5},{4,2},{5,3},{6,0},{7,1},{8,14},{9,15},{10,... | collective-permute-start | bytes 18440 | tf_op jit(solution)/shard_map/ppermute | solution.py:54
  266.5 15.0 %collective-permute-start.79 = (bf16[2,1152,512]{2,1,0:T(8,128)(2,1)}, bf16[2,1152,512]{2,1,0:T(8,128)(2,1)}, u32[]{:S(2)}, u32[]{:S(2)}) collective-permute-start(bf16[2,1152,512]{2,1,0:T(8,128)(2,1)} %get-tuple-element.161), channel_id=1, source_target_pairs={{0,8},{8,0},{16,24},{24,16},{1,9},{9,1},{17,25},{25,17},{2,10},{10... | collective-permute-start | bytes 7077896 | tf_op jit(solution)/shard_map/ppermute | solution.py:38
  266.6 5.7 %collective-permute-start.73 = (f32[2,512]{1,0:T(2,128)S(1)}, f32[2,512]{1,0:T(2,128)S(1)}, u32[]{:S(2)}, u32[]{:S(2)}) collective-permute-start(f32[2,512]{1,0:T(2,128)S(1)} %get-tuple-element.156), channel_id=1, source_target_pairs={{0,1},{1,0},{2,3},{3,2},{4,5},{5,4},{6,7},{7,6},{8,9},{9,8},{10,11... | collective-permute-start | bytes 12296 | tf_op jit(solution)/shard_map/ppermute | solution.py:54
  269.4 9.5 %collective-permute-start.76 = (bf16[1,288,512]{2,1,0:T(8,128)(2,1)S(1)}, bf16[1,288,512]{2,1,0:T(8,128)(2,1)S(1)}, u32[]{:S(2)}, u32[]{:S(2)}) collective-permute-start(bf16[1,288,512]{2,1,0:T(8,128)(2,1)S(1)} %add_convert_fusion.27), channel_id=1, source_target_pairs={{0,2},{1,3},{2,0},{3,1},{4,6},{5,7},{6,4},{7,5},{8,10},{9,11},{10,... | collective-permute-start | bytes 884744 | tf_op jit(solution)/shard_map/ppermute | solution.py:38
  272.4 8.0 %collective-permute-start.77 = (f32[2,512]{1,0:T(2,128)S(1)}, f32[2,512]{1,0:T(2,128)S(1)}, u32[]{:S(2)}, u32[]{:S(2)}) collective-permute-start(f32[2,512]{1,0:T(2,128)S(1)} %add_add_fusion.5), channel_id=1, source_target_pairs={{0,4},{1,5},{2,6},{3,7},{4,0},{5,1},{6,2},{7,3},{8,12},{9,13},{10,... | collective-permute-start | bytes 12296 | tf_op jit(solution)/shard_map/ppermute | solution.py:54
  274.8 5.6 %collective-permute-start.78 = (f32[2,512]{1,0:T(2,128)S(1)}, f32[2,512]{1,0:T(2,128)S(1)}, u32[]{:S(2)}, u32[]{:S(2)}) collective-permute-start(f32[2,512]{1,0:T(2,128)S(1)} %add_add_fusion.5), channel_id=1, source_target_pairs={{0,6},{1,7},{2,4},{3,5},{4,2},{5,3},{6,0},{7,1},{8,14},{9,15},{10,... | collective-permute-start | bytes 12296 | tf_op jit(solution)/shard_map/ppermute | solution.py:54
  285.4 26.6 %collective-permute-start.81 = (bf16[2,576,512]{2,1,0:T(8,128)(2,1)S(1)}, bf16[2,576,512]{2,1,0:T(8,128)(2,1)}, u32[]{:S(2)}, u32[]{:S(2)}) collective-permute-start(bf16[2,576,512]{2,1,0:T(8,128)(2,1)S(1)} %get-tuple-element.214), channel_id=1, source_target_pairs={{0,1},{1,0},{2,3},{3,2},{4,5},{5,4},{6,7},{7,6},{8,9},{9,8},{10,11... | collective-permute-start | bytes 3538952 | tf_op jit(solution)/shard_map/ppermute | solution.py:38
  286.0 17.2 %collective-permute-start.82 = (bf16[1,576,512]{2,1,0:T(8,128)(2,1)S(1)}, bf16[1,576,512]{2,1,0:T(8,128)(2,1)S(1)}, u32[]{:S(2)}, u32[]{:S(2)}) collective-permute-start(bf16[1,576,512]{2,1,0:T(8,128)(2,1)S(1)} %get-tuple-element.227), channel_id=1, source_target_pairs={{0,2},{1,3},{2,0},{3,1},{4,6},{5,7},{6,4},{7,5},{8,10},{9,11},{10,... | collective-permute-start | bytes 1769480 | tf_op jit(solution)/shard_map/ppermute | solution.py:38
  293.6 15.4 %collective-permute-start.80 = (bf16[2,864,128]{2,1,0:T(8,128)(2,1)S(1)}, bf16[2,864,128]{2,1,0:T(8,128)(2,1)S(1)}, u32[]{:S(2)}, u32[]{:S(2)}) collective-permute-start(bf16[2,864,128]{2,1,0:T(8,128)(2,1)S(1)} %get-tuple-element.233), channel_id=1, source_target_pairs={{0,16},{8,24},{16,0},{24,8},{1,17},{9,25},{17,1},{25,9},{2,18},{10... | collective-permute-start | bytes 1327112 | tf_op jit(solution)/shard_map/ppermute | solution.py:38
  294.6 14.4 %collective-permute-start.83 = (bf16[1,288,512]{2,1,0:T(8,128)(2,1)S(1)}, bf16[1,288,512]{2,1,0:T(8,128)(2,1)S(1)}, u32[]{:S(2)}, u32[]{:S(2)}) collective-permute-start(bf16[1,288,512]{2,1,0:T(8,128)(2,1)S(1)} %add_convert_fusion.25), channel_id=1, source_target_pairs={{0,4},{1,5},{2,6},{3,7},{4,0},{5,1},{6,2},{7,3},{8,12},{9,13},{10,... | collective-permute-start | bytes 884744 | tf_op jit(solution)/shard_map/ppermute | solution.py:38
  312.0 6.9 %collective-permute-start.84 = (bf16[2,640,512]{2,1,0:T(8,128)(2,1)}, bf16[2,640,512]{2,1,0:T(8,128)(2,1)}, u32[]{:S(2)}, u32[]{:S(2)}) collective-permute-start(bf16[2,640,512]{2,1,0:T(8,128)(2,1)} %get-tuple-element.174), channel_id=1, source_target_pairs={{0,8},{8,0},{16,24},{24,16},{1,9},{9,1},{17,25},{25,17},{2,10},{10... | collective-permute-start | bytes 3932168 | tf_op jit(solution)/shard_map/ppermute | solution.py:38
  312.1 16.0 %collective-permute-start.87 = (bf16[2,864,128]{2,1,0:T(8,128)(2,1)}, bf16[2,864,128]{2,1,0:T(8,128)(2,1)S(1)}, u32[]{:S(2)}, u32[]{:S(2)}) collective-permute-start(bf16[2,864,128]{2,1,0:T(8,128)(2,1)} %get-tuple-element.231), channel_id=1, source_target_pairs={{0,8},{8,0},{16,24},{24,16},{1,9},{9,1},{17,25},{25,17},{2,10},{10... | collective-permute-start | bytes 1327112 | tf_op jit(solution)/shard_map/ppermute | solution.py:38
  312.6 15.5 %collective-permute-start.88 = (bf16[2,864,128]{2,1,0:T(8,128)(2,1)}, bf16[2,864,128]{2,1,0:T(8,128)(2,1)S(1)}, u32[]{:S(2)}, u32[]{:S(2)}) collective-permute-start(bf16[2,864,128]{2,1,0:T(8,128)(2,1)} %get-tuple-element.230), channel_id=1, source_target_pairs={{0,24},{8,16},{16,8},{24,0},{1,25},{9,17},{17,9},{25,1},{2,26},{10... | collective-permute-start | bytes 1327112 | tf_op jit(solution)/shard_map/ppermute | solution.py:38
  318.2 15.8 %collective-permute-start.86 = (bf16[1,288,512]{2,1,0:T(8,128)(2,1)}, bf16[1,288,512]{2,1,0:T(8,128)(2,1)}, u32[]{:S(2)}, u32[]{:S(2)}) collective-permute-start(bf16[1,288,512]{2,1,0:T(8,128)(2,1)} %add_convert_fusion.22), channel_id=1, source_target_pairs={{0,1},{1,0},{2,3},{3,2},{4,5},{5,4},{6,7},{7,6},{8,9},{9,8},{10,11... | collective-permute-start | bytes 884744 | tf_op jit(solution)/shard_map/ppermute | solution.py:38
  321.6 20.2 %collective-permute-start.85 = (bf16[2,320,512]{2,1,0:T(8,128)(2,1)}, bf16[2,320,512]{2,1,0:T(8,128)(2,1)S(1)}, u32[]{:S(2)}, u32[]{:S(2)}) collective-permute-start(bf16[2,320,512]{2,1,0:T(8,128)(2,1)} %get-tuple-element.223), channel_id=1, source_target_pairs={{0,1},{1,0},{2,3},{3,2},{4,5},{5,4},{6,7},{7,6},{8,9},{9,8},{10,11... | collective-permute-start | bytes 1966088 | tf_op jit(solution)/shard_map/ppermute | solution.py:38
  327.0 23.7 %collective-permute-start.93 = (bf16[1,576,512]{2,1,0:T(8,128)(2,1)}, bf16[1,576,512]{2,1,0:T(8,128)(2,1)S(1)}, u32[]{:S(2)}, u32[]{:S(2)}) collective-permute-start(bf16[1,576,512]{2,1,0:T(8,128)(2,1)} %get-tuple-element.225), channel_id=1, source_target_pairs={{0,16},{8,24},{16,0},{24,8},{1,17},{9,25},{17,1},{25,9},{2,18},{10... | collective-permute-start | bytes 1769480 | tf_op jit(solution)/shard_map/ppermute | solution.py:38
  342.0 17.2 %collective-permute-start.92 = (bf16[2,160,512]{2,1,0:T(8,128)(2,1)S(1)}, bf16[2,160,512]{2,1,0:T(8,128)(2,1)S(1)}, u32[]{:S(2)}, u32[]{:S(2)}) collective-permute-start(bf16[2,160,512]{2,1,0:T(8,128)(2,1)S(1)} %get-tuple-element.239), channel_id=1, source_target_pairs={{0,2},{1,3},{2,0},{3,1},{4,6},{5,7},{6,4},{7,5},{8,10},{9,11},{10,... | collective-permute-start | bytes 983048 | tf_op jit(solution)/shard_map/ppermute | solution.py:38
  343.4 22.2 %collective-permute-start.91 = (bf16[1,288,512]{2,1,0:T(8,128)(2,1)S(1)}, bf16[1,288,512]{2,1,0:T(8,128)(2,1)S(1)}, u32[]{:S(2)}, u32[]{:S(2)}) collective-permute-start(bf16[1,288,512]{2,1,0:T(8,128)(2,1)S(1)} %add_convert_fusion.24), channel_id=1, source_target_pairs={{0,2},{1,3},{2,0},{3,1},{4,6},{5,7},{6,4},{7,5},{8,10},{9,11},{10,... | collective-permute-start | bytes 884744 | tf_op jit(solution)/shard_map/ppermute | solution.py:38
  344.9 22.7 %collective-permute-start.90 = (bf16[1,288,512]{2,1,0:T(8,128)(2,1)S(1)}, bf16[1,288,512]{2,1,0:T(8,128)(2,1)S(1)}, u32[]{:S(2)}, u32[]{:S(2)}) collective-permute-start(bf16[1,288,512]{2,1,0:T(8,128)(2,1)S(1)} %add_convert_fusion.21), channel_id=1, source_target_pairs={{0,4},{1,5},{2,6},{3,7},{4,0},{5,1},{6,2},{7,3},{8,12},{9,13},{10,... | collective-permute-start | bytes 884744 | tf_op jit(solution)/shard_map/ppermute | solution.py:38
  345.7 22.6 %collective-permute-start.94 = (bf16[2,64,320]{2,1,0:T(8,128)(2,1)S(1)}, bf16[2,64,320]{2,1,0:T(8,128)(2,1)S(1)}, u32[]{:S(2)}, u32[]{:S(2)}) collective-permute-start(bf16[2,64,320]{2,1,0:T(8,128)(2,1)S(1)} %get-tuple-element.179), channel_id=1, source_target_pairs={{0,1},{1,2},{2,3},{3,4},{4,5},{5,6},{6,7},{8,9},{9,10},{10,11},{11... | collective-permute-start | bytes 245768 | tf_op jit(solution)/shard_map/ppermute | solution.py:48
  350.7 40.9 %collective-permute-start.89 = (bf16[2,80,128]{2,1,0:T(8,128)(2,1)S(1)}, bf16[2,80,128]{2,1,0:T(8,128)(2,1)S(1)}, u32[]{:S(2)}, u32[]{:S(2)}) collective-permute-start(bf16[2,80,128]{2,1,0:T(8,128)(2,1)S(1)} %get-tuple-element.184), channel_id=1, source_target_pairs={{0,1},{1,2},{2,3},{3,4},{4,5},{5,6},{6,7},{8,9},{9,10},{10,11},{11... | collective-permute-start | bytes 122888 | tf_op jit(solution)/shard_map/ppermute | solution.py:48
  359.2 11.8 %collective-permute-start.98 = (bf16[1,288,512]{2,1,0:T(8,128)(2,1)S(1)}, bf16[1,288,512]{2,1,0:T(8,128)(2,1)S(1)}, u32[]{:S(2)}, u32[]{:S(2)}) collective-permute-start(bf16[1,288,512]{2,1,0:T(8,128)(2,1)S(1)} %add_convert_fusion.20), channel_id=1, source_target_pairs={{0,2},{1,3},{2,0},{3,1},{4,6},{5,7},{6,4},{7,5},{8,10},{9,11},{10,... | collective-permute-start | bytes 884744 | tf_op jit(solution)/shard_map/ppermute | solution.py:38
  367.6 37.6 %collective-permute-start.105 = (bf16[1,576,512]{2,1,0:T(8,128)(2,1)}, bf16[1,576,512]{2,1,0:T(8,128)(2,1)S(1)}, u32[]{:S(2)}, u32[]{:S(2)}) collective-permute-start(bf16[1,576,512]{2,1,0:T(8,128)(2,1)} %maximum_select_fusion), channel_id=1, source_target_pairs={{0,1},{1,0},{2,3},{3,2},{4,5},{5,4},{6,7},{7,6},{8,9},{9,8},{10,11... | collective-permute-start | bytes 1769480 | tf_op jit(solution)/shard_map/ppermute | solution.py:38
  368.4 18.2 %collective-permute-start.97 = (bf16[1,288,512]{2,1,0:T(8,128)(2,1)S(1)}, bf16[1,288,512]{2,1,0:T(8,128)(2,1)S(1)}, u32[]{:S(2)}, u32[]{:S(2)}) collective-permute-start(bf16[1,288,512]{2,1,0:T(8,128)(2,1)S(1)} %add_convert_fusion.19), channel_id=1, source_target_pairs={{0,1},{1,0},{2,3},{3,2},{4,5},{5,4},{6,7},{7,6},{8,9},{9,8},{10,11... | collective-permute-start | bytes 884744 | tf_op jit(solution)/shard_map/ppermute | solution.py:38
  370.9 16.7 %collective-permute-start.96 = (bf16[1,160,512]{2,1,0:T(8,128)(2,1)S(1)}, bf16[1,160,512]{2,1,0:T(8,128)(2,1)S(1)}, u32[]{:S(2)}, u32[]{:S(2)}) collective-permute-start(bf16[1,160,512]{2,1,0:T(8,128)(2,1)S(1)} %add_convert_fusion.29), channel_id=1, source_target_pairs={{0,4},{1,5},{2,6},{3,7},{4,0},{5,1},{6,2},{7,3},{8,12},{9,13},{10,... | collective-permute-start | bytes 491528 | tf_op jit(solution)/shard_map/ppermute | solution.py:38
  371.1 19.4 %collective-permute-start.100 = (bf16[1,288,512]{2,1,0:T(8,128)(2,1)S(1)}, bf16[1,288,512]{2,1,0:T(8,128)(2,1)S(1)}, u32[]{:S(2)}, u32[]{:S(2)}) collective-permute-start(bf16[1,288,512]{2,1,0:T(8,128)(2,1)S(1)} %add_convert_fusion.17), channel_id=1, source_target_pairs={{0,4},{1,5},{2,6},{3,7},{4,0},{5,1},{6,2},{7,3},{8,12},{9,13},{10,... | collective-permute-start | bytes 884744 | tf_op jit(solution)/shard_map/ppermute | solution.py:38
  387.7 8.0 %collective-permute-start.99 = (bf16[1,160,512]{2,1,0:T(8,128)(2,1)S(1)}, bf16[1,160,512]{2,1,0:T(8,128)(2,1)S(1)}, u32[]{:S(2)}, u32[]{:S(2)}) collective-permute-start(bf16[1,160,512]{2,1,0:T(8,128)(2,1)S(1)} %add_convert_fusion.28), channel_id=1, source_target_pairs={{0,2},{1,3},{2,0},{3,1},{4,6},{5,7},{6,4},{7,5},{8,10},{9,11},{10,... | collective-permute-start | bytes 491528 | tf_op jit(solution)/shard_map/ppermute | solution.py:38
  390.6 10.6 %collective-permute-start.102 = (bf16[1,288,512]{2,1,0:T(8,128)(2,1)S(1)}, bf16[1,288,512]{2,1,0:T(8,128)(2,1)S(1)}, u32[]{:S(2)}, u32[]{:S(2)}) collective-permute-start(bf16[1,288,512]{2,1,0:T(8,128)(2,1)S(1)} %add_convert_fusion.16), channel_id=1, source_target_pairs={{0,2},{1,3},{2,0},{3,1},{4,6},{5,7},{6,4},{7,5},{8,10},{9,11},{10,... | collective-permute-start | bytes 884744 | tf_op jit(solution)/shard_map/ppermute | solution.py:38
  393.6 30.0 %collective-permute-start.104 = (bf16[1,576,512]{2,1,0:T(8,128)(2,1)}, bf16[1,576,512]{2,1,0:T(8,128)(2,1)S(1)}, u32[]{:S(2)}, u32[]{:S(2)}) collective-permute-start(bf16[1,576,512]{2,1,0:T(8,128)(2,1)} %maximum_select_fusion.1), channel_id=1, source_target_pairs={{0,2},{1,3},{2,0},{3,1},{4,6},{5,7},{6,4},{7,5},{8,10},{9,11},{10,... | collective-permute-start | bytes 1769480 | tf_op jit(solution)/shard_map/ppermute | solution.py:38
  401.4 22.2 %collective-permute-start.103 = (bf16[1,576,512]{2,1,0:T(8,128)(2,1)S(1)}, bf16[1,576,512]{2,1,0:T(8,128)(2,1)S(1)}, u32[]{:S(2)}, u32[]{:S(2)}) collective-permute-start(bf16[1,576,512]{2,1,0:T(8,128)(2,1)S(1)} %maximum_select_fusion.2), channel_id=1, source_target_pairs={{0,1},{1,0},{2,3},{3,2},{4,5},{5,4},{6,7},{7,6},{8,9},{9,8},{10,11... | collective-permute-start | bytes 1769480 | tf_op jit(solution)/shard_map/ppermute | solution.py:38
  403.5 18.4 %collective-permute-start.101 = (bf16[1,320,512]{2,1,0:T(8,128)(2,1)S(1)}, bf16[1,320,512]{2,1,0:T(8,128)(2,1)S(1)}, u32[]{:S(2)}, u32[]{:S(2)}) collective-permute-start(bf16[1,320,512]{2,1,0:T(8,128)(2,1)S(1)} %maximum_select_fusion.7), channel_id=1, source_target_pairs={{0,1},{1,0},{2,3},{3,2},{4,5},{5,4},{6,7},{7,6},{8,9},{9,8},{10,11... | collective-permute-start | bytes 983048 | tf_op jit(solution)/shard_map/ppermute | solution.py:38
  (93 other events, 722.3 us)

commit v3 on v2

--- a/solution.py
+++ b/solution.py
@@ -92,9 +92,9 @@
             both = exchanged(value, pair[0][0] ^ pair[1][0], pair[0][1] ^ pair[1][1], plan)
         done = []
         if i == 0:
-            done = [job(one) for job in early]
+            done = [job(one, [two, both] if len(pair) == 2 else []) for job in early]
         elif i == 2:
-            done = [job(start) for job in late]
+            done = [job(one if takes == "one" else start) for takes, job in late]
         done = [token for token in jax.tree.leaves(done) if token is not None]
         if done:
             one = tied(one, *done)
@@ -945,7 +945,7 @@
         return lambda value: mid_shards.append(gathered(layer, plan, (value,)))
 
     mid_second = tied(conv_mid_w[1], stats)
-    stats = micro_sums(stats, plan, (), [second_hop(mid_first)])
+    stats = micro_sums(stats, plan, (), [("start", second_hop(mid_first))])
     mid_third = tied(conv_mid_w[2], stats)
     stat0, statp = stats[0:2], stats[2:4]
 
@@ -970,11 +970,11 @@
 
     z2, stat1, a_first = mid_forward((0,), (z0,), (stat0,), mid_shards[0], "mid_forward_a")
     og_parts = swapped(tied(grad_spread, stat1), plan)
-    stat1 = micro_sums(stat1, plan, (), [second_hop(mid_second)])
+    stat1 = micro_sums(stat1, plan, (), [("start", second_hop(mid_second))])
     z3, stat3, a_second, h1 = mid_forward(
         (1, 2), (z2, zp), (stat1, statp), mid_shards[1], "mid_forward_b"
     )
-    stat3 = micro_sums(stat3, plan, (), [second_hop(mid_third)])
+    stat3 = micro_sums(stat3, plan, (), [("start", second_hop(mid_third))])
     z4, stat4, a_third = mid_forward((3,), (z3,), (stat3,), mid_shards[2], "mid_forward_c")
     stat4 = micro_sums(tied(stat4, *og_parts[1:]), plan)
 
@@ -1021,9 +1021,9 @@
     sums_of = {}
 
     def weigh(key, a, ga, order, behind=()):
-        def job(value):
+        def job(value, far):
             keep, send = mid_weight(tied(a, value), ga, "mid_weight_" + key)
-            others = [part for other in behind for part in sums_of[other].received]
+            others = far + [part for other in behind for part in sums_of[other].received]
             if others:
                 send = tied(send, *others)
             sums_of[key] = WeightSum(keep, send, plan, order)
@@ -1037,14 +1037,14 @@
     back3 = micro_sums(
         tied(back3, *block_parts[1:]), plan,
         [weigh("c", a_third, ga_third, ["c", (0,), (1,), (2,)])],
-        [step("c")],
+        [("one", step("c"))],
     )
     ga_second, gh1, back12 = mid_backward(
         3, "join", g3, z3, stat3, back3, mid_shards[1], (z2, zp, stat1, statp, gh2), [],
         "mid_backward_b",
     )
     back12 = micro_sums(
-        back12, plan, [weigh("b", a_second, ga_second, ["c", (1,), (0,), (2,)], "c")], [step("b")]
+        back12, plan, [weigh("b", a_second, ga_second, ["c", (1,), (0,), (2,)], "c")], [("one", step("b"))]
     )
     ga_first, g1, back0, gzp = mid_backward(
         1, "entry", gh1, z2, stat1, back12, mid_shards[0], (z0, stat0, zp, statp),
@@ -1053,7 +1053,7 @@
     back0 = micro_sums(
         back0, plan,
         [weigh("a", a_first, ga_first, [(0,), "c", (1,), (2,)], "cb")],
-        [step("c")],
+        [("one", step("c"))],
     )
     (gm,) = call(
         functools.partial(entry_norm_kernel, plan),
@@ -1087,7 +1087,7 @@
     send = tied(
         send, gx_parts[chans // 2], *[part for key in "abc" for part in sums_of[key].received]
     )
-    sums_of["e"] = WeightSum(keep, send, plan, [(0,), (1,), "c", (2,)])
+    sums_of["e"] = WeightSum(keep, send, plan, [(1,), (0,), "c", (2,)])
 
     def chain(last, keys):
         for key in keys:

time: 433 us -> 422 us (0.975)
  waiting for transfers between devices: 145 us -> 130 us
    ppermute x55, waiting for transfers between devices: 108 us -> 94.4 us  [flipped(): return lax.ppermute(value, axis, [(i, i ^ bit) for i in range(count)])]
  transfers between devices with their start and end apart: 107 -> 107, of which waited for: 50 -> 46; matrix products, arithmetic and copies ran while one was open for 9% -> 9% of each run, Pallas kernels for 22% -> 24%
where the time goes in v3:
time: 422 us; the launch traced here: 416 us
  waiting for transfers between devices  130 us (31%)
  starting transfers between devices  116 us (27%)
  Pallas kernels  104 us (25%)
  other arithmetic  37.1 us (9%)
  local copies, waits for them, and re-layouts  26.1 us (6%)
    pallas_call x20, Pallas kernels, call(): pl.pallas_call(kernel, out_shape=shapes, in_specs=specs, out_specs=out_sp...  104 us
    ppermute x55, waiting for transfers between devices, flipped(): return lax.ppermute(value, axis, [(i, i ^ bit) for i in range(count)])  94.4 us
    ppermute x48, starting transfers between devices, exchanged(): lax.ppermute(value, ('chan', 'space'), [(i, i ^ flip) for i in range(coun...  62.8 us
    ppermute x55, starting transfers between devices, flipped(): return lax.ppermute(value, axis, [(i, i ^ bit) for i in range(count)])  45.1 us
    ppermute x48, waiting for transfers between devices, exchanged(): lax.ppermute(value, ('chan', 'space'), [(i, i ^ flip) for i in range(coun...  35.3 us
    convert_element_type x20, other arithmetic, added(): return total.astype(LOW)  27.3 us
    unnamed x98, local copies, waits for them, and re-layouts  13.7 us
  transfers between devices with their start and end apart: 107, of which 46 were waited for; matrix products, arithmetic and copies ran while one was open for 9% of the time, Pallas kernels for 24%

profile of v3, /device:TPU:0, one launch (start us, length us, event | category | flops | bytes accessed | tf_op | source)
XLA Modules:
  0.0 416.2 jit_solution(14904651243230649883)
XLA Ops:
  7.3 2.6 collective-permute-start.8
  11.0 3.5 slice_bitcast_fusion
  14.6 2.8 spread_features.1
  21.2 13.8 %collective-permute-done.5.refs_2_ = bf16[2,864,128]{2,1,0:T(8,128)(2,1)} collective-permute-done((bf16[2,864,128]{2,1,0:T(8,128)(2,1)}, bf16[2,864,128]{2,1,0:T(8,128)(2,1)}, u32[]{:S(2)}, u32[]{:S(2)}) %collective-permute-start.5) | collective-permute-done | bytes 442400 | tf_op jit(solution)/shard_map/ppermute | solution.py:38
  35.0 1.9 collective-permute-start.1
  37.0 7.2 %collective-permute-done.6.refs_3_ = bf16[2,864,128]{2,1,0:T(8,128)(2,1)} collective-permute-done((bf16[2,864,128]{2,1,0:T(8,128)(2,1)}, bf16[2,864,128]{2,1,0:T(8,128)(2,1)}, u32[]{:S(2)}, u32[]{:S(2)}) %collective-permute-start.6) | collective-permute-done | bytes 442400 | tf_op jit(solution)/shard_map/ppermute | solution.py:38
  53.0 6.4 %entry_forward.1 = (bf16[864,512]{1,0:T(8,128)(2,1)S(1)}, bf16[864,512]{1,0:T(8,128)(2,1)S(1)}, f32[4,512]{1,0:T(4,128)S(1)}, bf16[2,864,512]{2,1,0:T(8,128)(2,1)S(1)}) custom-call(f32[864,8]{1,0:T(8,128)S(1)} %convert_element_type.300.marks_ref, bf16[2,864,128]{2,1,0:T(8,128)(2,1)S(1)} %copy-done.24, bf16[2,864,128]{2,1,0:T(8,128)(2,1)} %collective-permute-done.4.refs_1_, ...), custom_call_target="tpu_custom_call" | custom-call | flops 2038431744 | bytes 7965696 | tf_op jit(solution)/shard_map/entry_forward/pallas_call | solution.py:817
  62.6 3.0 collective-permute-start.11
  68.7 4.0 collective-permute-done.17.refs_4_.refs_6_
  74.4 4.8 %collective-permute-start.14 = (f32[4,512]{1,0:T(4,128)S(1)}, f32[4,512]{1,0:T(4,128)S(1)}, u32[]{:S(2)}, u32[]{:S(2)}) collective-permute-start(f32[4,512]{1,0:T(4,128)S(1)} %add_add_fusion.3), channel_id=1, source_target_pairs={{0,4},{1,5},{2,6},{3,7},{4,0},{5,1},{6,2},{7,3},{8,12},{9,13},{10,... | collective-permute-start | bytes 24584 | tf_op jit(solution)/shard_map/ppermute | solution.py:54
  80.9 1.9 collective-permute-start.13
  86.0 7.4 %mid_forward_a.1 = (bf16[864,512]{1,0:T(8,128)(2,1)S(1)}, f32[2,512]{1,0:T(2,128)S(1)}, bf16[864,512]{1,0:T(8,128)(2,1)S(1)}) custom-call(s32[1]{0:T(128)} %bitcast.chan_ref, f32[1]{0:T(128)} %bitcast.2.inv_ref, f32[864,8]{1,0:T(8,128)S(1)} %convert_element_type.300.marks_ref, f32[10,512]{1,0:T(8,128)S(1)} %add.396.par_ref, bf16[864,512]{1,0:T(8,128)(2,1)S(1)} %copy-done.6, ...), custom_call_target="tpu_custom_call" | custom-call | flops 4076863488 | bytes 7429128 | tf_op jit(solution)/shard_map/mid_forward_a/pallas_call | solution.py:817
  98.0 3.2 collective-permute-done.26.refs_6_
  102.9 4.7 %collective-permute-start.23 = (f32[2,512]{1,0:T(2,128)S(1)}, f32[2,512]{1,0:T(2,128)S(1)}, u32[]{:S(2)}, u32[]{:S(2)}) collective-permute-start(f32[2,512]{1,0:T(2,128)S(1)} %add_add_fusion.15), channel_id=1, source_target_pairs={{0,4},{1,5},{2,6},{3,7},{4,0},{5,1},{6,2},{7,3},{8,12},{9,13},{10,... | collective-permute-start | bytes 12296 | tf_op jit(solution)/shard_map/ppermute | solution.py:54
  109.2 1.9 collective-permute-start.22
  111.1 1.9 collective-permute-done.24
  113.1 6.6 %mid_forward_b.1 = (bf16[864,512]{1,0:T(8,128)(2,1)S(1)}, f32[2,512]{1,0:T(2,128)S(1)}, bf16[864,512]{1,0:T(8,128)(2,1)S(1)}, bf16[864,512]{1,0:T(8,128)(2,1)S(1)}) custom-call(s32[1]{0:T(128)} %bitcast.chan_ref, f32[1]{0:T(128)} %bitcast.2.inv_ref, f32[864,8]{1,0:T(8,128)S(1)} %convert_element_type.300.marks_ref, f32[10,512]{1,0:T(8,128)S(1)} %add.396.par_ref, ...), custom_call_target="tpu_custom_call" | custom-call | flops 4076863488 | bytes 9202696 | tf_op jit(solution)/shard_map/mid_forward_b/pallas_call | solution.py:817
  124.3 5.2 %collective-permute-done.35.refs_4_.refs_6_ = bf16[3,3,128,512]{3,2,1,0:T(8,128)(2,1)S(1)} collective-permute-done((bf16[3,3,128,512]{3,2,1,0:T(8,128)(2,1)S(1)}, bf16[3,3,128,512]{3,2,1,0:T(8,128)(2,1)S(1)}, u32[]{:S(2)}, u32[]{:S(2)}) %collective-permute-start.35) | collective-permute-done | bytes 1179680 | tf_op jit(solution)/shard_map/ppermute | solution.py:38
  129.6 5.4 %collective-permute-start.32 = (f32[2,512]{1,0:T(2,128)S(1)}, f32[2,512]{1,0:T(2,128)S(1)}, u32[]{:S(2)}, u32[]{:S(2)}) collective-permute-start(f32[2,512]{1,0:T(2,128)S(1)} %add_add_fusion.13), channel_id=1, source_target_pairs={{0,4},{1,5},{2,6},{3,7},{4,0},{5,1},{6,2},{7,3},{8,12},{9,13},{10,... | collective-permute-start | bytes 12296 | tf_op jit(solution)/shard_map/ppermute | solution.py:54
  136.7 3.7 collective-permute-done.33
  141.5 6.4 %mid_forward_c.1 = (bf16[864,512]{1,0:T(8,128)(2,1)S(1)}, f32[2,512]{1,0:T(2,128)S(1)}, bf16[864,512]{1,0:T(8,128)(2,1)S(1)}) custom-call(s32[1]{0:T(128)} %bitcast.chan_ref, f32[1]{0:T(128)} %bitcast.2.inv_ref, f32[864,8]{1,0:T(8,128)S(1)} %convert_element_type.300.marks_ref, f32[10,512]{1,0:T(8,128)S(1)} %add.396.par_ref, ...), custom_call_target="tpu_custom_call" | custom-call | bytes 1 | tf_op jit(solution)/shard_map/mid_forward_c/pallas_call | solution.py:817
  159.2 2.3 collective-permute-done.45
  167.6 2.2 collective-permute-start.51
  173.5 7.3 %mid_backward_c.1 = (bf16[3,1056,512]{2,1,0:T(8,128)(2,1)S(1)}, bf16[864,512]{1,0:T(8,128)(2,1)S(1)}, f32[2,512]{1,0:T(2,128)S(1)}) custom-call(s32[1]{0:T(128)} %bitcast.chan_ref, f32[1]{0:T(128)} %bitcast.2.inv_ref, f32[864,8]{1,0:T(8,128)S(1)} %convert_element_type.300.marks_ref, f32[10,512]{1,0:T(8,128)S(1)} %add.396.par_ref, ...), custom_call_target="tpu_custom_call" | custom-call | bytes 1 | tf_op jit(solution)/shard_map/mid_backward_c/pallas_call | solution.py:817
  186.0 5.9 %mid_weight_c.1 = (bf16[2,1152,512]{2,1,0:T(8,128)(2,1)S(1)}, bf16[2,1152,512]{2,1,0:T(8,128)(2,1)S(1)}) custom-call(s32[1]{0:T(128)} %bitcast.chan_ref, bf16[864,512]{1,0:T(8,128)(2,1)S(1)} %get-tuple-element.137.a_ref, bf16[3,1056,512]{2,1,0:T(8,128)(2,1)S(1)} %get-tuple-element.138.ga_ref), custom_call_target="tpu_custom_call" | custom-call | flops 4076863488 | bytes 8847364 | tf_op jit(solution)/shard_map/mid_weight_c/pallas_call | solution.py:817
  193.9 2.2 collective-permute-done.58
  200.9 2.2 collective-permute-start.61
  203.9 2.4 collective-permute-done.61
  206.3 7.5 %mid_backward_b.1 = (bf16[3,1056,512]{2,1,0:T(8,128)(2,1)S(1)}, bf16[864,512]{1,0:T(8,128)(2,1)S(1)}, f32[3,512]{1,0:T(4,128)S(1)}) custom-call(s32[1]{0:T(128)} %bitcast.chan_ref, f32[1]{0:T(128)} %bitcast.2.inv_ref, f32[864,8]{1,0:T(8,128)S(1)} %convert_element_type.300.marks_ref, f32[10,512]{1,0:T(8,128)S(1)} %add.396.par_ref, ...), custom_call_target="tpu_custom_call" | custom-call | bytes 1 | tf_op jit(solution)/shard_map/mid_backward_b/pallas_call | solution.py:817
  215.8 7.2 %mid_weight_b.1 = (bf16[2,1152,512]{2,1,0:T(8,128)(2,1)S(1)}, bf16[2,1152,512]{2,1,0:T(8,128)(2,1)}) custom-call(s32[1]{0:T(128)} %bitcast.chan_ref, bf16[864,512]{1,0:T(8,128)(2,1)S(1)} %get-tuple-element.148.a_ref, bf16[3,1056,512]{2,1,0:T(8,128)(2,1)S(1)} %get-tuple-element.149.ga_ref), custom_call_target="tpu_custom_call" | custom-call | bytes 1 | tf_op jit(solution)/shard_map/mid_weight_b/pallas_call | solution.py:817
  223.0 3.6 collective-permute-done.65
  227.6 2.7 add_convert_fusion.12
  231.8 2.2 collective-permute-done.66
  234.1 4.2 %add_convert_fusion.2 = (bf16[1,1152,512]{2,1,0:T(8,128)(2,1)}, bf16[1,1152,512]{2,1,0:T(8,128)(2,1)S(1)}) fusion(bf16[2,1152,512]{2,1,0:T(8,128)(2,1)} %collective-permute-done.67, bf16[2,1152,512]{2,1,0:T(8,128)(2,1)} %copy-done.10), kind=kLoop, calls=%fused_computation.2 | loop fusion | flops 4718592 | bytes 7077888 | tf_op jit(solution)/shard_map/convert_element_type | solution.py:132
  242.2 1.9 collective-permute-start.69
  245.3 2.4 collective-permute-done.69
  247.7 9.0 %mid_backward_a.1 = (bf16[3,1056,512]{2,1,0:T(8,128)(2,1)S(1)}, bf16[864,512]{1,0:T(8,128)(2,1)S(1)}, f32[2,512]{1,0:T(2,128)S(1)}, bf16[864,512]{1,0:T(8,128)(2,1)S(1)}) custom-call(s32[1]{0:T(128)} %bitcast.chan_ref, f32[1]{0:T(128)} %bitcast.2.inv_ref, f32[864,8]{1,0:T(8,128)S(1)} %convert_element_type.300.marks_ref, f32[10,512]{1,0:T(8,128)S(1)} %add.396.par_ref, ...), custom_call_target="tpu_custom_call" | custom-call | bytes 1 | tf_op jit(solution)/shard_map/mid_backward_a/pallas_call | solution.py:817
  258.8 7.3 %mid_weight_a.1 = (bf16[2,1152,512]{2,1,0:T(8,128)(2,1)S(1)}, bf16[2,1152,512]{2,1,0:T(8,128)(2,1)}) custom-call(s32[1]{0:T(128)} %bitcast.chan_ref, bf16[864,512]{1,0:T(8,128)(2,1)S(1)} %copy-done.20, bf16[3,1056,512]{2,1,0:T(8,128)(2,1)S(1)} %get-tuple-element.161.ga_ref), custom_call_target="tpu_custom_call" | custom-call | bytes 1 | tf_op jit(solution)/shard_map/mid_weight_a/pallas_call | solution.py:817
  270.8 2.9 add_convert_fusion.10
  273.7 2.1 collective-permute-start.75
  276.4 1.9 collective-permute-start.78
  278.3 2.0 collective-permute-done.75
  283.5 3.4 add_convert_fusion
  287.9 6.4 %entry_backward.1 = bf16[4,2,864,128]{3,2,1,0:T(8,128)(2,1)S(1)} custom-call(f32[864,8]{1,0:T(8,128)S(1)} %convert_element_type.300.marks_ref, bf16[2,960,512]{2,1,0:T(8,128)(2,1)S(1)} %entry_norm.1.gm_ref, bf16[864,512]{1,0:T(8,128)(2,1)S(1)} %get-tuple-element.172.short_ref, bf16[10,64,512]{2,1,0:T(8,128)(2,1)S(1)} %pad_maximum_fusion.refs_4_.refs_0_, ...), custom_call_target="tpu_custom_call" | custom-call | bytes 1 | tf_op jit(solution)/shard_map/entry_backward/pallas_call | solution.py:817
  296.4 2.1 collective-permute-start.83
  298.6 6.1 %entry_weight.1 = (bf16[2,640,512]{2,1,0:T(8,128)(2,1)S(1)}, bf16[2,640,512]{2,1,0:T(8,128)(2,1)}) custom-call(bf16[2,864,512]{2,1,0:T(8,128)(2,1)S(1)} %copy-done.15, bf16[2,960,512]{2,1,0:T(8,128)(2,1)S(1)} %entry_norm.1.gm_ref, bf16[864,512]{1,0:T(8,128)(2,1)S(1)} %get-tuple-element.172.short_ref), custom_call_target="tpu_custom_call" | custom-call | bytes 1 | tf_op jit(solution)/shard_map/entry_weight/pallas_call | solution.py:817
  305.7 5.4 %collective-permute-done.83 = bf16[1,288,512]{2,1,0:T(8,128)(2,1)S(1)} collective-permute-done((bf16[1,288,512]{2,1,0:T(8,128)(2,1)S(1)}, bf16[1,288,512]{2,1,0:T(8,128)(2,1)S(1)}, u32[]{:S(2)}, u32[]{:S(2)}) %collective-permute-start.83) | collective-permute-done | bytes 294944 | tf_op jit(solution)/shard_map/ppermute | solution.py:38
  311.0 2.9 collective-permute-done.81
  316.4 3.0 add_convert_fusion.8
  320.9 2.7 add_convert_fusion.7
  325.4 2.8 collective-permute-done.106
  329.3 6.0 %join_features.1 = (f32[2,64,6720]{2,1,0:T(8,128)}, bf16[2,64,320]{2,1,0:T(8,128)(2,1)S(1)}) custom-call(s32[1]{0:T(128)} %bitcast.chan_ref, bf16[2,864,128]{2,1,0:T(8,128)(2,1)S(1)} %get-tuple-element.180.refs_0_, bf16[2,864,128]{2,1,0:T(8,128)(2,1)S(1)} %collective-permute-done.87.refs_1_, bf16[2,864,128]{2,1,0:T(8,128)(2,1)S(1)} %collective-permute-done.80.refs_2_, ...), custom_call_target="tpu_custom_call" | custom-call | bytes 5292036 | tf_op jit(solution)/shard_map/join_features/pallas_call | solution.py:817
  336.4 4.2 %collective-permute-done.85 = bf16[2,320,512]{2,1,0:T(8,128)(2,1)S(1)} collective-permute-done((bf16[2,320,512]{2,1,0:T(8,128)(2,1)}, bf16[2,320,512]{2,1,0:T(8,128)(2,1)S(1)}, u32[]{:S(2)}, u32[]{:S(2)}) %collective-permute-start.85) | collective-permute-done | bytes 655392 | tf_op jit(solution)/shard_map/ppermute | solution.py:38
  343.6 2.0 collective-permute-start.90
  345.6 2.8 collective-permute-start.94
  348.4 2.4 join_rows.1
  350.8 3.0 collective-permute-start.89
  355.0 3.7 collective-permute-done.91
  364.3 2.9 collective-permute-start.100
  367.2 12.4 %collective-permute-done.97 = bf16[1,288,512]{2,1,0:T(8,128)(2,1)S(1)} collective-permute-done((bf16[1,288,512]{2,1,0:T(8,128)(2,1)S(1)}, bf16[1,288,512]{2,1,0:T(8,128)(2,1)S(1)}, u32[]{:S(2)}, u32[]{:S(2)}) %collective-permute-start.97) | collective-permute-done | bytes 294944 | tf_op jit(solution)/shard_map/ppermute | solution.py:38
  386.0 2.1 collective-permute-start.104
  388.2 4.8 %collective-permute-done.102 = bf16[1,288,512]{2,1,0:T(8,128)(2,1)S(1)} collective-permute-done((bf16[1,288,512]{2,1,0:T(8,128)(2,1)S(1)}, bf16[1,288,512]{2,1,0:T(8,128)(2,1)S(1)}, u32[]{:S(2)}, u32[]{:S(2)}) %collective-permute-start.102) | collective-permute-done | bytes 294944 | tf_op jit(solution)/shard_map/ppermute | solution.py:38
  396.7 13.8 %collective-permute-done.101 = bf16[1,320,512]{2,1,0:T(8,128)(2,1)S(1)} collective-permute-done((bf16[1,320,512]{2,1,0:T(8,128)(2,1)S(1)}, bf16[1,320,512]{2,1,0:T(8,128)(2,1)S(1)}, u32[]{:S(2)}, u32[]{:S(2)}) %collective-permute-start.101) | collective-permute-done | bytes 327712 | tf_op jit(solution)/shard_map/ppermute | solution.py:38
  412.3 3.7 mid_assembly.1
  (367 shorter events, 134.9 us)
Async XLA Ops:
  1.4 19.2 %collective-permute-start = (f32[10,512]{1,0:T(8,128)S(1)}, f32[10,512]{1,0:T(8,128)S(1)}, u32[]{:S(2)}, u32[]{:S(2)}) collective-permute-start(f32[10,512]{1,0:T(8,128)S(1)} %constant_dynamic-update-slice_fusion.1), channel_id=1, source_target_pairs={{0,8},{8,0},{16,24},{24,16},{1,9},{9,1},{17,25},{25,17},{2,10},{10... | collective-permute-start | bytes 61448 | tf_op jit(solution)/shard_map/ppermute | solution.py:38
  2.7 11.9 %collective-permute-start.2 = (bf16[2,64,320]{2,1,0:T(8,128)(2,1)S(1)}, bf16[2,64,320]{2,1,0:T(8,128)(2,1)S(1)}, u32[]{:S(2)}, u32[]{:S(2)}) collective-permute-start(bf16[2,64,320]{2,1,0:T(8,128)(2,1)S(1)} %slice.182), channel_id=1, source_target_pairs={{1,0},{2,1},{3,2},{4,3},{5,4},{6,5},{7,6},{9,8},{10,9},{11,10},{12... | collective-permute-start | bytes 245768 | tf_op jit(solution)/shard_map/ppermute | solution.py:43
  4.8 9.8 %collective-permute-start.3 = (bf16[2,80,128]{2,1,0:T(8,128)(2,1)S(1)}, bf16[2,80,128]{2,1,0:T(8,128)(2,1)S(1)}, u32[]{:S(2)}, u32[]{:S(2)}) collective-permute-start(bf16[2,80,128]{2,1,0:T(8,128)(2,1)S(1)} %slice.233), channel_id=1, source_target_pairs={{1,0},{2,1},{3,2},{4,3},{5,4},{6,5},{7,6},{9,8},{10,9},{11,10},{12... | collective-permute-start | bytes 122888 | tf_op jit(solution)/shard_map/ppermute | solution.py:43
  7.3 42.0 %collective-permute-start.8 = (bf16[10,64,512]{2,1,0:T(8,128)(2,1)S(1)}, bf16[10,64,512]{2,1,0:T(8,128)(2,1)}, u32[]{:S(2)}, u32[]{:S(2)}) collective-permute-start(bf16[10,64,512]{2,1,0:T(8,128)(2,1)S(1)} %pad_maximum_fusion.refs_4_.refs_0_), channel_id=1, source_target_pairs={{0,16},{8,24},{16,0},{24,8},{1,17},{9,25},{17,1},{25,9},{2,18},{10... | collective-permute-start | bytes 1966088 | tf_op jit(solution)/shard_map/ppermute | solution.py:38
  18.7 27.2 %collective-permute-start.4 = (bf16[2,864,128]{2,1,0:T(8,128)(2,1)}, bf16[2,864,128]{2,1,0:T(8,128)(2,1)}, u32[]{:S(2)}, u32[]{:S(2)}) collective-permute-start(bf16[2,864,128]{2,1,0:T(8,128)(2,1)} %get-tuple-element.238), channel_id=1, source_target_pairs={{0,8},{8,0},{16,24},{24,16},{1,9},{9,1},{17,25},{25,17},{2,10},{10... | collective-permute-start | bytes 1327112 | tf_op jit(solution)/shard_map/ppermute | solution.py:38
  19.0 16.1 %collective-permute-start.5 = (bf16[2,864,128]{2,1,0:T(8,128)(2,1)}, bf16[2,864,128]{2,1,0:T(8,128)(2,1)}, u32[]{:S(2)}, u32[]{:S(2)}) collective-permute-start(bf16[2,864,128]{2,1,0:T(8,128)(2,1)} %get-tuple-element.237), channel_id=1, source_target_pairs={{0,16},{8,24},{16,0},{24,8},{1,17},{9,25},{17,1},{25,9},{2,18},{10... | collective-permute-start | bytes 1327112 | tf_op jit(solution)/shard_map/ppermute | solution.py:38
  19.3 24.9 %collective-permute-start.6 = (bf16[2,864,128]{2,1,0:T(8,128)(2,1)}, bf16[2,864,128]{2,1,0:T(8,128)(2,1)}, u32[]{:S(2)}, u32[]{:S(2)}) collective-permute-start(bf16[2,864,128]{2,1,0:T(8,128)(2,1)} %get-tuple-element.236), channel_id=1, source_target_pairs={{0,24},{8,16},{16,8},{24,0},{1,25},{9,17},{17,9},{25,1},{2,26},{10... | collective-permute-start | bytes 1327112 | tf_op jit(solution)/shard_map/ppermute | solution.py:38
  20.6 31.4 %collective-permute-start.7 = (bf16[10,64,512]{2,1,0:T(8,128)(2,1)S(1)}, bf16[10,64,512]{2,1,0:T(8,128)(2,1)}, u32[]{:S(2)}, u32[]{:S(2)}) collective-permute-start(bf16[10,64,512]{2,1,0:T(8,128)(2,1)S(1)} %pad_maximum_fusion.refs_4_.refs_0_), channel_id=1, source_target_pairs={{0,8},{8,0},{16,24},{24,16},{1,9},{9,1},{17,25},{25,17},{2,10},{10... | collective-permute-start | bytes 1966088 | tf_op jit(solution)/shard_map/ppermute | solution.py:38
  35.0 10.8 %collective-permute-start.1 = (f32[10,512]{1,0:T(8,128)S(1)}, f32[10,512]{1,0:T(8,128)S(1)}, u32[]{:S(2)}, u32[]{:S(2)}) collective-permute-start(f32[10,512]{1,0:T(8,128)S(1)} %constant_dynamic-update-slice_fusion), channel_id=1, source_target_pairs={{0,16},{8,24},{16,0},{24,8},{1,17},{9,25},{17,1},{25,9},{2,18},{10... | collective-permute-start | bytes 61448 | tf_op jit(solution)/shard_map/ppermute | solution.py:38
  44.1 28.5 %collective-permute-start.17 = (bf16[3,3,128,512]{3,2,1,0:T(8,128)(2,1)}, bf16[3,3,128,512]{3,2,1,0:T(8,128)(2,1)}, u32[]{:S(2)}, u32[]{:S(2)}) collective-permute-start(bf16[3,3,128,512]{3,2,1,0:T(8,128)(2,1)} %get-tuple-element.113.refs_2_.refs_4_), channel_id=1, source_target_pairs={{0,16},{8,24},{16,0},{24,8},{1,17},{9,25},{17,1},{25,9},{2,18},{10... | collective-permute-start | bytes 3538952 | tf_op jit(solution)/shard_map/ppermute | solution.py:38
  65.7 19.1 %collective-permute-start.16 = (bf16[3,3,128,512]{3,2,1,0:T(8,128)(2,1)}, bf16[3,3,128,512]{3,2,1,0:T(8,128)(2,1)}, u32[]{:S(2)}, u32[]{:S(2)}) collective-permute-start(bf16[3,3,128,512]{3,2,1,0:T(8,128)(2,1)} %get-tuple-element.113.refs_2_.refs_4_), channel_id=1, source_target_pairs={{0,8},{8,0},{16,24},{24,16},{1,9},{9,1},{17,25},{25,17},{2,10},{10... | collective-permute-start | bytes 3538952 | tf_op jit(solution)/shard_map/ppermute | solution.py:38
  72.7 12.1 %collective-permute-start.18 = (bf16[3,3,128,512]{3,2,1,0:T(8,128)(2,1)}, bf16[3,3,128,512]{3,2,1,0:T(8,128)(2,1)}, u32[]{:S(2)}, u32[]{:S(2)}) collective-permute-start(bf16[3,3,128,512]{3,2,1,0:T(8,128)(2,1)} %collective-permute-done.17.refs_4_.refs_6_), channel_id=1, source_target_pairs={{0,8},{8,0},{16,24},{24,16},{1,9},{9,1},{17,25},{25,17},{2,10},{10... | collective-permute-start | bytes 3538952 | tf_op jit(solution)/shard_map/ppermute | solution.py:38
  72.7 28.5 %collective-permute-start.26 = (bf16[3,3,128,512]{3,2,1,0:T(8,128)(2,1)S(1)}, bf16[3,3,128,512]{3,2,1,0:T(8,128)(2,1)}, u32[]{:S(2)}, u32[]{:S(2)}) collective-permute-start(bf16[3,3,128,512]{3,2,1,0:T(8,128)(2,1)S(1)} %get-tuple-element.118.refs_4_), channel_id=1, source_target_pairs={{0,16},{8,24},{16,0},{24,8},{1,17},{9,25},{17,1},{25,9},{2,18},{10... | collective-permute-start | bytes 3538952 | tf_op jit(solution)/shard_map/ppermute | solution.py:38
  74.4 6.5 %collective-permute-start.14 = (f32[4,512]{1,0:T(4,128)S(1)}, f32[4,512]{1,0:T(4,128)S(1)}, u32[]{:S(2)}, u32[]{:S(2)}) collective-permute-start(f32[4,512]{1,0:T(4,128)S(1)} %add_add_fusion.3), channel_id=1, source_target_pairs={{0,4},{1,5},{2,6},{3,7},{4,0},{5,1},{6,2},{7,3},{8,12},{9,13},{10,... | collective-permute-start | bytes 24584 | tf_op jit(solution)/shard_map/ppermute | solution.py:54
  95.6 17.4 %collective-permute-start.25 = (bf16[3,3,128,512]{3,2,1,0:T(8,128)(2,1)S(1)}, bf16[3,3,128,512]{3,2,1,0:T(8,128)(2,1)S(1)}, u32[]{:S(2)}, u32[]{:S(2)}) collective-permute-start(bf16[3,3,128,512]{3,2,1,0:T(8,128)(2,1)S(1)} %get-tuple-element.118.refs_4_), channel_id=1, source_target_pairs={{0,8},{8,0},{16,24},{24,16},{1,9},{9,1},{17,25},{25,17},{2,10},{10... | collective-permute-start | bytes 3538952 | tf_op jit(solution)/shard_map/ppermute | solution.py:38
  101.2 11.9 %collective-permute-start.27 = (bf16[3,3,128,512]{3,2,1,0:T(8,128)(2,1)}, bf16[3,3,128,512]{3,2,1,0:T(8,128)(2,1)S(1)}, u32[]{:S(2)}, u32[]{:S(2)}) collective-permute-start(bf16[3,3,128,512]{3,2,1,0:T(8,128)(2,1)} %collective-permute-done.26.refs_6_), channel_id=1, source_target_pairs={{0,8},{8,0},{16,24},{24,16},{1,9},{9,1},{17,25},{25,17},{2,10},{10... | collective-permute-start | bytes 3538952 | tf_op jit(solution)/shard_map/ppermute | solution.py:38
  101.2 28.4 %collective-permute-start.35 = (bf16[3,3,128,512]{3,2,1,0:T(8,128)(2,1)S(1)}, bf16[3,3,128,512]{3,2,1,0:T(8,128)(2,1)S(1)}, u32[]{:S(2)}, u32[]{:S(2)}) collective-permute-start(bf16[3,3,128,512]{3,2,1,0:T(8,128)(2,1)S(1)} %get-tuple-element.122.refs_2_.refs_4_), channel_id=1, source_target_pairs={{0,16},{8,24},{16,0},{24,8},{1,17},{9,25},{17,1},{25,9},{2,18},{10... | collective-permute-start | bytes 3538952 | tf_op jit(solution)/shard_map/ppermute | solution.py:38
  102.9 6.3 %collective-permute-start.23 = (f32[2,512]{1,0:T(2,128)S(1)}, f32[2,512]{1,0:T(2,128)S(1)}, u32[]{:S(2)}, u32[]{:S(2)}) collective-permute-start(f32[2,512]{1,0:T(2,128)S(1)} %add_add_fusion.15), channel_id=1, source_target_pairs={{0,4},{1,5},{2,6},{3,7},{4,0},{5,1},{6,2},{7,3},{8,12},{9,13},{10,... | collective-permute-start | bytes 12296 | tf_op jit(solution)/shard_map/ppermute | solution.py:54
  122.0 19.5 %collective-permute-start.34 = (bf16[3,3,128,512]{3,2,1,0:T(8,128)(2,1)S(1)}, bf16[3,3,128,512]{3,2,1,0:T(8,128)(2,1)S(1)}, u32[]{:S(2)}, u32[]{:S(2)}) collective-permute-start(bf16[3,3,128,512]{3,2,1,0:T(8,128)(2,1)S(1)} %get-tuple-element.122.refs_2_.refs_4_), channel_id=1, source_target_pairs={{0,8},{8,0},{16,24},{24,16},{1,9},{9,1},{17,25},{25,17},{2,10},{10... | collective-permute-start | bytes 3538952 | tf_op jit(solution)/shard_map/ppermute | solution.py:38
  129.6 11.9 %collective-permute-start.36 = (bf16[3,3,128,512]{3,2,1,0:T(8,128)(2,1)S(1)}, bf16[3,3,128,512]{3,2,1,0:T(8,128)(2,1)S(1)}, u32[]{:S(2)}, u32[]{:S(2)}) collective-permute-start(bf16[3,3,128,512]{3,2,1,0:T(8,128)(2,1)S(1)} %collective-permute-done.35.refs_4_.refs_6_), channel_id=1, source_target_pairs={{0,8},{8,0},{16,24},{24,16},{1,9},{9,1},{17,25},{25,17},{2,10},{10... | collective-permute-start | bytes 3538952 | tf_op jit(solution)/shard_map/ppermute | solution.py:38
  129.6 7.0 %collective-permute-start.32 = (f32[2,512]{1,0:T(2,128)S(1)}, f32[2,512]{1,0:T(2,128)S(1)}, u32[]{:S(2)}, u32[]{:S(2)}) collective-permute-start(f32[2,512]{1,0:T(2,128)S(1)} %add_add_fusion.13), channel_id=1, source_target_pairs={{0,4},{1,5},{2,6},{3,7},{4,0},{5,1},{6,2},{7,3},{8,12},{9,13},{10,... | collective-permute-start | bytes 12296 | tf_op jit(solution)/shard_map/ppermute | solution.py:54
  136.6 11.3 %collective-permute-start.37 = (bf16[864,128]{1,0:T(8,128)(2,1)S(1)}, bf16[864,128]{1,0:T(8,128)(2,1)S(1)}, u32[]{:S(2)}, u32[]{:S(2)}) collective-permute-start(bf16[864,128]{1,0:T(8,128)(2,1)S(1)} %get-tuple-element.249), channel_id=1, source_target_pairs={{0,8},{8,0},{16,24},{24,16},{1,9},{9,1},{17,25},{25,17},{2,10},{10... | collective-permute-start | bytes 663560 | tf_op jit(solution)/shard_map/ppermute | solution.py:38
  140.4 8.4 %collective-permute-start.38 = (bf16[864,128]{1,0:T(8,128)(2,1)S(1)}, bf16[864,128]{1,0:T(8,128)(2,1)S(1)}, u32[]{:S(2)}, u32[]{:S(2)}) collective-permute-start(bf16[864,128]{1,0:T(8,128)(2,1)S(1)} %get-tuple-element.248), channel_id=1, source_target_pairs={{0,16},{8,24},{16,0},{24,8},{1,17},{9,25},{17,1},{25,9},{2,18},{10... | collective-permute-start | bytes 663560 | tf_op jit(solution)/shard_map/ppermute | solution.py:38
  141.4 8.7 %collective-permute-start.39 = (bf16[864,128]{1,0:T(8,128)(2,1)S(1)}, bf16[864,128]{1,0:T(8,128)(2,1)S(1)}, u32[]{:S(2)}, u32[]{:S(2)}) collective-permute-start(bf16[864,128]{1,0:T(8,128)(2,1)S(1)} %get-tuple-element.247), channel_id=1, source_target_pairs={{0,24},{8,16},{16,8},{24,0},{1,25},{9,17},{17,9},{25,1},{2,26},{10... | collective-permute-start | bytes 663560 | tf_op jit(solution)/shard_map/ppermute | solution.py:38
  171.2 9.6 %collective-permute-start.52 = (bf16[864,128]{1,0:T(8,128)(2,1)S(1)}, bf16[864,128]{1,0:T(8,128)(2,1)S(1)}, u32[]{:S(2)}, u32[]{:S(2)}) collective-permute-start(bf16[864,128]{1,0:T(8,128)(2,1)S(1)} %get-tuple-element.244), channel_id=1, source_target_pairs={{0,8},{8,0},{16,24},{24,16},{1,9},{9,1},{17,25},{25,17},{2,10},{10... | collective-permute-start | bytes 663560 | tf_op jit(solution)/shard_map/ppermute | solution.py:38
  171.2 10.3 %collective-permute-start.53 = (bf16[864,128]{1,0:T(8,128)(2,1)S(1)}, bf16[864,128]{1,0:T(8,128)(2,1)S(1)}, u32[]{:S(2)}, u32[]{:S(2)}) collective-permute-start(bf16[864,128]{1,0:T(8,128)(2,1)S(1)} %get-tuple-element.243), channel_id=1, source_target_pairs={{0,16},{8,24},{16,0},{24,8},{1,17},{9,25},{17,1},{25,9},{2,18},{10... | collective-permute-start | bytes 663560 | tf_op jit(solution)/shard_map/ppermute | solution.py:38
  172.3 11.1 %collective-permute-start.54 = (bf16[864,128]{1,0:T(8,128)(2,1)S(1)}, bf16[864,128]{1,0:T(8,128)(2,1)S(1)}, u32[]{:S(2)}, u32[]{:S(2)}) collective-permute-start(bf16[864,128]{1,0:T(8,128)(2,1)S(1)} %get-tuple-element.242), channel_id=1, source_target_pairs={{0,24},{8,16},{16,8},{24,0},{1,25},{9,17},{17,9},{25,1},{2,26},{10... | collective-permute-start | bytes 663560 | tf_op jit(solution)/shard_map/ppermute | solution.py:38
  184.3 7.6 %collective-permute-start.56 = (f32[2,512]{1,0:T(2,128)S(1)}, f32[2,512]{1,0:T(2,128)S(1)}, u32[]{:S(2)}, u32[]{:S(2)}) collective-permute-start(f32[2,512]{1,0:T(2,128)S(1)} %get-tuple-element.135), channel_id=1, source_target_pairs={{0,1},{1,0},{2,3},{3,2},{4,5},{5,4},{6,7},{7,6},{8,9},{9,8},{10,11... | collective-permute-start | bytes 12296 | tf_op jit(solution)/shard_map/ppermute | solution.py:54
  198.3 28.2 %collective-permute-start.65 = (bf16[1,1152,512]{2,1,0:T(8,128)(2,1)S(1)}, bf16[1,1152,512]{2,1,0:T(8,128)(2,1)S(1)}, u32[]{:S(2)}, u32[]{:S(2)}) collective-permute-start(bf16[1,1152,512]{2,1,0:T(8,128)(2,1)S(1)} %get-tuple-element.220), channel_id=1, source_target_pairs={{0,16},{8,24},{16,0},{24,8},{1,17},{9,25},{17,1},{25,9},{2,18},{10... | collective-permute-start | bytes 3538952 | tf_op jit(solution)/shard_map/ppermute | solution.py:38
  213.9 9.1 %collective-permute-start.63 = (f32[3,512]{1,0:T(4,128)S(1)}, f32[3,512]{1,0:T(4,128)S(1)}, u32[]{:S(2)}, u32[]{:S(2)}) collective-permute-start(f32[3,512]{1,0:T(4,128)S(1)} %get-tuple-element.146), channel_id=1, source_target_pairs={{0,1},{1,0},{2,3},{3,2},{4,5},{5,4},{6,7},{7,6},{8,9},{9,8},{10,11... | collective-permute-start | bytes 18440 | tf_op jit(solution)/shard_map/ppermute | solution.py:54
  215.4 7.6 %collective-permute-start.64 = (f32[3,512]{1,0:T(4,128)S(1)}, f32[3,512]{1,0:T(4,128)S(1)}, u32[]{:S(2)}, u32[]{:S(2)}) collective-permute-start(f32[3,512]{1,0:T(4,128)S(1)} %get-tuple-element.146), channel_id=1, source_target_pairs={{0,9},{1,8},{2,11},{3,10},{4,13},{5,12},{6,15},{7,14},{8,1},{9,0},... | collective-permute-start | bytes 18440 | tf_op jit(solution)/shard_map/ppermute | solution.py:54
  227.6 6.5 %collective-permute-start.67 = (bf16[2,1152,512]{2,1,0:T(8,128)(2,1)}, bf16[2,1152,512]{2,1,0:T(8,128)(2,1)}, u32[]{:S(2)}, u32[]{:S(2)}) collective-permute-start(bf16[2,1152,512]{2,1,0:T(8,128)(2,1)} %get-tuple-element.151), channel_id=1, source_target_pairs={{0,8},{8,0},{16,24},{24,16},{1,9},{9,1},{17,25},{25,17},{2,10},{10... | collective-permute-start | bytes 7077896 | tf_op jit(solution)/shard_map/ppermute | solution.py:38
  238.3 29.2 %collective-permute-start.74 = (bf16[1,1152,512]{2,1,0:T(8,128)(2,1)S(1)}, bf16[1,1152,512]{2,1,0:T(8,128)(2,1)S(1)}, u32[]{:S(2)}, u32[]{:S(2)}) collective-permute-start(bf16[1,1152,512]{2,1,0:T(8,128)(2,1)S(1)} %get-tuple-element.218), channel_id=1, source_target_pairs={{0,16},{8,24},{16,0},{24,8},{1,17},{9,25},{17,1},{25,9},{2,18},{10... | collective-permute-start | bytes 3538952 | tf_op jit(solution)/shard_map/ppermute | solution.py:38
  239.3 28.1 %collective-permute-start.73 = (bf16[1,576,512]{2,1,0:T(8,128)(2,1)S(1)}, bf16[1,576,512]{2,1,0:T(8,128)(2,1)S(1)}, u32[]{:S(2)}, u32[]{:S(2)}) collective-permute-start(bf16[1,576,512]{2,1,0:T(8,128)(2,1)S(1)} %get-tuple-element.231), channel_id=1, source_target_pairs={{0,1},{1,0},{2,3},{3,2},{4,5},{5,4},{6,7},{7,6},{8,9},{9,8},{10,11... | collective-permute-start | bytes 1769480 | tf_op jit(solution)/shard_map/ppermute | solution.py:38
  256.9 10.6 %collective-permute-start.71 = (f32[2,512]{1,0:T(2,128)S(1)}, f32[2,512]{1,0:T(2,128)S(1)}, u32[]{:S(2)}, u32[]{:S(2)}) collective-permute-start(f32[2,512]{1,0:T(2,128)S(1)} %get-tuple-element.158), channel_id=1, source_target_pairs={{0,1},{1,0},{2,3},{3,2},{4,5},{5,4},{6,7},{7,6},{8,9},{9,8},{10,11... | collective-permute-start | bytes 12296 | tf_op jit(solution)/shard_map/ppermute | solution.py:54
  257.6 9.9 %collective-permute-start.72 = (f32[2,512]{1,0:T(2,128)S(1)}, f32[2,512]{1,0:T(2,128)S(1)}, u32[]{:S(2)}, u32[]{:S(2)}) collective-permute-start(f32[2,512]{1,0:T(2,128)S(1)} %get-tuple-element.158), channel_id=1, source_target_pairs={{0,9},{1,8},{2,11},{3,10},{4,13},{5,12},{6,15},{7,14},{8,1},{9,0},... | collective-permute-start | bytes 12296 | tf_op jit(solution)/shard_map/ppermute | solution.py:54
  268.7 14.2 %collective-permute-start.79 = (bf16[2,1152,512]{2,1,0:T(8,128)(2,1)}, bf16[2,1152,512]{2,1,0:T(8,128)(2,1)}, u32[]{:S(2)}, u32[]{:S(2)}) collective-permute-start(bf16[2,1152,512]{2,1,0:T(8,128)(2,1)} %get-tuple-element.163), channel_id=1, source_target_pairs={{0,8},{8,0},{16,24},{24,16},{1,9},{9,1},{17,25},{25,17},{2,10},{10... | collective-permute-start | bytes 7077896 | tf_op jit(solution)/shard_map/ppermute | solution.py:38
  270.8 9.5 %collective-permute-start.76 = (bf16[1,288,512]{2,1,0:T(8,128)(2,1)}, bf16[1,288,512]{2,1,0:T(8,128)(2,1)}, u32[]{:S(2)}, u32[]{:S(2)}) collective-permute-start(bf16[1,288,512]{2,1,0:T(8,128)(2,1)} %add_convert_fusion.27), channel_id=1, source_target_pairs={{0,2},{1,3},{2,0},{3,1},{4,6},{5,7},{6,4},{7,5},{8,10},{9,11},{10,... | collective-permute-start | bytes 884744 | tf_op jit(solution)/shard_map/ppermute | solution.py:38
  273.7 6.5 %collective-permute-start.75 = (f32[2,512]{1,0:T(2,128)S(1)}, f32[2,512]{1,0:T(2,128)S(1)}, u32[]{:S(2)}, u32[]{:S(2)}) collective-permute-start(f32[2,512]{1,0:T(2,128)S(1)} %add_add_fusion.5), channel_id=1, source_target_pairs={{0,2},{1,3},{2,0},{3,1},{4,6},{5,7},{6,4},{7,5},{8,10},{9,11},{10,... | collective-permute-start | bytes 12296 | tf_op jit(solution)/shard_map/ppermute | solution.py:54
  286.8 27.1 %collective-permute-start.81 = (bf16[2,576,512]{2,1,0:T(8,128)(2,1)S(1)}, bf16[2,576,512]{2,1,0:T(8,128)(2,1)}, u32[]{:S(2)}, u32[]{:S(2)}) collective-permute-start(bf16[2,576,512]{2,1,0:T(8,128)(2,1)S(1)} %get-tuple-element.216), channel_id=1, source_target_pairs={{0,1},{1,0},{2,3},{3,2},{4,5},{5,4},{6,7},{7,6},{8,9},{9,8},{10,11... | collective-permute-start | bytes 3538952 | tf_op jit(solution)/shard_map/ppermute | solution.py:38
  287.8 17.9 %collective-permute-start.82 = (bf16[1,576,512]{2,1,0:T(8,128)(2,1)S(1)}, bf16[1,576,512]{2,1,0:T(8,128)(2,1)S(1)}, u32[]{:S(2)}, u32[]{:S(2)}) collective-permute-start(bf16[1,576,512]{2,1,0:T(8,128)(2,1)S(1)} %copy-done.44), channel_id=1, source_target_pairs={{0,2},{1,3},{2,0},{3,1},{4,6},{5,7},{6,4},{7,5},{8,10},{9,11},{10,... | collective-permute-start | bytes 1769480 | tf_op jit(solution)/shard_map/ppermute | solution.py:38
  295.4 15.6 %collective-permute-start.80 = (bf16[2,864,128]{2,1,0:T(8,128)(2,1)S(1)}, bf16[2,864,128]{2,1,0:T(8,128)(2,1)S(1)}, u32[]{:S(2)}, u32[]{:S(2)}) collective-permute-start(bf16[2,864,128]{2,1,0:T(8,128)(2,1)S(1)} %get-tuple-element.235), channel_id=1, source_target_pairs={{0,16},{8,24},{16,0},{24,8},{1,17},{9,25},{17,1},{25,9},{2,18},{10... | collective-permute-start | bytes 1327112 | tf_op jit(solution)/shard_map/ppermute | solution.py:38
  296.4 14.6 %collective-permute-start.83 = (bf16[1,288,512]{2,1,0:T(8,128)(2,1)S(1)}, bf16[1,288,512]{2,1,0:T(8,128)(2,1)S(1)}, u32[]{:S(2)}, u32[]{:S(2)}) collective-permute-start(bf16[1,288,512]{2,1,0:T(8,128)(2,1)S(1)} %add_convert_fusion.25), channel_id=1, source_target_pairs={{0,4},{1,5},{2,6},{3,7},{4,0},{5,1},{6,2},{7,3},{8,12},{9,13},{10,... | collective-permute-start | bytes 884744 | tf_op jit(solution)/shard_map/ppermute | solution.py:38
  314.0 6.9 %collective-permute-start.84 = (bf16[2,640,512]{2,1,0:T(8,128)(2,1)}, bf16[2,640,512]{2,1,0:T(8,128)(2,1)}, u32[]{:S(2)}, u32[]{:S(2)}) collective-permute-start(bf16[2,640,512]{2,1,0:T(8,128)(2,1)} %get-tuple-element.176), channel_id=1, source_target_pairs={{0,8},{8,0},{16,24},{24,16},{1,9},{9,1},{17,25},{25,17},{2,10},{10... | collective-permute-start | bytes 3932168 | tf_op jit(solution)/shard_map/ppermute | solution.py:38
  314.0 15.2 %collective-permute-start.87 = (bf16[2,864,128]{2,1,0:T(8,128)(2,1)}, bf16[2,864,128]{2,1,0:T(8,128)(2,1)S(1)}, u32[]{:S(2)}, u32[]{:S(2)}) collective-permute-start(bf16[2,864,128]{2,1,0:T(8,128)(2,1)} %get-tuple-element.233), channel_id=1, source_target_pairs={{0,8},{8,0},{16,24},{24,16},{1,9},{9,1},{17,25},{25,17},{2,10},{10... | collective-permute-start | bytes 1327112 | tf_op jit(solution)/shard_map/ppermute | solution.py:38
  314.6 14.7 %collective-permute-start.88 = (bf16[2,864,128]{2,1,0:T(8,128)(2,1)}, bf16[2,864,128]{2,1,0:T(8,128)(2,1)S(1)}, u32[]{:S(2)}, u32[]{:S(2)}) collective-permute-start(bf16[2,864,128]{2,1,0:T(8,128)(2,1)} %get-tuple-element.232), channel_id=1, source_target_pairs={{0,24},{8,16},{16,8},{24,0},{1,25},{9,17},{17,9},{25,1},{2,26},{10... | collective-permute-start | bytes 1327112 | tf_op jit(solution)/shard_map/ppermute | solution.py:38
  320.2 15.0 %collective-permute-start.86 = (bf16[1,288,512]{2,1,0:T(8,128)(2,1)}, bf16[1,288,512]{2,1,0:T(8,128)(2,1)}, u32[]{:S(2)}, u32[]{:S(2)}) collective-permute-start(bf16[1,288,512]{2,1,0:T(8,128)(2,1)} %add_convert_fusion.22), channel_id=1, source_target_pairs={{0,1},{1,0},{2,3},{3,2},{4,5},{5,4},{6,7},{7,6},{8,9},{9,8},{10,11... | collective-permute-start | bytes 884744 | tf_op jit(solution)/shard_map/ppermute | solution.py:38
  323.6 17.0 %collective-permute-start.85 = (bf16[2,320,512]{2,1,0:T(8,128)(2,1)}, bf16[2,320,512]{2,1,0:T(8,128)(2,1)S(1)}, u32[]{:S(2)}, u32[]{:S(2)}) collective-permute-start(bf16[2,320,512]{2,1,0:T(8,128)(2,1)} %get-tuple-element.225), channel_id=1, source_target_pairs={{0,2},{1,3},{2,0},{3,1},{4,6},{5,7},{6,4},{7,5},{8,10},{9,11},{10,... | collective-permute-start | bytes 1966088 | tf_op jit(solution)/shard_map/ppermute | solution.py:38
  328.2 22.6 %collective-permute-start.93 = (bf16[1,576,512]{2,1,0:T(8,128)(2,1)}, bf16[1,576,512]{2,1,0:T(8,128)(2,1)S(1)}, u32[]{:S(2)}, u32[]{:S(2)}) collective-permute-start(bf16[1,576,512]{2,1,0:T(8,128)(2,1)} %get-tuple-element.227), channel_id=1, source_target_pairs={{0,16},{8,24},{16,0},{24,8},{1,17},{9,25},{17,1},{25,9},{2,18},{10... | collective-permute-start | bytes 1769480 | tf_op jit(solution)/shard_map/ppermute | solution.py:38
  340.8 13.1 %collective-permute-start.92 = (bf16[2,160,512]{2,1,0:T(8,128)(2,1)S(1)}, bf16[2,160,512]{2,1,0:T(8,128)(2,1)S(1)}, u32[]{:S(2)}, u32[]{:S(2)}) collective-permute-start(bf16[2,160,512]{2,1,0:T(8,128)(2,1)S(1)} %get-tuple-element.241), channel_id=1, source_target_pairs={{0,1},{1,0},{2,3},{3,2},{4,5},{5,4},{6,7},{7,6},{8,9},{9,8},{10,11... | collective-permute-start | bytes 983048 | tf_op jit(solution)/shard_map/ppermute | solution.py:38
  343.0 15.6 %collective-permute-start.91 = (bf16[1,288,512]{2,1,0:T(8,128)(2,1)S(1)}, bf16[1,288,512]{2,1,0:T(8,128)(2,1)S(1)}, u32[]{:S(2)}, u32[]{:S(2)}) collective-permute-start(bf16[1,288,512]{2,1,0:T(8,128)(2,1)S(1)} %add_convert_fusion.24), channel_id=1, source_target_pairs={{0,2},{1,3},{2,0},{3,1},{4,6},{5,7},{6,4},{7,5},{8,10},{9,11},{10,... | collective-permute-start | bytes 884744 | tf_op jit(solution)/shard_map/ppermute | solution.py:38
  343.6 17.2 %collective-permute-start.90 = (bf16[1,288,512]{2,1,0:T(8,128)(2,1)S(1)}, bf16[1,288,512]{2,1,0:T(8,128)(2,1)S(1)}, u32[]{:S(2)}, u32[]{:S(2)}) collective-permute-start(bf16[1,288,512]{2,1,0:T(8,128)(2,1)S(1)} %add_convert_fusion.21), channel_id=1, source_target_pairs={{0,4},{1,5},{2,6},{3,7},{4,0},{5,1},{6,2},{7,3},{8,12},{9,13},{10,... | collective-permute-start | bytes 884744 | tf_op jit(solution)/shard_map/ppermute | solution.py:38
  345.6 15.9 %collective-permute-start.94 = (bf16[2,64,320]{2,1,0:T(8,128)(2,1)S(1)}, bf16[2,64,320]{2,1,0:T(8,128)(2,1)S(1)}, u32[]{:S(2)}, u32[]{:S(2)}) collective-permute-start(bf16[2,64,320]{2,1,0:T(8,128)(2,1)S(1)} %get-tuple-element.181), channel_id=1, source_target_pairs={{0,1},{1,2},{2,3},{3,4},{4,5},{5,6},{6,7},{8,9},{9,10},{10,11},{11... | collective-permute-start | bytes 245768 | tf_op jit(solution)/shard_map/ppermute | solution.py:48
  350.8 33.2 %collective-permute-start.89 = (bf16[2,80,128]{2,1,0:T(8,128)(2,1)S(1)}, bf16[2,80,128]{2,1,0:T(8,128)(2,1)S(1)}, u32[]{:S(2)}, u32[]{:S(2)}) collective-permute-start(bf16[2,80,128]{2,1,0:T(8,128)(2,1)S(1)} %get-tuple-element.186), channel_id=1, source_target_pairs={{0,1},{1,2},{2,3},{3,4},{4,5},{5,6},{6,7},{8,9},{9,10},{10,11},{11... | collective-permute-start | bytes 122888 | tf_op jit(solution)/shard_map/ppermute | solution.py:48
  353.9 10.2 %collective-permute-start.98 = (bf16[1,288,512]{2,1,0:T(8,128)(2,1)S(1)}, bf16[1,288,512]{2,1,0:T(8,128)(2,1)S(1)}, u32[]{:S(2)}, u32[]{:S(2)}) collective-permute-start(bf16[1,288,512]{2,1,0:T(8,128)(2,1)S(1)} %add_convert_fusion.20), channel_id=1, source_target_pairs={{0,2},{1,3},{2,0},{3,1},{4,6},{5,7},{6,4},{7,5},{8,10},{9,11},{10,... | collective-permute-start | bytes 884744 | tf_op jit(solution)/shard_map/ppermute | solution.py:38
  360.8 35.7 %collective-permute-start.105 = (bf16[1,576,512]{2,1,0:T(8,128)(2,1)}, bf16[1,576,512]{2,1,0:T(8,128)(2,1)S(1)}, u32[]{:S(2)}, u32[]{:S(2)}) collective-permute-start(bf16[1,576,512]{2,1,0:T(8,128)(2,1)} %maximum_select_fusion), channel_id=1, source_target_pairs={{0,1},{1,0},{2,3},{3,2},{4,5},{5,4},{6,7},{7,6},{8,9},{9,8},{10,11... | collective-permute-start | bytes 1769480 | tf_op jit(solution)/shard_map/ppermute | solution.py:38
  361.5 18.1 %collective-permute-start.97 = (bf16[1,288,512]{2,1,0:T(8,128)(2,1)S(1)}, bf16[1,288,512]{2,1,0:T(8,128)(2,1)S(1)}, u32[]{:S(2)}, u32[]{:S(2)}) collective-permute-start(bf16[1,288,512]{2,1,0:T(8,128)(2,1)S(1)} %add_convert_fusion.19), channel_id=1, source_target_pairs={{0,1},{1,0},{2,3},{3,2},{4,5},{5,4},{6,7},{7,6},{8,9},{9,8},{10,11... | collective-permute-start | bytes 884744 | tf_op jit(solution)/shard_map/ppermute | solution.py:38
  364.0 16.6 %collective-permute-start.96 = (bf16[1,160,512]{2,1,0:T(8,128)(2,1)S(1)}, bf16[1,160,512]{2,1,0:T(8,128)(2,1)S(1)}, u32[]{:S(2)}, u32[]{:S(2)}) collective-permute-start(bf16[1,160,512]{2,1,0:T(8,128)(2,1)S(1)} %add_convert_fusion.29), channel_id=1, source_target_pairs={{0,4},{1,5},{2,6},{3,7},{4,0},{5,1},{6,2},{7,3},{8,12},{9,13},{10,... | collective-permute-start | bytes 491528 | tf_op jit(solution)/shard_map/ppermute | solution.py:38
  364.3 18.6 %collective-permute-start.100 = (bf16[1,288,512]{2,1,0:T(8,128)(2,1)S(1)}, bf16[1,288,512]{2,1,0:T(8,128)(2,1)S(1)}, u32[]{:S(2)}, u32[]{:S(2)}) collective-permute-start(bf16[1,288,512]{2,1,0:T(8,128)(2,1)S(1)} %add_convert_fusion.17), channel_id=1, source_target_pairs={{0,4},{1,5},{2,6},{3,7},{4,0},{5,1},{6,2},{7,3},{8,12},{9,13},{10,... | collective-permute-start | bytes 884744 | tf_op jit(solution)/shard_map/ppermute | solution.py:38
  380.7 7.3 %collective-permute-start.99 = (bf16[1,160,512]{2,1,0:T(8,128)(2,1)S(1)}, bf16[1,160,512]{2,1,0:T(8,128)(2,1)S(1)}, u32[]{:S(2)}, u32[]{:S(2)}) collective-permute-start(bf16[1,160,512]{2,1,0:T(8,128)(2,1)S(1)} %add_convert_fusion.28), channel_id=1, source_target_pairs={{0,1},{1,0},{2,3},{3,2},{4,5},{5,4},{6,7},{7,6},{8,9},{9,8},{10,11... | collective-permute-start | bytes 491528 | tf_op jit(solution)/shard_map/ppermute | solution.py:38
  382.9 10.0 %collective-permute-start.102 = (bf16[1,288,512]{2,1,0:T(8,128)(2,1)S(1)}, bf16[1,288,512]{2,1,0:T(8,128)(2,1)S(1)}, u32[]{:S(2)}, u32[]{:S(2)}) collective-permute-start(bf16[1,288,512]{2,1,0:T(8,128)(2,1)S(1)} %add_convert_fusion.16), channel_id=1, source_target_pairs={{0,2},{1,3},{2,0},{3,1},{4,6},{5,7},{6,4},{7,5},{8,10},{9,11},{10,... | collective-permute-start | bytes 884744 | tf_op jit(solution)/shard_map/ppermute | solution.py:38
  386.0 26.3 %collective-permute-start.104 = (bf16[1,576,512]{2,1,0:T(8,128)(2,1)}, bf16[1,576,512]{2,1,0:T(8,128)(2,1)S(1)}, u32[]{:S(2)}, u32[]{:S(2)}) collective-permute-start(bf16[1,576,512]{2,1,0:T(8,128)(2,1)} %maximum_select_fusion.1), channel_id=1, source_target_pairs={{0,2},{1,3},{2,0},{3,1},{4,6},{5,7},{6,4},{7,5},{8,10},{9,11},{10,... | collective-permute-start | bytes 1769480 | tf_op jit(solution)/shard_map/ppermute | solution.py:38
  393.2 19.1 %collective-permute-start.103 = (bf16[1,576,512]{2,1,0:T(8,128)(2,1)S(1)}, bf16[1,576,512]{2,1,0:T(8,128)(2,1)S(1)}, u32[]{:S(2)}, u32[]{:S(2)}) collective-permute-start(bf16[1,576,512]{2,1,0:T(8,128)(2,1)S(1)} %maximum_select_fusion.2), channel_id=1, source_target_pairs={{0,1},{1,0},{2,3},{3,2},{4,5},{5,4},{6,7},{7,6},{8,9},{9,8},{10,11... | collective-permute-start | bytes 1769480 | tf_op jit(solution)/shard_map/ppermute | solution.py:38
  396.2 14.4 %collective-permute-start.101 = (bf16[1,320,512]{2,1,0:T(8,128)(2,1)S(1)}, bf16[1,320,512]{2,1,0:T(8,128)(2,1)S(1)}, u32[]{:S(2)}, u32[]{:S(2)}) collective-permute-start(bf16[1,320,512]{2,1,0:T(8,128)(2,1)S(1)} %maximum_select_fusion.7), channel_id=1, source_target_pairs={{0,2},{1,3},{2,0},{3,1},{4,6},{5,7},{6,4},{7,5},{8,10},{9,11},{10,... | collective-permute-start | bytes 983048 | tf_op jit(solution)/shard_map/ppermute | solution.py:38
  (93 other events, 712.3 us)

commit v4 on v3

--- a/solution.py
+++ b/solution.py
@@ -1146,6 +1146,7 @@
         "mid_assembly",
     )
     entry_own, entry_other = sums_of["e"].halves(token)
+    entry_own = tied(entry_own, conv_mid_grad)
     conv_mid_grad = conv_mid_grad.reshape(3, 3, 3, chans_out, wide)
     conv_in_grad, proj_grad = call(
         entry_assembly_kernel,

time: 422 us -> 422 us (level)
  transfers between devices with their start and end apart: 107 -> 107, of which waited for: 46 -> 46; matrix products, arithmetic and copies ran while one was open for 9% -> 9% of each run, Pallas kernels for 24% -> 23%
where the time goes in v4:
time: 422 us; the launch traced here: 416 us
  waiting for transfers between devices  130 us (31%)
  starting transfers between devices  116 us (27%)
  Pallas kernels  104 us (25%)
  other arithmetic  37.1 us (9%)
  local copies, waits for them, and re-layouts  26.1 us (6%)
    pallas_call x20, Pallas kernels, call(): pl.pallas_call(kernel, out_shape=shapes, in_specs=specs, out_specs=out_sp...  104 us
    ppermute x55, waiting for transfers between devices, flipped(): return lax.ppermute(value, axis, [(i, i ^ bit) for i in range(count)])  94.4 us
    ppermute x48, starting transfers between devices, exchanged(): lax.ppermute(value, ('chan', 'space'), [(i, i ^ flip) for i in range(coun...  62.8 us
    ppermute x55, starting transfers between devices, flipped(): return lax.ppermute(value, axis, [(i, i ^ bit) for i in range(count)])  45.1 us
    ppermute x48, waiting for transfers between devices, exchanged(): lax.ppermute(value, ('chan', 'space'), [(i, i ^ flip) for i in range(coun...  35.3 us
    convert_element_type x20, other arithmetic, added(): return total.astype(LOW)  27.3 us
    unnamed x98, local copies, waits for them, and re-layouts  13.7 us
  transfers between devices with their start and end apart: 107, of which 46 were waited for; matrix products, arithmetic and copies ran while one was open for 9% of the time, Pallas kernels for 23%

profile of v4, /device:TPU:0, one launch (start us, length us, event | category | flops | bytes accessed | tf_op | source)
XLA Modules:
  0.0 416.1 jit_solution(16329602263335626019)
XLA Ops:
  7.3 2.6 collective-permute-start.8
  11.0 3.5 slice_bitcast_fusion
  14.6 2.8 spread_features.1
  21.2 13.8 %collective-permute-done.5.refs_2_ = bf16[2,864,128]{2,1,0:T(8,128)(2,1)} collective-permute-done((bf16[2,864,128]{2,1,0:T(8,128)(2,1)}, bf16[2,864,128]{2,1,0:T(8,128)(2,1)}, u32[]{:S(2)}, u32[]{:S(2)}) %collective-permute-start.5) | collective-permute-done | bytes 442400 | tf_op jit(solution)/shard_map/ppermute | solution.py:38
  35.0 1.9 collective-permute-start.1
  37.0 7.2 %collective-permute-done.6.refs_3_ = bf16[2,864,128]{2,1,0:T(8,128)(2,1)} collective-permute-done((bf16[2,864,128]{2,1,0:T(8,128)(2,1)}, bf16[2,864,128]{2,1,0:T(8,128)(2,1)}, u32[]{:S(2)}, u32[]{:S(2)}) %collective-permute-start.6) | collective-permute-done | bytes 442400 | tf_op jit(solution)/shard_map/ppermute | solution.py:38
  53.0 6.4 %entry_forward.1 = (bf16[864,512]{1,0:T(8,128)(2,1)S(1)}, bf16[864,512]{1,0:T(8,128)(2,1)S(1)}, f32[4,512]{1,0:T(4,128)S(1)}, bf16[2,864,512]{2,1,0:T(8,128)(2,1)S(1)}) custom-call(f32[864,8]{1,0:T(8,128)S(1)} %convert_element_type.300.marks_ref, bf16[2,864,128]{2,1,0:T(8,128)(2,1)S(1)} %copy-done.24, bf16[2,864,128]{2,1,0:T(8,128)(2,1)} %collective-permute-done.4.refs_1_, ...), custom_call_target="tpu_custom_call" | custom-call | flops 2038431744 | bytes 7965696 | tf_op jit(solution)/shard_map/entry_forward/pallas_call | solution.py:817
  62.6 3.0 collective-permute-start.11
  68.7 4.0 collective-permute-done.17.refs_4_.refs_6_
  74.4 4.8 %collective-permute-start.14 = (f32[4,512]{1,0:T(4,128)S(1)}, f32[4,512]{1,0:T(4,128)S(1)}, u32[]{:S(2)}, u32[]{:S(2)}) collective-permute-start(f32[4,512]{1,0:T(4,128)S(1)} %add_add_fusion.3), channel_id=1, source_target_pairs={{0,4},{1,5},{2,6},{3,7},{4,0},{5,1},{6,2},{7,3},{8,12},{9,13},{10,... | collective-permute-start | bytes 24584 | tf_op jit(solution)/shard_map/ppermute | solution.py:54
  80.9 1.9 collective-permute-start.13
  86.0 7.4 %mid_forward_a.1 = (bf16[864,512]{1,0:T(8,128)(2,1)S(1)}, f32[2,512]{1,0:T(2,128)S(1)}, bf16[864,512]{1,0:T(8,128)(2,1)S(1)}) custom-call(s32[1]{0:T(128)} %bitcast.chan_ref, f32[1]{0:T(128)} %bitcast.2.inv_ref, f32[864,8]{1,0:T(8,128)S(1)} %convert_element_type.300.marks_ref, f32[10,512]{1,0:T(8,128)S(1)} %add.396.par_ref, bf16[864,512]{1,0:T(8,128)(2,1)S(1)} %copy-done.6, ...), custom_call_target="tpu_custom_call" | custom-call | flops 4076863488 | bytes 7429128 | tf_op jit(solution)/shard_map/mid_forward_a/pallas_call | solution.py:817
  98.0 3.2 collective-permute-done.26.refs_6_
  102.9 4.7 %collective-permute-start.23 = (f32[2,512]{1,0:T(2,128)S(1)}, f32[2,512]{1,0:T(2,128)S(1)}, u32[]{:S(2)}, u32[]{:S(2)}) collective-permute-start(f32[2,512]{1,0:T(2,128)S(1)} %add_add_fusion.15), channel_id=1, source_target_pairs={{0,4},{1,5},{2,6},{3,7},{4,0},{5,1},{6,2},{7,3},{8,12},{9,13},{10,... | collective-permute-start | bytes 12296 | tf_op jit(solution)/shard_map/ppermute | solution.py:54
  109.2 1.9 collective-permute-start.22
  111.1 1.9 collective-permute-done.24
  113.1 6.6 %mid_forward_b.1 = (bf16[864,512]{1,0:T(8,128)(2,1)S(1)}, f32[2,512]{1,0:T(2,128)S(1)}, bf16[864,512]{1,0:T(8,128)(2,1)S(1)}, bf16[864,512]{1,0:T(8,128)(2,1)S(1)}) custom-call(s32[1]{0:T(128)} %bitcast.chan_ref, f32[1]{0:T(128)} %bitcast.2.inv_ref, f32[864,8]{1,0:T(8,128)S(1)} %convert_element_type.300.marks_ref, f32[10,512]{1,0:T(8,128)S(1)} %add.396.par_ref, ...), custom_call_target="tpu_custom_call" | custom-call | flops 4076863488 | bytes 9202696 | tf_op jit(solution)/shard_map/mid_forward_b/pallas_call | solution.py:817
  124.3 5.2 %collective-permute-done.35.refs_4_.refs_6_ = bf16[3,3,128,512]{3,2,1,0:T(8,128)(2,1)S(1)} collective-permute-done((bf16[3,3,128,512]{3,2,1,0:T(8,128)(2,1)S(1)}, bf16[3,3,128,512]{3,2,1,0:T(8,128)(2,1)S(1)}, u32[]{:S(2)}, u32[]{:S(2)}) %collective-permute-start.35) | collective-permute-done | bytes 1179680 | tf_op jit(solution)/shard_map/ppermute | solution.py:38
  129.6 5.4 %collective-permute-start.32 = (f32[2,512]{1,0:T(2,128)S(1)}, f32[2,512]{1,0:T(2,128)S(1)}, u32[]{:S(2)}, u32[]{:S(2)}) collective-permute-start(f32[2,512]{1,0:T(2,128)S(1)} %add_add_fusion.13), channel_id=1, source_target_pairs={{0,4},{1,5},{2,6},{3,7},{4,0},{5,1},{6,2},{7,3},{8,12},{9,13},{10,... | collective-permute-start | bytes 12296 | tf_op jit(solution)/shard_map/ppermute | solution.py:54
  136.7 3.7 collective-permute-done.33
  141.5 6.4 %mid_forward_c.1 = (bf16[864,512]{1,0:T(8,128)(2,1)S(1)}, f32[2,512]{1,0:T(2,128)S(1)}, bf16[864,512]{1,0:T(8,128)(2,1)S(1)}) custom-call(s32[1]{0:T(128)} %bitcast.chan_ref, f32[1]{0:T(128)} %bitcast.2.inv_ref, f32[864,8]{1,0:T(8,128)S(1)} %convert_element_type.300.marks_ref, f32[10,512]{1,0:T(8,128)S(1)} %add.396.par_ref, ...), custom_call_target="tpu_custom_call" | custom-call | bytes 1 | tf_op jit(solution)/shard_map/mid_forward_c/pallas_call | solution.py:817
  159.2 2.3 collective-permute-done.45
  167.6 2.2 collective-permute-start.51
  173.5 7.3 %mid_backward_c.1 = (bf16[3,1056,512]{2,1,0:T(8,128)(2,1)S(1)}, bf16[864,512]{1,0:T(8,128)(2,1)S(1)}, f32[2,512]{1,0:T(2,128)S(1)}) custom-call(s32[1]{0:T(128)} %bitcast.chan_ref, f32[1]{0:T(128)} %bitcast.2.inv_ref, f32[864,8]{1,0:T(8,128)S(1)} %convert_element_type.300.marks_ref, f32[10,512]{1,0:T(8,128)S(1)} %add.396.par_ref, ...), custom_call_target="tpu_custom_call" | custom-call | bytes 1 | tf_op jit(solution)/shard_map/mid_backward_c/pallas_call | solution.py:817
  186.0 5.9 %mid_weight_c.1 = (bf16[2,1152,512]{2,1,0:T(8,128)(2,1)S(1)}, bf16[2,1152,512]{2,1,0:T(8,128)(2,1)S(1)}) custom-call(s32[1]{0:T(128)} %bitcast.chan_ref, bf16[864,512]{1,0:T(8,128)(2,1)S(1)} %get-tuple-element.138.a_ref, bf16[3,1056,512]{2,1,0:T(8,128)(2,1)S(1)} %get-tuple-element.139.ga_ref), custom_call_target="tpu_custom_call" | custom-call | flops 4076863488 | bytes 8847364 | tf_op jit(solution)/shard_map/mid_weight_c/pallas_call | solution.py:817
  193.9 2.2 collective-permute-done.58
  200.9 2.2 collective-permute-start.61
  203.9 2.4 collective-permute-done.61
  206.3 7.5 %mid_backward_b.1 = (bf16[3,1056,512]{2,1,0:T(8,128)(2,1)S(1)}, bf16[864,512]{1,0:T(8,128)(2,1)S(1)}, f32[3,512]{1,0:T(4,128)S(1)}) custom-call(s32[1]{0:T(128)} %bitcast.chan_ref, f32[1]{0:T(128)} %bitcast.2.inv_ref, f32[864,8]{1,0:T(8,128)S(1)} %convert_element_type.300.marks_ref, f32[10,512]{1,0:T(8,128)S(1)} %add.396.par_ref, ...), custom_call_target="tpu_custom_call" | custom-call | bytes 1 | tf_op jit(solution)/shard_map/mid_backward_b/pallas_call | solution.py:817
  215.8 7.2 %mid_weight_b.1 = (bf16[2,1152,512]{2,1,0:T(8,128)(2,1)S(1)}, bf16[2,1152,512]{2,1,0:T(8,128)(2,1)}) custom-call(s32[1]{0:T(128)} %bitcast.chan_ref, bf16[864,512]{1,0:T(8,128)(2,1)S(1)} %get-tuple-element.149.a_ref, bf16[3,1056,512]{2,1,0:T(8,128)(2,1)S(1)} %get-tuple-element.150.ga_ref), custom_call_target="tpu_custom_call" | custom-call | bytes 1 | tf_op jit(solution)/shard_map/mid_weight_b/pallas_call | solution.py:817
  223.0 3.6 collective-permute-done.65
  227.6 2.7 add_convert_fusion.12
  231.8 2.2 collective-permute-done.66
  234.1 4.2 %add_convert_fusion.2 = (bf16[1,1152,512]{2,1,0:T(8,128)(2,1)}, bf16[1,1152,512]{2,1,0:T(8,128)(2,1)S(1)}) fusion(bf16[2,1152,512]{2,1,0:T(8,128)(2,1)} %collective-permute-done.67, bf16[2,1152,512]{2,1,0:T(8,128)(2,1)} %copy-done.10), kind=kLoop, calls=%fused_computation.2 | loop fusion | flops 4718592 | bytes 7077888 | tf_op jit(solution)/shard_map/convert_element_type | solution.py:132
  242.2 1.9 collective-permute-start.69
  245.3 2.4 collective-permute-done.69
  247.7 9.0 %mid_backward_a.1 = (bf16[3,1056,512]{2,1,0:T(8,128)(2,1)S(1)}, bf16[864,512]{1,0:T(8,128)(2,1)S(1)}, f32[2,512]{1,0:T(2,128)S(1)}, bf16[864,512]{1,0:T(8,128)(2,1)S(1)}) custom-call(s32[1]{0:T(128)} %bitcast.chan_ref, f32[1]{0:T(128)} %bitcast.2.inv_ref, f32[864,8]{1,0:T(8,128)S(1)} %convert_element_type.300.marks_ref, f32[10,512]{1,0:T(8,128)S(1)} %add.396.par_ref, ...), custom_call_target="tpu_custom_call" | custom-call | bytes 1 | tf_op jit(solution)/shard_map/mid_backward_a/pallas_call | solution.py:817
  258.8 7.3 %mid_weight_a.1 = (bf16[2,1152,512]{2,1,0:T(8,128)(2,1)S(1)}, bf16[2,1152,512]{2,1,0:T(8,128)(2,1)}) custom-call(s32[1]{0:T(128)} %bitcast.chan_ref, bf16[864,512]{1,0:T(8,128)(2,1)S(1)} %copy-done.20, bf16[3,1056,512]{2,1,0:T(8,128)(2,1)S(1)} %get-tuple-element.162.ga_ref), custom_call_target="tpu_custom_call" | custom-call | bytes 1 | tf_op jit(solution)/shard_map/mid_weight_a/pallas_call | solution.py:817
  270.8 2.9 add_convert_fusion.10
  273.7 2.1 collective-permute-start.75
  276.4 1.9 collective-permute-start.78
  278.3 2.0 collective-permute-done.75
  283.5 3.4 add_convert_fusion
  287.9 6.4 %entry_backward.1 = bf16[4,2,864,128]{3,2,1,0:T(8,128)(2,1)S(1)} custom-call(f32[864,8]{1,0:T(8,128)S(1)} %convert_element_type.300.marks_ref, bf16[2,960,512]{2,1,0:T(8,128)(2,1)S(1)} %entry_norm.1.gm_ref, bf16[864,512]{1,0:T(8,128)(2,1)S(1)} %get-tuple-element.173.short_ref, bf16[10,64,512]{2,1,0:T(8,128)(2,1)S(1)} %pad_maximum_fusion.refs_4_.refs_0_, ...), custom_call_target="tpu_custom_call" | custom-call | bytes 1 | tf_op jit(solution)/shard_map/entry_backward/pallas_call | solution.py:817
  296.4 2.1 collective-permute-start.83
  298.6 6.1 %entry_weight.1 = (bf16[2,640,512]{2,1,0:T(8,128)(2,1)S(1)}, bf16[2,640,512]{2,1,0:T(8,128)(2,1)}) custom-call(bf16[2,864,512]{2,1,0:T(8,128)(2,1)S(1)} %copy-done.15, bf16[2,960,512]{2,1,0:T(8,128)(2,1)S(1)} %entry_norm.1.gm_ref, bf16[864,512]{1,0:T(8,128)(2,1)S(1)} %get-tuple-element.173.short_ref), custom_call_target="tpu_custom_call" | custom-call | bytes 1 | tf_op jit(solution)/shard_map/entry_weight/pallas_call | solution.py:817
  305.7 5.4 %collective-permute-done.83 = bf16[1,288,512]{2,1,0:T(8,128)(2,1)S(1)} collective-permute-done((bf16[1,288,512]{2,1,0:T(8,128)(2,1)S(1)}, bf16[1,288,512]{2,1,0:T(8,128)(2,1)S(1)}, u32[]{:S(2)}, u32[]{:S(2)}) %collective-permute-start.83) | collective-permute-done | bytes 294944 | tf_op jit(solution)/shard_map/ppermute | solution.py:38
  311.0 2.9 collective-permute-done.81
  316.4 3.0 add_convert_fusion.8
  320.9 2.7 add_convert_fusion.7
  325.4 2.8 collective-permute-done.106
  329.3 6.0 %join_features.1 = (f32[2,64,6720]{2,1,0:T(8,128)}, bf16[2,64,320]{2,1,0:T(8,128)(2,1)S(1)}) custom-call(s32[1]{0:T(128)} %bitcast.chan_ref, bf16[2,864,128]{2,1,0:T(8,128)(2,1)S(1)} %get-tuple-element.181.refs_0_, bf16[2,864,128]{2,1,0:T(8,128)(2,1)S(1)} %collective-permute-done.87.refs_1_, bf16[2,864,128]{2,1,0:T(8,128)(2,1)S(1)} %collective-permute-done.80.refs_2_, ...), custom_call_target="tpu_custom_call" | custom-call | bytes 5292036 | tf_op jit(solution)/shard_map/join_features/pallas_call | solution.py:817
  336.4 4.2 %collective-permute-done.85 = bf16[2,320,512]{2,1,0:T(8,128)(2,1)S(1)} collective-permute-done((bf16[2,320,512]{2,1,0:T(8,128)(2,1)}, bf16[2,320,512]{2,1,0:T(8,128)(2,1)S(1)}, u32[]{:S(2)}, u32[]{:S(2)}) %collective-permute-start.85) | collective-permute-done | bytes 655392 | tf_op jit(solution)/shard_map/ppermute | solution.py:38
  343.6 2.0 collective-permute-start.90
  345.6 2.8 collective-permute-start.94
  348.4 2.4 join_rows.1
  350.8 3.0 collective-permute-start.89
  355.0 3.7 collective-permute-done.91
  364.3 2.9 collective-permute-start.100
  367.2 12.4 %collective-permute-done.97 = bf16[1,288,512]{2,1,0:T(8,128)(2,1)S(1)} collective-permute-done((bf16[1,288,512]{2,1,0:T(8,128)(2,1)S(1)}, bf16[1,288,512]{2,1,0:T(8,128)(2,1)S(1)}, u32[]{:S(2)}, u32[]{:S(2)}) %collective-permute-start.97) | collective-permute-done | bytes 294944 | tf_op jit(solution)/shard_map/ppermute | solution.py:38
  386.0 2.1 collective-permute-start.103
  388.2 4.8 %collective-permute-done.101 = bf16[1,288,512]{2,1,0:T(8,128)(2,1)S(1)} collective-permute-done((bf16[1,288,512]{2,1,0:T(8,128)(2,1)S(1)}, bf16[1,288,512]{2,1,0:T(8,128)(2,1)S(1)}, u32[]{:S(2)}, u32[]{:S(2)}) %collective-permute-start.101) | collective-permute-done | bytes 294944 | tf_op jit(solution)/shard_map/ppermute | solution.py:38
  396.7 13.8 %collective-permute-done.105 = bf16[1,320,512]{2,1,0:T(8,128)(2,1)S(1)} collective-permute-done((bf16[1,320,512]{2,1,0:T(8,128)(2,1)S(1)}, bf16[1,320,512]{2,1,0:T(8,128)(2,1)S(1)}, u32[]{:S(2)}, u32[]{:S(2)}) %collective-permute-start.105) | collective-permute-done | bytes 327712 | tf_op jit(solution)/shard_map/ppermute | solution.py:38
  410.5 3.7 mid_assembly.1
  (367 shorter events, 134.9 us)
Async XLA Ops:
  1.4 19.2 %collective-permute-start = (f32[10,512]{1,0:T(8,128)S(1)}, f32[10,512]{1,0:T(8,128)S(1)}, u32[]{:S(2)}, u32[]{:S(2)}) collective-permute-start(f32[10,512]{1,0:T(8,128)S(1)} %constant_dynamic-update-slice_fusion.1), channel_id=1, source_target_pairs={{0,8},{8,0},{16,24},{24,16},{1,9},{9,1},{17,25},{25,17},{2,10},{10... | collective-permute-start | bytes 61448 | tf_op jit(solution)/shard_map/ppermute | solution.py:38
  2.7 11.9 %collective-permute-start.2 = (bf16[2,64,320]{2,1,0:T(8,128)(2,1)S(1)}, bf16[2,64,320]{2,1,0:T(8,128)(2,1)S(1)}, u32[]{:S(2)}, u32[]{:S(2)}) collective-permute-start(bf16[2,64,320]{2,1,0:T(8,128)(2,1)S(1)} %slice.182), channel_id=1, source_target_pairs={{1,0},{2,1},{3,2},{4,3},{5,4},{6,5},{7,6},{9,8},{10,9},{11,10},{12... | collective-permute-start | bytes 245768 | tf_op jit(solution)/shard_map/ppermute | solution.py:43
  4.8 9.8 %collective-permute-start.3 = (bf16[2,80,128]{2,1,0:T(8,128)(2,1)S(1)}, bf16[2,80,128]{2,1,0:T(8,128)(2,1)S(1)}, u32[]{:S(2)}, u32[]{:S(2)}) collective-permute-start(bf16[2,80,128]{2,1,0:T(8,128)(2,1)S(1)} %slice.233), channel_id=1, source_target_pairs={{1,0},{2,1},{3,2},{4,3},{5,4},{6,5},{7,6},{9,8},{10,9},{11,10},{12... | collective-permute-start | bytes 122888 | tf_op jit(solution)/shard_map/ppermute | solution.py:43
  7.3 42.0 %collective-permute-start.8 = (bf16[10,64,512]{2,1,0:T(8,128)(2,1)S(1)}, bf16[10,64,512]{2,1,0:T(8,128)(2,1)}, u32[]{:S(2)}, u32[]{:S(2)}) collective-permute-start(bf16[10,64,512]{2,1,0:T(8,128)(2,1)S(1)} %pad_maximum_fusion.refs_4_.refs_0_), channel_id=1, source_target_pairs={{0,16},{8,24},{16,0},{24,8},{1,17},{9,25},{17,1},{25,9},{2,18},{10... | collective-permute-start | bytes 1966088 | tf_op jit(solution)/shard_map/ppermute | solution.py:38
  18.7 27.2 %collective-permute-start.4 = (bf16[2,864,128]{2,1,0:T(8,128)(2,1)}, bf16[2,864,128]{2,1,0:T(8,128)(2,1)}, u32[]{:S(2)}, u32[]{:S(2)}) collective-permute-start(bf16[2,864,128]{2,1,0:T(8,128)(2,1)} %get-tuple-element.240), channel_id=1, source_target_pairs={{0,8},{8,0},{16,24},{24,16},{1,9},{9,1},{17,25},{25,17},{2,10},{10... | collective-permute-start | bytes 1327112 | tf_op jit(solution)/shard_map/ppermute | solution.py:38
  19.0 16.1 %collective-permute-start.5 = (bf16[2,864,128]{2,1,0:T(8,128)(2,1)}, bf16[2,864,128]{2,1,0:T(8,128)(2,1)}, u32[]{:S(2)}, u32[]{:S(2)}) collective-permute-start(bf16[2,864,128]{2,1,0:T(8,128)(2,1)} %get-tuple-element.239), channel_id=1, source_target_pairs={{0,16},{8,24},{16,0},{24,8},{1,17},{9,25},{17,1},{25,9},{2,18},{10... | collective-permute-start | bytes 1327112 | tf_op jit(solution)/shard_map/ppermute | solution.py:38
  19.3 24.9 %collective-permute-start.6 = (bf16[2,864,128]{2,1,0:T(8,128)(2,1)}, bf16[2,864,128]{2,1,0:T(8,128)(2,1)}, u32[]{:S(2)}, u32[]{:S(2)}) collective-permute-start(bf16[2,864,128]{2,1,0:T(8,128)(2,1)} %get-tuple-element.238), channel_id=1, source_target_pairs={{0,24},{8,16},{16,8},{24,0},{1,25},{9,17},{17,9},{25,1},{2,26},{10... | collective-permute-start | bytes 1327112 | tf_op jit(solution)/shard_map/ppermute | solution.py:38
  20.6 31.4 %collective-permute-start.7 = (bf16[10,64,512]{2,1,0:T(8,128)(2,1)S(1)}, bf16[10,64,512]{2,1,0:T(8,128)(2,1)}, u32[]{:S(2)}, u32[]{:S(2)}) collective-permute-start(bf16[10,64,512]{2,1,0:T(8,128)(2,1)S(1)} %pad_maximum_fusion.refs_4_.refs_0_), channel_id=1, source_target_pairs={{0,8},{8,0},{16,24},{24,16},{1,9},{9,1},{17,25},{25,17},{2,10},{10... | collective-permute-start | bytes 1966088 | tf_op jit(solution)/shard_map/ppermute | solution.py:38
  35.0 10.8 %collective-permute-start.1 = (f32[10,512]{1,0:T(8,128)S(1)}, f32[10,512]{1,0:T(8,128)S(1)}, u32[]{:S(2)}, u32[]{:S(2)}) collective-permute-start(f32[10,512]{1,0:T(8,128)S(1)} %constant_dynamic-update-slice_fusion), channel_id=1, source_target_pairs={{0,16},{8,24},{16,0},{24,8},{1,17},{9,25},{17,1},{25,9},{2,18},{10... | collective-permute-start | bytes 61448 | tf_op jit(solution)/shard_map/ppermute | solution.py:38
  44.1 28.5 %collective-permute-start.17 = (bf16[3,3,128,512]{3,2,1,0:T(8,128)(2,1)}, bf16[3,3,128,512]{3,2,1,0:T(8,128)(2,1)}, u32[]{:S(2)}, u32[]{:S(2)}) collective-permute-start(bf16[3,3,128,512]{3,2,1,0:T(8,128)(2,1)} %get-tuple-element.114.refs_2_.refs_4_), channel_id=1, source_target_pairs={{0,16},{8,24},{16,0},{24,8},{1,17},{9,25},{17,1},{25,9},{2,18},{10... | collective-permute-start | bytes 3538952 | tf_op jit(solution)/shard_map/ppermute | solution.py:38
  65.7 19.1 %collective-permute-start.16 = (bf16[3,3,128,512]{3,2,1,0:T(8,128)(2,1)}, bf16[3,3,128,512]{3,2,1,0:T(8,128)(2,1)}, u32[]{:S(2)}, u32[]{:S(2)}) collective-permute-start(bf16[3,3,128,512]{3,2,1,0:T(8,128)(2,1)} %get-tuple-element.114.refs_2_.refs_4_), channel_id=1, source_target_pairs={{0,8},{8,0},{16,24},{24,16},{1,9},{9,1},{17,25},{25,17},{2,10},{10... | collective-permute-start | bytes 3538952 | tf_op jit(solution)/shard_map/ppermute | solution.py:38
  72.7 12.1 %collective-permute-start.18 = (bf16[3,3,128,512]{3,2,1,0:T(8,128)(2,1)}, bf16[3,3,128,512]{3,2,1,0:T(8,128)(2,1)}, u32[]{:S(2)}, u32[]{:S(2)}) collective-permute-start(bf16[3,3,128,512]{3,2,1,0:T(8,128)(2,1)} %collective-permute-done.17.refs_4_.refs_6_), channel_id=1, source_target_pairs={{0,8},{8,0},{16,24},{24,16},{1,9},{9,1},{17,25},{25,17},{2,10},{10... | collective-permute-start | bytes 3538952 | tf_op jit(solution)/shard_map/ppermute | solution.py:38
  72.7 28.5 %collective-permute-start.26 = (bf16[3,3,128,512]{3,2,1,0:T(8,128)(2,1)S(1)}, bf16[3,3,128,512]{3,2,1,0:T(8,128)(2,1)}, u32[]{:S(2)}, u32[]{:S(2)}) collective-permute-start(bf16[3,3,128,512]{3,2,1,0:T(8,128)(2,1)S(1)} %get-tuple-element.119.refs_4_), channel_id=1, source_target_pairs={{0,16},{8,24},{16,0},{24,8},{1,17},{9,25},{17,1},{25,9},{2,18},{10... | collective-permute-start | bytes 3538952 | tf_op jit(solution)/shard_map/ppermute | solution.py:38
  74.4 6.5 %collective-permute-start.14 = (f32[4,512]{1,0:T(4,128)S(1)}, f32[4,512]{1,0:T(4,128)S(1)}, u32[]{:S(2)}, u32[]{:S(2)}) collective-permute-start(f32[4,512]{1,0:T(4,128)S(1)} %add_add_fusion.3), channel_id=1, source_target_pairs={{0,4},{1,5},{2,6},{3,7},{4,0},{5,1},{6,2},{7,3},{8,12},{9,13},{10,... | collective-permute-start | bytes 24584 | tf_op jit(solution)/shard_map/ppermute | solution.py:54
  95.6 17.4 %collective-permute-start.25 = (bf16[3,3,128,512]{3,2,1,0:T(8,128)(2,1)S(1)}, bf16[3,3,128,512]{3,2,1,0:T(8,128)(2,1)S(1)}, u32[]{:S(2)}, u32[]{:S(2)}) collective-permute-start(bf16[3,3,128,512]{3,2,1,0:T(8,128)(2,1)S(1)} %get-tuple-element.119.refs_4_), channel_id=1, source_target_pairs={{0,8},{8,0},{16,24},{24,16},{1,9},{9,1},{17,25},{25,17},{2,10},{10... | collective-permute-start | bytes 3538952 | tf_op jit(solution)/shard_map/ppermute | solution.py:38
  101.2 11.9 %collective-permute-start.27 = (bf16[3,3,128,512]{3,2,1,0:T(8,128)(2,1)}, bf16[3,3,128,512]{3,2,1,0:T(8,128)(2,1)S(1)}, u32[]{:S(2)}, u32[]{:S(2)}) collective-permute-start(bf16[3,3,128,512]{3,2,1,0:T(8,128)(2,1)} %collective-permute-done.26.refs_6_), channel_id=1, source_target_pairs={{0,8},{8,0},{16,24},{24,16},{1,9},{9,1},{17,25},{25,17},{2,10},{10... | collective-permute-start | bytes 3538952 | tf_op jit(solution)/shard_map/ppermute | solution.py:38
  101.2 28.4 %collective-permute-start.35 = (bf16[3,3,128,512]{3,2,1,0:T(8,128)(2,1)S(1)}, bf16[3,3,128,512]{3,2,1,0:T(8,128)(2,1)S(1)}, u32[]{:S(2)}, u32[]{:S(2)}) collective-permute-start(bf16[3,3,128,512]{3,2,1,0:T(8,128)(2,1)S(1)} %get-tuple-element.123.refs_2_.refs_4_), channel_id=1, source_target_pairs={{0,16},{8,24},{16,0},{24,8},{1,17},{9,25},{17,1},{25,9},{2,18},{10... | collective-permute-start | bytes 3538952 | tf_op jit(solution)/shard_map/ppermute | solution.py:38
  102.9 6.3 %collective-permute-start.23 = (f32[2,512]{1,0:T(2,128)S(1)}, f32[2,512]{1,0:T(2,128)S(1)}, u32[]{:S(2)}, u32[]{:S(2)}) collective-permute-start(f32[2,512]{1,0:T(2,128)S(1)} %add_add_fusion.15), channel_id=1, source_target_pairs={{0,4},{1,5},{2,6},{3,7},{4,0},{5,1},{6,2},{7,3},{8,12},{9,13},{10,... | collective-permute-start | bytes 12296 | tf_op jit(solution)/shard_map/ppermute | solution.py:54
  122.0 19.5 %collective-permute-start.34 = (bf16[3,3,128,512]{3,2,1,0:T(8,128)(2,1)S(1)}, bf16[3,3,128,512]{3,2,1,0:T(8,128)(2,1)S(1)}, u32[]{:S(2)}, u32[]{:S(2)}) collective-permute-start(bf16[3,3,128,512]{3,2,1,0:T(8,128)(2,1)S(1)} %get-tuple-element.123.refs_2_.refs_4_), channel_id=1, source_target_pairs={{0,8},{8,0},{16,24},{24,16},{1,9},{9,1},{17,25},{25,17},{2,10},{10... | collective-permute-start | bytes 3538952 | tf_op jit(solution)/shard_map/ppermute | solution.py:38
  129.6 11.9 %collective-permute-start.36 = (bf16[3,3,128,512]{3,2,1,0:T(8,128)(2,1)S(1)}, bf16[3,3,128,512]{3,2,1,0:T(8,128)(2,1)S(1)}, u32[]{:S(2)}, u32[]{:S(2)}) collective-permute-start(bf16[3,3,128,512]{3,2,1,0:T(8,128)(2,1)S(1)} %collective-permute-done.35.refs_4_.refs_6_), channel_id=1, source_target_pairs={{0,8},{8,0},{16,24},{24,16},{1,9},{9,1},{17,25},{25,17},{2,10},{10... | collective-permute-start | bytes 3538952 | tf_op jit(solution)/shard_map/ppermute | solution.py:38
  129.6 7.0 %collective-permute-start.32 = (f32[2,512]{1,0:T(2,128)S(1)}, f32[2,512]{1,0:T(2,128)S(1)}, u32[]{:S(2)}, u32[]{:S(2)}) collective-permute-start(f32[2,512]{1,0:T(2,128)S(1)} %add_add_fusion.13), channel_id=1, source_target_pairs={{0,4},{1,5},{2,6},{3,7},{4,0},{5,1},{6,2},{7,3},{8,12},{9,13},{10,... | collective-permute-start | bytes 12296 | tf_op jit(solution)/shard_map/ppermute | solution.py:54
  136.6 11.3 %collective-permute-start.37 = (bf16[864,128]{1,0:T(8,128)(2,1)S(1)}, bf16[864,128]{1,0:T(8,128)(2,1)S(1)}, u32[]{:S(2)}, u32[]{:S(2)}) collective-permute-start(bf16[864,128]{1,0:T(8,128)(2,1)S(1)} %get-tuple-element.251), channel_id=1, source_target_pairs={{0,8},{8,0},{16,24},{24,16},{1,9},{9,1},{17,25},{25,17},{2,10},{10... | collective-permute-start | bytes 663560 | tf_op jit(solution)/shard_map/ppermute | solution.py:38
  140.4 8.4 %collective-permute-start.38 = (bf16[864,128]{1,0:T(8,128)(2,1)S(1)}, bf16[864,128]{1,0:T(8,128)(2,1)S(1)}, u32[]{:S(2)}, u32[]{:S(2)}) collective-permute-start(bf16[864,128]{1,0:T(8,128)(2,1)S(1)} %get-tuple-element.250), channel_id=1, source_target_pairs={{0,16},{8,24},{16,0},{24,8},{1,17},{9,25},{17,1},{25,9},{2,18},{10... | collective-permute-start | bytes 663560 | tf_op jit(solution)/shard_map/ppermute | solution.py:38
  141.4 8.7 %collective-permute-start.39 = (bf16[864,128]{1,0:T(8,128)(2,1)S(1)}, bf16[864,128]{1,0:T(8,128)(2,1)S(1)}, u32[]{:S(2)}, u32[]{:S(2)}) collective-permute-start(bf16[864,128]{1,0:T(8,128)(2,1)S(1)} %get-tuple-element.249), channel_id=1, source_target_pairs={{0,24},{8,16},{16,8},{24,0},{1,25},{9,17},{17,9},{25,1},{2,26},{10... | collective-permute-start | bytes 663560 | tf_op jit(solution)/shard_map/ppermute | solution.py:38
  171.2 9.6 %collective-permute-start.52 = (bf16[864,128]{1,0:T(8,128)(2,1)S(1)}, bf16[864,128]{1,0:T(8,128)(2,1)S(1)}, u32[]{:S(2)}, u32[]{:S(2)}) collective-permute-start(bf16[864,128]{1,0:T(8,128)(2,1)S(1)} %get-tuple-element.246), channel_id=1, source_target_pairs={{0,8},{8,0},{16,24},{24,16},{1,9},{9,1},{17,25},{25,17},{2,10},{10... | collective-permute-start | bytes 663560 | tf_op jit(solution)/shard_map/ppermute | solution.py:38
  171.2 10.3 %collective-permute-start.53 = (bf16[864,128]{1,0:T(8,128)(2,1)S(1)}, bf16[864,128]{1,0:T(8,128)(2,1)S(1)}, u32[]{:S(2)}, u32[]{:S(2)}) collective-permute-start(bf16[864,128]{1,0:T(8,128)(2,1)S(1)} %get-tuple-element.245), channel_id=1, source_target_pairs={{0,16},{8,24},{16,0},{24,8},{1,17},{9,25},{17,1},{25,9},{2,18},{10... | collective-permute-start | bytes 663560 | tf_op jit(solution)/shard_map/ppermute | solution.py:38
  172.3 11.1 %collective-permute-start.54 = (bf16[864,128]{1,0:T(8,128)(2,1)S(1)}, bf16[864,128]{1,0:T(8,128)(2,1)S(1)}, u32[]{:S(2)}, u32[]{:S(2)}) collective-permute-start(bf16[864,128]{1,0:T(8,128)(2,1)S(1)} %get-tuple-element.244), channel_id=1, source_target_pairs={{0,24},{8,16},{16,8},{24,0},{1,25},{9,17},{17,9},{25,1},{2,26},{10... | collective-permute-start | bytes 663560 | tf_op jit(solution)/shard_map/ppermute | solution.py:38
  184.3 7.6 %collective-permute-start.56 = (f32[2,512]{1,0:T(2,128)S(1)}, f32[2,512]{1,0:T(2,128)S(1)}, u32[]{:S(2)}, u32[]{:S(2)}) collective-permute-start(f32[2,512]{1,0:T(2,128)S(1)} %get-tuple-element.136), channel_id=1, source_target_pairs={{0,1},{1,0},{2,3},{3,2},{4,5},{5,4},{6,7},{7,6},{8,9},{9,8},{10,11... | collective-permute-start | bytes 12296 | tf_op jit(solution)/shard_map/ppermute | solution.py:54
  198.3 28.2 %collective-permute-start.65 = (bf16[1,1152,512]{2,1,0:T(8,128)(2,1)S(1)}, bf16[1,1152,512]{2,1,0:T(8,128)(2,1)S(1)}, u32[]{:S(2)}, u32[]{:S(2)}) collective-permute-start(bf16[1,1152,512]{2,1,0:T(8,128)(2,1)S(1)} %get-tuple-element.222), channel_id=1, source_target_pairs={{0,16},{8,24},{16,0},{24,8},{1,17},{9,25},{17,1},{25,9},{2,18},{10... | collective-permute-start | bytes 3538952 | tf_op jit(solution)/shard_map/ppermute | solution.py:38
  213.9 9.1 %collective-permute-start.63 = (f32[3,512]{1,0:T(4,128)S(1)}, f32[3,512]{1,0:T(4,128)S(1)}, u32[]{:S(2)}, u32[]{:S(2)}) collective-permute-start(f32[3,512]{1,0:T(4,128)S(1)} %get-tuple-element.147), channel_id=1, source_target_pairs={{0,1},{1,0},{2,3},{3,2},{4,5},{5,4},{6,7},{7,6},{8,9},{9,8},{10,11... | collective-permute-start | bytes 18440 | tf_op jit(solution)/shard_map/ppermute | solution.py:54
  215.4 7.6 %collective-permute-start.64 = (f32[3,512]{1,0:T(4,128)S(1)}, f32[3,512]{1,0:T(4,128)S(1)}, u32[]{:S(2)}, u32[]{:S(2)}) collective-permute-start(f32[3,512]{1,0:T(4,128)S(1)} %get-tuple-element.147), channel_id=1, source_target_pairs={{0,9},{1,8},{2,11},{3,10},{4,13},{5,12},{6,15},{7,14},{8,1},{9,0},... | collective-permute-start | bytes 18440 | tf_op jit(solution)/shard_map/ppermute | solution.py:54
  227.6 6.5 %collective-permute-start.67 = (bf16[2,1152,512]{2,1,0:T(8,128)(2,1)}, bf16[2,1152,512]{2,1,0:T(8,128)(2,1)}, u32[]{:S(2)}, u32[]{:S(2)}) collective-permute-start(bf16[2,1152,512]{2,1,0:T(8,128)(2,1)} %get-tuple-element.152), channel_id=1, source_target_pairs={{0,8},{8,0},{16,24},{24,16},{1,9},{9,1},{17,25},{25,17},{2,10},{10... | collective-permute-start | bytes 7077896 | tf_op jit(solution)/shard_map/ppermute | solution.py:38
  238.3 29.2 %collective-permute-start.74 = (bf16[1,1152,512]{2,1,0:T(8,128)(2,1)S(1)}, bf16[1,1152,512]{2,1,0:T(8,128)(2,1)S(1)}, u32[]{:S(2)}, u32[]{:S(2)}) collective-permute-start(bf16[1,1152,512]{2,1,0:T(8,128)(2,1)S(1)} %get-tuple-element.220), channel_id=1, source_target_pairs={{0,16},{8,24},{16,0},{24,8},{1,17},{9,25},{17,1},{25,9},{2,18},{10... | collective-permute-start | bytes 3538952 | tf_op jit(solution)/shard_map/ppermute | solution.py:38
  239.3 28.1 %collective-permute-start.73 = (bf16[1,576,512]{2,1,0:T(8,128)(2,1)S(1)}, bf16[1,576,512]{2,1,0:T(8,128)(2,1)S(1)}, u32[]{:S(2)}, u32[]{:S(2)}) collective-permute-start(bf16[1,576,512]{2,1,0:T(8,128)(2,1)S(1)} %get-tuple-element.233), channel_id=1, source_target_pairs={{0,1},{1,0},{2,3},{3,2},{4,5},{5,4},{6,7},{7,6},{8,9},{9,8},{10,11... | collective-permute-start | bytes 1769480 | tf_op jit(solution)/shard_map/ppermute | solution.py:38
  256.9 10.6 %collective-permute-start.71 = (f32[2,512]{1,0:T(2,128)S(1)}, f32[2,512]{1,0:T(2,128)S(1)}, u32[]{:S(2)}, u32[]{:S(2)}) collective-permute-start(f32[2,512]{1,0:T(2,128)S(1)} %get-tuple-element.159), channel_id=1, source_target_pairs={{0,1},{1,0},{2,3},{3,2},{4,5},{5,4},{6,7},{7,6},{8,9},{9,8},{10,11... | collective-permute-start | bytes 12296 | tf_op jit(solution)/shard_map/ppermute | solution.py:54
  257.6 9.9 %collective-permute-start.72 = (f32[2,512]{1,0:T(2,128)S(1)}, f32[2,512]{1,0:T(2,128)S(1)}, u32[]{:S(2)}, u32[]{:S(2)}) collective-permute-start(f32[2,512]{1,0:T(2,128)S(1)} %get-tuple-element.159), channel_id=1, source_target_pairs={{0,9},{1,8},{2,11},{3,10},{4,13},{5,12},{6,15},{7,14},{8,1},{9,0},... | collective-permute-start | bytes 12296 | tf_op jit(solution)/shard_map/ppermute | solution.py:54
  268.7 14.2 %collective-permute-start.79 = (bf16[2,1152,512]{2,1,0:T(8,128)(2,1)}, bf16[2,1152,512]{2,1,0:T(8,128)(2,1)}, u32[]{:S(2)}, u32[]{:S(2)}) collective-permute-start(bf16[2,1152,512]{2,1,0:T(8,128)(2,1)} %get-tuple-element.164), channel_id=1, source_target_pairs={{0,8},{8,0},{16,24},{24,16},{1,9},{9,1},{17,25},{25,17},{2,10},{10... | collective-permute-start | bytes 7077896 | tf_op jit(solution)/shard_map/ppermute | solution.py:38
  270.8 9.5 %collective-permute-start.76 = (bf16[1,288,512]{2,1,0:T(8,128)(2,1)}, bf16[1,288,512]{2,1,0:T(8,128)(2,1)}, u32[]{:S(2)}, u32[]{:S(2)}) collective-permute-start(bf16[1,288,512]{2,1,0:T(8,128)(2,1)} %add_convert_fusion.27), channel_id=1, source_target_pairs={{0,2},{1,3},{2,0},{3,1},{4,6},{5,7},{6,4},{7,5},{8,10},{9,11},{10,... | collective-permute-start | bytes 884744 | tf_op jit(solution)/shard_map/ppermute | solution.py:38
  273.7 6.5 %collective-permute-start.75 = (f32[2,512]{1,0:T(2,128)S(1)}, f32[2,512]{1,0:T(2,128)S(1)}, u32[]{:S(2)}, u32[]{:S(2)}) collective-permute-start(f32[2,512]{1,0:T(2,128)S(1)} %add_add_fusion.5), channel_id=1, source_target_pairs={{0,2},{1,3},{2,0},{3,1},{4,6},{5,7},{6,4},{7,5},{8,10},{9,11},{10,... | collective-permute-start | bytes 12296 | tf_op jit(solution)/shard_map/ppermute | solution.py:54
  286.8 27.1 %collective-permute-start.81 = (bf16[2,576,512]{2,1,0:T(8,128)(2,1)S(1)}, bf16[2,576,512]{2,1,0:T(8,128)(2,1)}, u32[]{:S(2)}, u32[]{:S(2)}) collective-permute-start(bf16[2,576,512]{2,1,0:T(8,128)(2,1)S(1)} %get-tuple-element.218), channel_id=1, source_target_pairs={{0,1},{1,0},{2,3},{3,2},{4,5},{5,4},{6,7},{7,6},{8,9},{9,8},{10,11... | collective-permute-start | bytes 3538952 | tf_op jit(solution)/shard_map/ppermute | solution.py:38
  287.8 17.9 %collective-permute-start.82 = (bf16[1,576,512]{2,1,0:T(8,128)(2,1)S(1)}, bf16[1,576,512]{2,1,0:T(8,128)(2,1)S(1)}, u32[]{:S(2)}, u32[]{:S(2)}) collective-permute-start(bf16[1,576,512]{2,1,0:T(8,128)(2,1)S(1)} %copy-done.44), channel_id=1, source_target_pairs={{0,2},{1,3},{2,0},{3,1},{4,6},{5,7},{6,4},{7,5},{8,10},{9,11},{10,... | collective-permute-start | bytes 1769480 | tf_op jit(solution)/shard_map/ppermute | solution.py:38
  295.4 15.6 %collective-permute-start.80 = (bf16[2,864,128]{2,1,0:T(8,128)(2,1)S(1)}, bf16[2,864,128]{2,1,0:T(8,128)(2,1)S(1)}, u32[]{:S(2)}, u32[]{:S(2)}) collective-permute-start(bf16[2,864,128]{2,1,0:T(8,128)(2,1)S(1)} %get-tuple-element.237), channel_id=1, source_target_pairs={{0,16},{8,24},{16,0},{24,8},{1,17},{9,25},{17,1},{25,9},{2,18},{10... | collective-permute-start | bytes 1327112 | tf_op jit(solution)/shard_map/ppermute | solution.py:38
  296.4 14.6 %collective-permute-start.83 = (bf16[1,288,512]{2,1,0:T(8,128)(2,1)S(1)}, bf16[1,288,512]{2,1,0:T(8,128)(2,1)S(1)}, u32[]{:S(2)}, u32[]{:S(2)}) collective-permute-start(bf16[1,288,512]{2,1,0:T(8,128)(2,1)S(1)} %add_convert_fusion.25), channel_id=1, source_target_pairs={{0,4},{1,5},{2,6},{3,7},{4,0},{5,1},{6,2},{7,3},{8,12},{9,13},{10,... | collective-permute-start | bytes 884744 | tf_op jit(solution)/shard_map/ppermute | solution.py:38
  314.0 6.9 %collective-permute-start.84 = (bf16[2,640,512]{2,1,0:T(8,128)(2,1)}, bf16[2,640,512]{2,1,0:T(8,128)(2,1)}, u32[]{:S(2)}, u32[]{:S(2)}) collective-permute-start(bf16[2,640,512]{2,1,0:T(8,128)(2,1)} %get-tuple-element.177), channel_id=1, source_target_pairs={{0,8},{8,0},{16,24},{24,16},{1,9},{9,1},{17,25},{25,17},{2,10},{10... | collective-permute-start | bytes 3932168 | tf_op jit(solution)/shard_map/ppermute | solution.py:38
  314.0 15.2 %collective-permute-start.87 = (bf16[2,864,128]{2,1,0:T(8,128)(2,1)}, bf16[2,864,128]{2,1,0:T(8,128)(2,1)S(1)}, u32[]{:S(2)}, u32[]{:S(2)}) collective-permute-start(bf16[2,864,128]{2,1,0:T(8,128)(2,1)} %get-tuple-element.235), channel_id=1, source_target_pairs={{0,8},{8,0},{16,24},{24,16},{1,9},{9,1},{17,25},{25,17},{2,10},{10... | collective-permute-start | bytes 1327112 | tf_op jit(solution)/shard_map/ppermute | solution.py:38
  314.6 14.7 %collective-permute-start.88 = (bf16[2,864,128]{2,1,0:T(8,128)(2,1)}, bf16[2,864,128]{2,1,0:T(8,128)(2,1)S(1)}, u32[]{:S(2)}, u32[]{:S(2)}) collective-permute-start(bf16[2,864,128]{2,1,0:T(8,128)(2,1)} %get-tuple-element.234), channel_id=1, source_target_pairs={{0,24},{8,16},{16,8},{24,0},{1,25},{9,17},{17,9},{25,1},{2,26},{10... | collective-permute-start | bytes 1327112 | tf_op jit(solution)/shard_map/ppermute | solution.py:38
  320.2 15.0 %collective-permute-start.86 = (bf16[1,288,512]{2,1,0:T(8,128)(2,1)}, bf16[1,288,512]{2,1,0:T(8,128)(2,1)}, u32[]{:S(2)}, u32[]{:S(2)}) collective-permute-start(bf16[1,288,512]{2,1,0:T(8,128)(2,1)} %add_convert_fusion.22), channel_id=1, source_target_pairs={{0,1},{1,0},{2,3},{3,2},{4,5},{5,4},{6,7},{7,6},{8,9},{9,8},{10,11... | collective-permute-start | bytes 884744 | tf_op jit(solution)/shard_map/ppermute | solution.py:38
  323.6 17.0 %collective-permute-start.85 = (bf16[2,320,512]{2,1,0:T(8,128)(2,1)}, bf16[2,320,512]{2,1,0:T(8,128)(2,1)S(1)}, u32[]{:S(2)}, u32[]{:S(2)}) collective-permute-start(bf16[2,320,512]{2,1,0:T(8,128)(2,1)} %get-tuple-element.227), channel_id=1, source_target_pairs={{0,2},{1,3},{2,0},{3,1},{4,6},{5,7},{6,4},{7,5},{8,10},{9,11},{10,... | collective-permute-start | bytes 1966088 | tf_op jit(solution)/shard_map/ppermute | solution.py:38
  328.2 22.6 %collective-permute-start.93 = (bf16[1,576,512]{2,1,0:T(8,128)(2,1)}, bf16[1,576,512]{2,1,0:T(8,128)(2,1)S(1)}, u32[]{:S(2)}, u32[]{:S(2)}) collective-permute-start(bf16[1,576,512]{2,1,0:T(8,128)(2,1)} %get-tuple-element.229), channel_id=1, source_target_pairs={{0,16},{8,24},{16,0},{24,8},{1,17},{9,25},{17,1},{25,9},{2,18},{10... | collective-permute-start | bytes 1769480 | tf_op jit(solution)/shard_map/ppermute | solution.py:38
  340.8 13.1 %collective-permute-start.92 = (bf16[2,160,512]{2,1,0:T(8,128)(2,1)S(1)}, bf16[2,160,512]{2,1,0:T(8,128)(2,1)S(1)}, u32[]{:S(2)}, u32[]{:S(2)}) collective-permute-start(bf16[2,160,512]{2,1,0:T(8,128)(2,1)S(1)} %get-tuple-element.243), channel_id=1, source_target_pairs={{0,1},{1,0},{2,3},{3,2},{4,5},{5,4},{6,7},{7,6},{8,9},{9,8},{10,11... | collective-permute-start | bytes 983048 | tf_op jit(solution)/shard_map/ppermute | solution.py:38
  343.0 15.6 %collective-permute-start.91 = (bf16[1,288,512]{2,1,0:T(8,128)(2,1)S(1)}, bf16[1,288,512]{2,1,0:T(8,128)(2,1)S(1)}, u32[]{:S(2)}, u32[]{:S(2)}) collective-permute-start(bf16[1,288,512]{2,1,0:T(8,128)(2,1)S(1)} %add_convert_fusion.24), channel_id=1, source_target_pairs={{0,2},{1,3},{2,0},{3,1},{4,6},{5,7},{6,4},{7,5},{8,10},{9,11},{10,... | collective-permute-start | bytes 884744 | tf_op jit(solution)/shard_map/ppermute | solution.py:38
  343.6 17.2 %collective-permute-start.90 = (bf16[1,288,512]{2,1,0:T(8,128)(2,1)S(1)}, bf16[1,288,512]{2,1,0:T(8,128)(2,1)S(1)}, u32[]{:S(2)}, u32[]{:S(2)}) collective-permute-start(bf16[1,288,512]{2,1,0:T(8,128)(2,1)S(1)} %add_convert_fusion.21), channel_id=1, source_target_pairs={{0,4},{1,5},{2,6},{3,7},{4,0},{5,1},{6,2},{7,3},{8,12},{9,13},{10,... | collective-permute-start | bytes 884744 | tf_op jit(solution)/shard_map/ppermute | solution.py:38
  345.6 15.9 %collective-permute-start.94 = (bf16[2,64,320]{2,1,0:T(8,128)(2,1)S(1)}, bf16[2,64,320]{2,1,0:T(8,128)(2,1)S(1)}, u32[]{:S(2)}, u32[]{:S(2)}) collective-permute-start(bf16[2,64,320]{2,1,0:T(8,128)(2,1)S(1)} %get-tuple-element.182), channel_id=1, source_target_pairs={{0,1},{1,2},{2,3},{3,4},{4,5},{5,6},{6,7},{8,9},{9,10},{10,11},{11... | collective-permute-start | bytes 245768 | tf_op jit(solution)/shard_map/ppermute | solution.py:48
  350.8 33.2 %collective-permute-start.89 = (bf16[2,80,128]{2,1,0:T(8,128)(2,1)S(1)}, bf16[2,80,128]{2,1,0:T(8,128)(2,1)S(1)}, u32[]{:S(2)}, u32[]{:S(2)}) collective-permute-start(bf16[2,80,128]{2,1,0:T(8,128)(2,1)S(1)} %get-tuple-element.187), channel_id=1, source_target_pairs={{0,1},{1,2},{2,3},{3,4},{4,5},{5,6},{6,7},{8,9},{9,10},{10,11},{11... | collective-permute-start | bytes 122888 | tf_op jit(solution)/shard_map/ppermute | solution.py:48
  353.9 10.2 %collective-permute-start.98 = (bf16[1,288,512]{2,1,0:T(8,128)(2,1)S(1)}, bf16[1,288,512]{2,1,0:T(8,128)(2,1)S(1)}, u32[]{:S(2)}, u32[]{:S(2)}) collective-permute-start(bf16[1,288,512]{2,1,0:T(8,128)(2,1)S(1)} %add_convert_fusion.20), channel_id=1, source_target_pairs={{0,2},{1,3},{2,0},{3,1},{4,6},{5,7},{6,4},{7,5},{8,10},{9,11},{10,... | collective-permute-start | bytes 884744 | tf_op jit(solution)/shard_map/ppermute | solution.py:38
  360.8 35.7 %collective-permute-start.104 = (bf16[1,576,512]{2,1,0:T(8,128)(2,1)}, bf16[1,576,512]{2,1,0:T(8,128)(2,1)S(1)}, u32[]{:S(2)}, u32[]{:S(2)}) collective-permute-start(bf16[1,576,512]{2,1,0:T(8,128)(2,1)} %maximum_select_fusion), channel_id=1, source_target_pairs={{0,1},{1,0},{2,3},{3,2},{4,5},{5,4},{6,7},{7,6},{8,9},{9,8},{10,11... | collective-permute-start | bytes 1769480 | tf_op jit(solution)/shard_map/ppermute | solution.py:38
  361.5 18.1 %collective-permute-start.97 = (bf16[1,288,512]{2,1,0:T(8,128)(2,1)S(1)}, bf16[1,288,512]{2,1,0:T(8,128)(2,1)S(1)}, u32[]{:S(2)}, u32[]{:S(2)}) collective-permute-start(bf16[1,288,512]{2,1,0:T(8,128)(2,1)S(1)} %add_convert_fusion.19), channel_id=1, source_target_pairs={{0,1},{1,0},{2,3},{3,2},{4,5},{5,4},{6,7},{7,6},{8,9},{9,8},{10,11... | collective-permute-start | bytes 884744 | tf_op jit(solution)/shard_map/ppermute | solution.py:38
  364.0 16.6 %collective-permute-start.96 = (bf16[1,160,512]{2,1,0:T(8,128)(2,1)S(1)}, bf16[1,160,512]{2,1,0:T(8,128)(2,1)S(1)}, u32[]{:S(2)}, u32[]{:S(2)}) collective-permute-start(bf16[1,160,512]{2,1,0:T(8,128)(2,1)S(1)} %add_convert_fusion.29), channel_id=1, source_target_pairs={{0,4},{1,5},{2,6},{3,7},{4,0},{5,1},{6,2},{7,3},{8,12},{9,13},{10,... | collective-permute-start | bytes 491528 | tf_op jit(solution)/shard_map/ppermute | solution.py:38
  364.3 18.6 %collective-permute-start.100 = (bf16[1,288,512]{2,1,0:T(8,128)(2,1)S(1)}, bf16[1,288,512]{2,1,0:T(8,128)(2,1)S(1)}, u32[]{:S(2)}, u32[]{:S(2)}) collective-permute-start(bf16[1,288,512]{2,1,0:T(8,128)(2,1)S(1)} %add_convert_fusion.17), channel_id=1, source_target_pairs={{0,4},{1,5},{2,6},{3,7},{4,0},{5,1},{6,2},{7,3},{8,12},{9,13},{10,... | collective-permute-start | bytes 884744 | tf_op jit(solution)/shard_map/ppermute | solution.py:38
  380.7 7.3 %collective-permute-start.99 = (bf16[1,160,512]{2,1,0:T(8,128)(2,1)S(1)}, bf16[1,160,512]{2,1,0:T(8,128)(2,1)S(1)}, u32[]{:S(2)}, u32[]{:S(2)}) collective-permute-start(bf16[1,160,512]{2,1,0:T(8,128)(2,1)S(1)} %add_convert_fusion.28), channel_id=1, source_target_pairs={{0,1},{1,0},{2,3},{3,2},{4,5},{5,4},{6,7},{7,6},{8,9},{9,8},{10,11... | collective-permute-start | bytes 491528 | tf_op jit(solution)/shard_map/ppermute | solution.py:38
  382.9 10.0 %collective-permute-start.101 = (bf16[1,288,512]{2,1,0:T(8,128)(2,1)S(1)}, bf16[1,288,512]{2,1,0:T(8,128)(2,1)S(1)}, u32[]{:S(2)}, u32[]{:S(2)}) collective-permute-start(bf16[1,288,512]{2,1,0:T(8,128)(2,1)S(1)} %add_convert_fusion.16), channel_id=1, source_target_pairs={{0,2},{1,3},{2,0},{3,1},{4,6},{5,7},{6,4},{7,5},{8,10},{9,11},{10,... | collective-permute-start | bytes 884744 | tf_op jit(solution)/shard_map/ppermute | solution.py:38
  386.0 24.6 %collective-permute-start.103 = (bf16[1,576,512]{2,1,0:T(8,128)(2,1)}, bf16[1,576,512]{2,1,0:T(8,128)(2,1)S(1)}, u32[]{:S(2)}, u32[]{:S(2)}) collective-permute-start(bf16[1,576,512]{2,1,0:T(8,128)(2,1)} %maximum_select_fusion.1), channel_id=1, source_target_pairs={{0,2},{1,3},{2,0},{3,1},{4,6},{5,7},{6,4},{7,5},{8,10},{9,11},{10,... | collective-permute-start | bytes 1769480 | tf_op jit(solution)/shard_map/ppermute | solution.py:38
  393.2 17.4 %collective-permute-start.102 = (bf16[1,576,512]{2,1,0:T(8,128)(2,1)S(1)}, bf16[1,576,512]{2,1,0:T(8,128)(2,1)S(1)}, u32[]{:S(2)}, u32[]{:S(2)}) collective-permute-start(bf16[1,576,512]{2,1,0:T(8,128)(2,1)S(1)} %maximum_select_fusion.3), channel_id=1, source_target_pairs={{0,1},{1,0},{2,3},{3,2},{4,5},{5,4},{6,7},{7,6},{8,9},{9,8},{10,11... | collective-permute-start | bytes 1769480 | tf_op jit(solution)/shard_map/ppermute | solution.py:38
  396.2 14.4 %collective-permute-start.105 = (bf16[1,320,512]{2,1,0:T(8,128)(2,1)S(1)}, bf16[1,320,512]{2,1,0:T(8,128)(2,1)S(1)}, u32[]{:S(2)}, u32[]{:S(2)}) collective-permute-start(bf16[1,320,512]{2,1,0:T(8,128)(2,1)S(1)} %maximum_select_fusion.7), channel_id=1, source_target_pairs={{0,2},{1,3},{2,0},{3,1},{4,6},{5,7},{6,4},{7,5},{8,10},{9,11},{10,... | collective-permute-start | bytes 983048 | tf_op jit(solution)/shard_map/ppermute | solution.py:38
  (93 other events, 712.3 us)
